TPU v7x, 128 devices: a whole 4x4x4 slice. The times are simulated.
128 devices in a mesh: ctr: 8 (over x_hi, y), row: 4 (over z), col: 4 (over x_lo, core).
Axes of the slice: x: 4 (x_hi: 2, x_lo: 2; x = x_hi * 2 + x_lo), y: 4, z: 4, core: 2. Of those that a mesh axis runs over, the one named last changes fastest.
Arguments:
- amps: bfloat16 [4, 1024, 16, 1024], P('row', 'ctr', 'col'), may hold values from -6 to 6
- w_cycle: bfloat16 [16, 1024, 4, 1024], P('ctr', 'row', 'col'), may hold values from -0.125 to 0.125
- w_cross: bfloat16 [16, 1024, 4, 1024], P('ctr', 'row', 'col'), may hold values from -0.125 to 0.125
- occ_sizes: int32 [8], replicated, may hold values from 1 to 50, 200 in all
- virt_sizes: int32 [8], replicated, may hold values from 1 to 256, 1024 in all
- slab_occ: int32 [4], replicated, may hold values from 0 to 199
- k_occ: int32 [16], replicated, may hold values from 0 to 199
- j_occ: int32 [4], replicated, may hold values from 0 to 199
Outputs:
- update: bfloat16 [4, 1024, 4, 1024], P('row', 'ctr', 'col')
Inputs may be any that keep to these rules, and one draw needn't show every extreme that they name: occ_sizes sum to 200. virt_sizes sum to 1024.
All inputs are finite; a program needn't handle non-finite values.
Results may differ from a plain program's by a relative error of at most 0.001.
Values may be sent and summed in bfloat16 or wider, within the bound.
No kernel may reach another device: no remote copies, remote signals or barrier semaphores. Data moves between devices by JAX's collectives and lax.ppermute only.
A program may use at most 64 MiB of HBM per device.

v0:
```python
import jax
import jax.numpy as jnp
from jax import lax
from jax.sharding import PartitionSpec as P


def irreps_of(index, sizes):
    bounds = jnp.cumsum(sizes)[:7]
    return jnp.sum((index[..., None] >= bounds).astype(jnp.int32), axis=-1)


def on_device(amps, w_cycle, w_cross, occ_sizes, virt_sizes, slab_occ, k_occ, j_occ):
    slab_count = amps.shape[0]
    virt = amps.shape[3]
    k_count = w_cycle.shape[0]
    j_count = w_cycle.shape[2]
    gathered = lax.all_gather(amps, "col", axis=2, tiled=True)
    moved = lax.all_to_all(gathered, "ctr", split_axis=2, concat_axis=1, tiled=True)
    irr_i = irreps_of(
        lax.dynamic_slice_in_dim(slab_occ, lax.axis_index("row") * slab_count, slab_count),
        occ_sizes,
    )
    irr_k = irreps_of(
        lax.dynamic_slice_in_dim(k_occ, lax.axis_index("ctr") * k_count, k_count), occ_sizes
    )
    irr_j = irreps_of(
        lax.dynamic_slice_in_dim(j_occ, lax.axis_index("col") * j_count, j_count), occ_sizes
    )
    irr_v = irreps_of(jnp.arange(virt, dtype=jnp.int32), virt_sizes)
    keep = (
        jnp.bitwise_xor(
            jnp.bitwise_xor(irr_i[:, None, None, None], irr_v[None, :, None, None]),
            jnp.bitwise_xor(irr_k[None, None, :, None], irr_v[None, None, None, :]),
        )
        == 0
    )
    t_sym = jnp.where(keep, moved, jnp.zeros((), moved.dtype))
    cycle_part = jnp.einsum(
        "iakc,kcjb->iajb",
        t_sym,
        lax.all_gather(w_cycle, "row", axis=1, tiled=True),
        preferred_element_type=jnp.float32,
    )
    cross_part = jnp.einsum(
        "idka,kdjb->iajb",
        t_sym,
        lax.all_gather(w_cross, "row", axis=1, tiled=True),
        preferred_element_type=jnp.float32,
    )
    total = lax.psum_scatter(cycle_part, "ctr", scatter_dimension=1, tiled=True) + lax.psum_scatter(
        cross_part, "ctr", scatter_dimension=1, tiled=True
    )
    a_count = total.shape[1]
    irr_a = lax.dynamic_slice_in_dim(irr_v, lax.axis_index("ctr") * a_count, a_count)
    out_keep = (
        jnp.bitwise_xor(
            jnp.bitwise_xor(irr_i[:, None, None, None], irr_a[None, :, None, None]),
            jnp.bitwise_xor(irr_j[None, None, :, None], irr_v[None, None, None, :]),
        )
        == 0
    )
    return jnp.where(out_keep, total, jnp.zeros((), total.dtype)).astype(jnp.bfloat16)


def solution(mesh):
    return jax.shard_map(
        on_device,
        mesh=mesh,
        in_specs=(
            P("row", "ctr", "col", None),
            P("ctr", "row", "col", None),
            P("ctr", "row", "col", None),
            P(),
            P(),
            P(),
            P(),
            P(),
        ),
        out_specs=P("row", "ctr", "col", None),
        check_vma=False,
    )
```

profile of v0, /device:TPU:0, one launch (start us, length us, event | category | flops | bytes accessed | tf_op | source)
XLA Modules:
  0.0 264.2 jit_solution(2786227205000035787)
XLA Ops:
  6.5 2.6 copy.18
  9.2 0.7 all-gather.8.cloned.1.call-update
  9.9 0.7 all-gather.6.cloned.1.call-update
  10.7 47.1 %all-gather.4.cloned.1.call-done = bf16[1,128,16,1024]{3,1,0,2:T(8,128)(2,1)} async-done(((bf16[1,128,4,1024]{3,1,0,2:T(8,128)(2,1)}), bf16[1,128,16,1024]{3,1,0,2:T(8,128)(2,1)}) %all-gather.4.cloned.1.call-update) | async-done | bytes 4194320 | tf_op jit(solution)/shard_map/all_gather | solution.py:17
  57.7 6.4 %all-to-all-start = ((bf16[1,128,16,1024]{3,1,0,2:T(8,128)(2,1)}), bf16[1,128,16,1024]{3,1,0,2:T(8,128)(2,1)}, u32[]{:S(2)}, u32[]{:S(2)}) async-start(bf16[1,128,16,1024]{3,1,0,2:T(8,128)(2,1)} %all-gather.4.cloned.1.call-done), calls=%async_computation | async-start | bytes 8388608 | tf_op jit(solution)/shard_map/all_to_all | solution.py:18
  64.2 0.2 reduce-window.6
  64.4 0.2 reduce-window.9
  64.6 0.6 dynamic_slice.12
  65.2 0.6 dynamic_slice.14
  65.8 0.1 dynamic_slice.15
  65.9 1.9 fusion.16
  67.8 0.1 convert_reduce_fusion
  67.9 0.2 fusion.14
  68.0 1.3 broadcast_xor_fusion.2
  69.3 0.1 broadcast_xor_fusion
  69.4 44.7 %all-to-all-done = bf16[1,128,16,1024]{3,1,0,2:T(8,128)(2,1)} async-done(((bf16[1,128,16,1024]{3,1,0,2:T(8,128)(2,1)}), bf16[1,128,16,1024]{3,1,0,2:T(8,128)(2,1)}, u32[]{:S(2)}, u32[]{:S(2)}) %all-to-all-start) | async-done | bytes 4194336 | tf_op jit(solution)/shard_map/all_to_all | solution.py:18
  114.1 6.8 %copy.19 = bf16[1,8,128,2,1024]{2,1,4,3,0:T(8,128)(2,1)} copy(bf16[1,8,128,2,1024]{4,2,3,1,0:T(8,128)(2,1)} %bitcast.7) | data formatting | bytes 8388608 | tf_op jit(solution)/shard_map/all_to_all | solution.py:18
  120.9 7.4 %all_to_all.16 = bf16[1024,2,1024]{0,2,1:T(8,128)(2,1)} reshape(bf16[1,8,128,2,1024]{2,1,4,3,0:T(8,128)(2,1)} %copy.19) | data formatting | bytes 8388608 | tf_op jit(solution)/shard_map/all_to_all | solution.py:18
  128.3 10.1 %fusion.2 = f32[1024,1024,1]{1,0,2:T(8,128)} fusion(bf16[2,1024,1,1024]{3,1,0,2:T(8,128)(2,1)} %all-gather.8.cloned.1.call-done, bf16[1024,2,1024]{0,2,1:T(8,128)(2,1)} %all_to_all.16, s32[2,1024]{1,0:T(2,128)S(1)} %broadcast_xor_fusion, s32[1024]{0:T(1024)S(1)} %get-tuple-element.8), kind=kOutput, calls=%fused_computation.4 | convolution fusion | flops 4301258752 | bytes 12595200 | tf_op jit(solution)/shard_map/idka,kdjb->iajb/dot_general | solution.py:44
  138.4 21.3 %all-gather.6.cloned.1.call-done = bf16[2,1024,1,1024]{3,1,0,2:T(8,128)(2,1)} async-done(((bf16[2,256,1,1024]{3,1,0,2:T(8,128)(2,1)}), bf16[2,1024,1,1024]{3,1,0,2:T(8,128)(2,1)}) %all-gather.6.cloned.1.call-update) | async-done | bytes 4194320 | tf_op jit(solution)/shard_map/all_gather | solution.py:41
  159.7 11.3 %fusion.1 = f32[1,1024,1,1024]{3,1,2,0:T(8,128)} fusion(f32[1024,1024,1]{1,0,2:T(8,128)} %fusion.2, bf16[2,1024,1,1024]{3,1,0,2:T(8,128)(2,1)} %all-gather.6.cloned.1.call-done, bf16[1024,2,1024]{0,2,1:T(8,128)(2,1)} %all_to_all.16, s32[2,1024]{1,0:T(2,128)S(1)} %broadcast_xor_fusion, s32[1024]{0:T(1024)S(1)} %get-tuple-element.8), kind=kOutput, calls=%fused_computation.3 | convolution fusion | flops 4302307328 | bytes 16789504 | tf_op jit(solution)/shard_map/iakc,kcjb->iajb/dot_general | solution.py:38
  171.1 0.7 dynamic-slice_xor_fusion
  171.8 84.0 %reduce-scatter.2.cloned.1.call-done = f32[1,128,1,1024]{3,1,2,0:T(8,128)} async-done(((f32[1,1024,1,1024]{3,1,2,0:T(8,128)}), f32[1,128,1,1024]{3,1,2,0:T(8,128)}) %reduce-scatter.2.cloned.1.call-update) | async-done | bytes 524304 | tf_op jit(solution)/shard_map/reduce_scatter | solution.py:50
  255.8 1.9 select_convert_fusion
  (18 shorter events, 0.2 us)
Async XLA Ops:
  6.5 51.2 %all-gather.4.cloned.1.call-start = ((), (), s32[]{:S(2)}) async-start(), calls=%async_computation.2 | async-start | bytes 5242880 | tf_op jit(solution)/shard_map/all_gather | solution.py:17
  9.1 119.2 %all-gather.8.cloned.1.call-start = ((), (), s32[]{:S(2)}) async-start(), calls=%async_computation.4 | async-start | bytes 5242880 | tf_op jit(solution)/shard_map/all_gather | solution.py:47
  9.9 149.8 %all-gather.6.cloned.1.call-start = ((), (), s32[]{:S(2)}) async-start(), calls=%async_computation.3 | async-start | bytes 5242880 | tf_op jit(solution)/shard_map/all_gather | solution.py:41
  10.6 53.6 %copy-start = (s32[8]{0:T(128)S(1)}, s32[8]{0:T(128)}, u32[]{:S(2)}) copy-start(s32[8]{0:T(128)} %param.11) | copy-start | bytes 100
  10.6 53.8 %copy-start.1 = (s32[8]{0:T(128)S(1)}, s32[8]{0:T(128)}, u32[]{:S(2)}) copy-start(s32[8]{0:T(128)} %param.12) | copy-start | bytes 100
  10.6 53.9 %copy-start.2 = (s32[4]{0:T(128)S(1)}, s32[4]{0:T(128)}, u32[]{:S(2)}) copy-start(s32[4]{0:T(128)} %param.13) | copy-start | bytes 52
  10.7 54.5 %copy-start.3 = (s32[4]{0:T(128)S(1)}, s32[4]{0:T(128)}, u32[]{:S(2)}) copy-start(s32[4]{0:T(128)} %param.15) | copy-start | bytes 52
  10.7 55.1 %copy-start.4 = (s32[16]{0:T(128)S(1)}, s32[16]{0:T(128)}, u32[]{:S(2)}) copy-start(s32[16]{0:T(128)} %param.14) | copy-start | bytes 196
  57.7 56.4 %all-to-all-start = ((bf16[1,128,16,1024]{3,1,0,2:T(8,128)(2,1)}), bf16[1,128,16,1024]{3,1,0,2:T(8,128)(2,1)}, u32[]{:S(2)}, u32[]{:S(2)}) async-start(bf16[1,128,16,1024]{3,1,0,2:T(8,128)(2,1)} %all-gather.4.cloned.1.call-done), calls=%async_computation | async-start | bytes 8388608 | tf_op jit(solution)/shard_map/all_to_all | solution.py:18
  64.1 191.7 %reduce-scatter.2.cloned.1.call-start = ((), (), s32[]{:S(2)}) async-start(), calls=%async_computation.5 | async-start | bytes 4718592 | tf_op jit(solution)/shard_map/reduce_scatter | solution.py:50
Sparse Core Ops, SparseCore 0:
  9.2 48.4 all-gather.3
  59.4 49.8 all-gather.7
  111.0 48.6 all-gather.5
  171.2 84.5 reduce-scatter.1
where the time goes:
time: 265 us; the launch traced here: 264 us
  waiting for transfers between devices  199 us (75%)
  matrix products  21.4 us (8%)
  local copies, waits for them, and re-layouts  18.1 us (7%)
  between operations  13.2 us (5%)
  starting transfers between devices  6.53 us (2%)
  other arithmetic  6.45 us (2%)
    reduce_scatter x1, waiting for transfers between devices, on_device(): lax.psum_scatter(cycle_part, 'ctr', scatter_dimension=1, tiled=True)  84 us
    all_gather x1, waiting for transfers between devices, on_device(): gathered = lax.all_gather(amps, 'col', axis=2, tiled=True)  47.1 us
    all_to_all x1, waiting for transfers between devices, on_device(): lax.all_to_all(gathered, 'ctr', split_axis=2, concat_axis=1, tiled=True)  44.7 us
    all_gather x1, waiting for transfers between devices, on_device(): lax.all_gather(w_cycle, 'row', axis=1, tiled=True)  21.3 us
    all_to_all x2, local copies, waits for them, and re-layouts, on_device(): lax.all_to_all(gathered, 'ctr', split_axis=2, concat_axis=1, tiled=True)  14.2 us
    dot_general x1, matrix products, on_device(): jnp.einsum('iakc,kcjb->iajb', t_sym, lax.all_gather(w_cycle, 'row', axis=...  11.3 us
    dot_general x1, matrix products, on_device(): jnp.einsum('idka,kdjb->iajb', t_sym, lax.all_gather(w_cross, 'row', axis=...  10.1 us
    all_to_all x1, starting transfers between devices, on_device(): lax.all_to_all(gathered, 'ctr', split_axis=2, concat_axis=1, tiled=True)  6.41 us
  transfers between devices with their start and end apart: 5, of which 4 were waited for; matrix products, arithmetic and copies ran while one was open for 9% of the time, Pallas kernels for 0%

commit v1 on v0

v1 whole, which is shorter than its diff:
```python
import jax
import jax.numpy as jnp
from jax import lax
from jax.sharding import PartitionSpec as P

FOLD = 256


def irreps_of(index, sizes):
    bounds = jnp.cumsum(sizes)[:7]
    return jnp.sum((index[..., None] >= bounds).astype(jnp.int32), axis=-1)


def fold(values, keep):
    kept = jnp.where(keep, values, jnp.zeros((), values.dtype))
    chunks = [kept[..., at : at + FOLD] for at in range(0, kept.shape[-1], FOLD)]
    return sum(chunks[1:], chunks[0])


def unfold(folded, keep):
    wide = jnp.concatenate([folded] * (keep.shape[-1] // FOLD), axis=-1)
    return jnp.where(keep, wide, jnp.zeros((), folded.dtype))


def shift(value, axis, count, step):
    return lax.ppermute(value, axis, [(at, (at + step) % count) for at in range(count)])


def swap(value, axis, count, mask):
    return lax.ppermute(value, axis, [(at, at ^ mask) for at in range(count)])


def on_device(amps, w_cycle, w_cross, occ_sizes, virt_sizes, slab_occ, k_occ, j_occ):
    ctr, row, col = lax.axis_index("ctr"), lax.axis_index("row"), lax.axis_index("col")
    virt = amps.shape[3]
    irr_v = irreps_of(jnp.arange(virt, dtype=jnp.int32), virt_sizes)
    irr_occ = irreps_of(jnp.concatenate([slab_occ, k_occ, j_occ]), occ_sizes)
    irr_i = lax.dynamic_slice_in_dim(irr_occ, row, 1)[0]
    irr_j = lax.dynamic_slice_in_dim(irr_occ, 20 + col, 1)[0]
    irr_kt = lax.dynamic_slice_in_dim(irr_occ, 4 + 4 * col, 4)
    irr_kw = lax.dynamic_slice_in_dim(irr_occ, 4 + 2 * ctr, 2)
    irr_a = lax.dynamic_slice_in_dim(irr_v, ctr * 128, 128)
    irr_c = lax.dynamic_slice_in_dim(irr_v, row * 256, 256)

    keep_w = (irr_kw ^ irr_j)[:, None, None] == (irr_c[:, None] ^ irr_v[None, :])[None]
    w = fold(w_cycle[:, :, 0, :], keep_w)
    u = fold(w_cross[:, :, 0, :], keep_w)
    w_up, u_down = shift(w, "row", 4, 1), shift(u, "row", 4, -1)
    w_down, u_up = shift(w, "row", 4, -1), shift(u, "row", 4, 1)
    w_far, u_far = shift(w_up, "row", 4, 1), shift(u_down, "row", 4, -1)

    keep_t = (irr_kt ^ irr_i)[:, None, None] == (irr_a[:, None] ^ irr_v[None, :])[None]
    t = fold(jnp.transpose(amps[0], (1, 0, 2)), keep_t)
    odd = ctr % 2
    arrived = []
    for flip in range(2):
        pairs = [
            (x * 4 + q, (2 * q + (x % 2 ^ flip)) * 4 + x // 2) for x in range(8) for q in range(4)
        ]
        piece = lax.dynamic_slice_in_dim(t, 2 * (odd ^ flip), 2)
        arrived.append(lax.ppermute(piece, ("ctr", "col"), pairs))
    quarter = jnp.stack(
        [
            jnp.where(odd == 0, arrived[0], arrived[1]),
            jnp.where(odd == 0, arrived[1], arrived[0]),
        ]
    )
    other = swap(quarter, "col", 4, 2)
    half = jnp.where(col // 2 == 0, jnp.stack([quarter, other]), jnp.stack([other, quarter]))
    there = swap(half, "col", 4, 1)
    odd_core = col % 2 == 1
    full = jnp.where(
        odd_core, jnp.stack([there, half], axis=1), jnp.stack([half, there], axis=1)
    )
    t_all = jnp.transpose(full.reshape(8, 2, 128, FOLD), (1, 0, 2, 3)).reshape(2, virt, FOLD)
    keep = (irr_kw ^ irr_i)[:, None, None] == (irr_v[:, None] ^ irr_v[None, :])[None]
    t_sym = unfold(t_all, keep)

    def laid(own, up, down, far):
        blocks = jnp.stack([own, up, far, down])
        order = (row - jnp.arange(4, dtype=jnp.int32)) % 4
        return jnp.transpose(blocks[order], (1, 0, 2, 3)).reshape(2, virt, FOLD)

    part = jnp.einsum(
        "kac,kcb->ab", t_sym, laid(w, w_up, w_down, w_far), preferred_element_type=jnp.float32
    ) + jnp.einsum(
        "kda,kdb->ab", t_sym, laid(u, u_up, u_down, u_far), preferred_element_type=jnp.float32
    )
    part = part.reshape(8, 128, FOLD)
    total = lax.dynamic_index_in_dim(part, ctr, 0, False)
    for mask in (4, 6, 5, 7, 2, 1, 3):
        total = total + swap(lax.dynamic_index_in_dim(part, ctr ^ mask, 0, False), "ctr", 8, mask)
    out_keep = (irr_a[:, None] ^ irr_v[None, :]) == (irr_i ^ irr_j)
    return unfold(total, out_keep).astype(jnp.bfloat16)[None, :, None, :]


def solution(mesh):
    return jax.shard_map(
        on_device,
        mesh=mesh,
        in_specs=(
            P("row", "ctr", "col", None),
            P("ctr", "row", "col", None),
            P("ctr", "row", "col", None),
            P(),
            P(),
            P(),
            P(),
            P(),
        ),
        out_specs=P("row", "ctr", "col", None),
        check_vma=False,
    )
```

time: 265 us -> 82.9 us (0.31)
  waiting for transfers between devices: 199 us -> 14.5 us
  starting transfers between devices: 6.53 us -> 33.1 us
  other arithmetic: 6.45 us -> 25.8 us
  matrix products: 21.4 us -> 2.57 us
  local copies, waits for them, and re-layouts: 18.1 us -> 4.98 us
  between operations: 13.2 us -> 1.68 us
    reduce_scatter x1 -> x0, waiting for transfers between devices: 84 us -> none  [on_device(): lax.psum_scatter(cycle_part, 'ctr', scatter_dimension=1, tiled=True)]
    all_gather x3 -> x0, waiting for transfers between devices: 68.4 us -> none  [the longest x1 47.1 us: on_device(): gathered = lax.all_gather(amps, 'col', axis=2, tiled=True)]
    all_to_all x1 -> x0, waiting for transfers between devices: 44.7 us -> none  [on_device(): lax.all_to_all(gathered, 'ctr', split_axis=2, concat_axis=1, tiled=True)]
    ppermute x0 -> x17, starting transfers between devices: none -> 33.1 us  [the longest x9 19.7 us: swap(): return lax.ppermute(value, axis, [(at, at ^ mask) for at in range(count)])]
    dot_general x2, matrix products: 21.4 us -> 2.57 us  [the longest x1 1.32 us: on_device(): jnp.einsum('kac,kcb->ab', t_sym, laid(w, w_up, w_down, w_far), preferred_...]
    ppermute x0 -> x17, waiting for transfers between devices: none -> 14.5 us  [the longest x9 8.13 us: swap(): return lax.ppermute(value, axis, [(at, at ^ mask) for at in range(count)])]
    all_to_all x2 -> x0, local copies, waits for them, and re-layouts: 14.2 us -> none  [on_device(): lax.all_to_all(gathered, 'ctr', split_axis=2, concat_axis=1, tiled=True)]
    select_n x0 -> x7, other arithmetic: none -> 12.9 us  [the longest x2 3.98 us: fold(): kept = jnp.where(keep, values, jnp.zeros((), values.dtype))]
  transfers between devices with their start and end apart: 5 -> 17, of which waited for: 4 -> 6; matrix products, arithmetic and copies ran while one was open for 9% -> 18% of each run, Pallas kernels for 0% -> 0%
where the time goes in v1:
time: 82.9 us; the launch traced here: 82.6 us
  starting transfers between devices  33.1 us (40%)
  other arithmetic  25.8 us (31%)
  waiting for transfers between devices  14.5 us (17%)
  local copies, waits for them, and re-layouts  4.98 us (6%)
  matrix products  2.57 us (3%)
  between operations  1.68 us (2%)
    ppermute x9, starting transfers between devices, swap(): return lax.ppermute(value, axis, [(at, at ^ mask) for at in range(count)])  19.7 us
    ppermute x6, starting transfers between devices, shift(): lax.ppermute(value, axis, [(at, (at + step) % count) for at in range(coun...  11 us
    ppermute x9, waiting for transfers between devices, swap(): return lax.ppermute(value, axis, [(at, at ^ mask) for at in range(count)])  8.13 us
    ppermute x6, waiting for transfers between devices, shift(): lax.ppermute(value, axis, [(at, (at + step) % count) for at in range(coun...  6.39 us
    select_n x2, other arithmetic, fold(): kept = jnp.where(keep, values, jnp.zeros((), values.dtype))  3.98 us
    select_n x1, other arithmetic, unfold(): return jnp.where(keep, wide, jnp.zeros((), folded.dtype))  3.44 us
    select_n x1, other arithmetic, on_device(): jnp.where(odd_core, jnp.stack([there, half], axis=1), jnp.stack([half, th...  3.07 us
    another operation x4, other arithmetic, laid(): blocks = jnp.stack([own, up, far, down])  2.5 us
  transfers between devices with their start and end apart: 17, of which 6 were waited for; matrix products, arithmetic and copies ran while one was open for 18% of the time, Pallas kernels for 0%

profile of v1, /device:TPU:0, one launch (start us, length us, event | category | flops | bytes accessed | tf_op | source)
XLA Modules:
  0.0 82.6 jit_solution(16364456713076396963)
XLA Ops:
  3.5 1.4 %broadcast_xor_fusion.3 = (s32[2]{0:T(128)S(1)}, s32[2]{0:T(128)S(1)}) fusion(s32[]{:T(128)} %bitcast.5, s32[24]{0:T(128)S(1)} %convert_reduce_fusion.1, s32[]{:T(128)S(6)} %select_n.162, s32[]{:T(128)} %bitcast.4), kind=kLoop, calls=%fused_computation.65 | loop fusion | flops 4 | bytes 36 | tf_op jit(solution)/shard_map/xor | solution.py:45
  4.9 1.9 %compare_select_fusion.2 = (bf16[2,256,1024]{2,1,0:T(8,128)(2,1)S(1)}, bf16[2,256,1024]{2,1,0:T(8,128)(2,1)S(1)}) fusion(bf16[2,256,1,1024]{3,1,2,0:T(8,128)(2,1)} %param.9, s32[256,1024]{1,0:T(8,128)S(1)} %broadcast_xor_fusion.1, s32[2]{0:T(128)S(1)} %get-tuple-element.18, bf16[2,256,1,1024]{3,1,2,0:T(8,128)(2,1)} %param.10), kind=kLoop, calls=%fused_computation.4 | loop fusion | flops 1572864 | bytes 5242888 | tf_op jit(solution)/shard_map/jit(_where)/select_n | solution.py:15
  6.8 4.2 %collective-permute-start.8 = (bf16[2,256,256]{2,1,0:T(8,128)(2,1)S(1)}, bf16[2,256,256]{2,1,0:T(8,128)(2,1)}, u32[]{:S(2)}, u32[]{:S(2)}) collective-permute-start(bf16[2,256,256]{2,1,0:T(8,128)(2,1)S(1)} %slice_add_fusion), channel_id=1, source_target_pairs={{0,12},{4,0},{8,4},{12,8},{1,13},{5,1},{9,5},{13,9},{2,14},{6,2},{... | collective-permute-start | bytes 786440 | tf_op jit(solution)/shard_map/ppermute | solution.py:26
  11.9 2.1 %compare_select_fusion.3 = bf16[4,128,1024]{2,0,1:T(4,128)(2,1)S(1)} fusion(bf16[1,128,4,1024]{3,2,1,0:T(4,128)(2,1)} %param.8, s32[128,1024]{1,0:T(8,128)S(1)} %broadcast_xor_fusion.2, s32[4]{0:T(128)S(1)} %dynamic-slice_xor_fusion), kind=kLoop, calls=%fused_computation.6 | loop fusion | flops 1048576 | bytes 2621456 | tf_op jit(solution)/shard_map/jit(_where)/select_n | solution.py:15
  15.2 1.7 %collective-permute-start.1 = (bf16[2,128,256]{2,0,1:T(2,128)(2,1)S(1)}, bf16[2,128,256]{2,0,1:T(2,128)(2,1)S(1)}, u32[]{:S(2)}, u32[]{:S(2)}) collective-permute-start(bf16[2,128,256]{2,0,1:T(2,128)(2,1)S(1)} %get-tuple-element.17), channel_id=1, source_target_pairs={{0,16},{1,48},{2,80},{3,112},{16,0},{17,32},{18,64},{19,96},{32,17... | collective-permute-start | bytes 393224 | tf_op jit(solution)/shard_map/ppermute | solution.py:61
  17.6 3.2 %collective-permute-start.6 = (bf16[2,256,256]{2,1,0:T(8,128)(2,1)}, bf16[2,256,256]{2,1,0:T(8,128)(2,1)}, u32[]{:S(2)}, u32[]{:S(2)}) collective-permute-start(bf16[2,256,256]{2,1,0:T(8,128)(2,1)} %slice_add_fusion.3), channel_id=1, source_target_pairs={{0,12},{4,0},{8,4},{12,8},{1,13},{5,1},{9,5},{13,9},{2,14},{6,2},{... | collective-permute-start | bytes 786440 | tf_op jit(solution)/shard_map/ppermute | solution.py:26
  20.8 2.3 %broadcast_xor_fusion = s32[1024,1024]{0,1:T(8,128)} fusion(s32[1024]{0:T(1024)S(1)} %convert_reduce_fusion), kind=kLoop, calls=%fused_computation.5 | loop fusion | flops 1048576 | bytes 4198400 | tf_op jit(solution)/shard_map/xor | solution.py:76
  23.9 4.3 %collective-permute-start.2 = (bf16[2,2,128,256]{3,1,2,0:T(2,128)(2,1)S(1)}, bf16[2,2,128,256]{3,1,2,0:T(2,128)(2,1)S(1)}, u32[]{:S(2)}, u32[]{:S(2)}) collective-permute-start(bf16[2,2,128,256]{3,1,2,0:T(2,128)(2,1)S(1)} %pad_maximum_fusion.2), channel_id=1, source_target_pairs={{0,2},{1,3},{2,0},{3,1},{4,6},{5,7},{6,4},{7,5},{8,10},{9,11},{10,... | collective-permute-start | bytes 786440 | tf_op jit(solution)/shard_map/ppermute | solution.py:30
  28.7 3.3 %collective-permute-start.9 = (bf16[2,256,256]{2,1,0:T(8,128)(2,1)}, bf16[2,256,256]{2,1,0:T(8,128)(2,1)S(1)}, u32[]{:S(2)}, u32[]{:S(2)}) collective-permute-start(bf16[2,256,256]{2,1,0:T(8,128)(2,1)} %collective-permute-done.8), channel_id=1, source_target_pairs={{0,12},{4,0},{8,4},{12,8},{1,13},{5,1},{9,5},{13,9},{2,14},{6,2},{... | collective-permute-start | bytes 786440 | tf_op jit(solution)/shard_map/ppermute | solution.py:26
  32.0 3.0 %collective-permute-done.2 = bf16[2,2,128,256]{3,1,2,0:T(2,128)(2,1)S(1)} collective-permute-done((bf16[2,2,128,256]{3,1,2,0:T(2,128)(2,1)S(1)}, bf16[2,2,128,256]{3,1,2,0:T(2,128)(2,1)S(1)}, u32[]{:S(2)}, u32[]{:S(2)}) %collective-permute-start.2) | collective-permute-done | bytes 262176 | tf_op jit(solution)/shard_map/ppermute | solution.py:30
  34.9 1.6 %broadcast_select_fusion.2 = bf16[2,2,2,128,256]{4,2,3,1,0:T(2,128)(2,1)} fusion(pred[]{:T(512)S(6)} %eq.74, bf16[1,2,2,128,256]{4,2,3,1,0:T(2,128)(2,1)S(1)} %bitcast.98, bf16[1,2,2,128,256]{4,2,3,1,0:T(2,128)(2,1)S(1)} %fusion.20), kind=kLoop, calls=%fused_computation.14 | loop fusion | flops 786432 | bytes 1048577 | tf_op jit(solution)/shard_map/jit(_where)/select_n | solution.py:69
  41.8 5.9 %collective-permute-done.5 = bf16[2,256,256]{2,1,0:T(8,128)(2,1)} collective-permute-done((bf16[2,256,256]{2,1,0:T(8,128)(2,1)}, bf16[2,256,256]{2,1,0:T(8,128)(2,1)}, u32[]{:S(2)}, u32[]{:S(2)}) %collective-permute-start.5) | collective-permute-done | bytes 262176 | tf_op jit(solution)/shard_map/ppermute | solution.py:26
  47.7 1.2 %pad_maximum_fusion = bf16[4,2,256,256]{3,2,1,0:T(8,128)(2,1)S(1)} fusion(bf16[1,2,256,256]{3,2,1,0:T(8,128)(2,1)} %bitcast.22, bf16[1,2,256,256]{3,2,1,0:T(8,128)(2,1)} %bitcast.21, bf16[1,2,256,256]{3,2,1,0:T(8,128)(2,1)} %bitcast.20, bf16[1,2,256,256]{3,2,1,0:T(8,128)(2,1)S(1)} %fusion.18), kind=kLoop, calls=%fused_computation.11 | loop fusion | flops 1572864 | bytes 2097152 | tf_op jit(solution)/shard_map/stack | solution.py:80
  49.7 3.1 %broadcast_select_fusion = bf16[2,2,2,2,128,256]{5,3,4,2,1,0:T(2,128)(2,1)S(1)} fusion(pred[]{:T(512)S(6)} %eq.73, bf16[2,1,2,2,128,256]{5,3,4,2,1,0:T(2,128)(2,1)S(1)} %broadcast_select_fusion.1, bf16[2,1,2,2,128,256]{5,3,4,2,1,0:T(2,128)(2,1)} %bitcast.12), kind=kLoop, calls=%fused_computation.7 | loop fusion | flops 1572864 | bytes 2097153 | tf_op jit(solution)/shard_map/jit(_where)/select_n | solution.py:72
  52.7 1.5 %copy.22 = bf16[2,1024,256]{1,2,0:T(8,128)(2,1)S(1)} copy(bf16[2,1024,256]{2,0,1:T(2,128)(2,1)S(1)} %bitcast.91) | data formatting | bytes 2097152 | tf_op jit(solution)/shard_map/reshape | solution.py:75
  54.2 3.4 %compare_select_fusion = bf16[2,1024,1024]{1,2,0:T(8,128)(2,1)S(1)} fusion(bf16[2,1024,256]{1,2,0:T(8,128)(2,1)S(1)} %copy.22, s32[1024,1024]{0,1:T(8,128)} %broadcast_xor_fusion, s32[2]{0:T(128)S(1)} %get-tuple-element.19), kind=kLoop, calls=%fused_computation.2 | loop fusion | flops 20971520 | bytes 9437192 | tf_op jit(solution)/shard_map/jit(_where)/select_n | solution.py:22
  57.7 1.3 %convolution_bitcast_fusion = f32[1024,256]{1,0:T(8,128)S(1)} fusion(bf16[2,1024,1024]{1,2,0:T(8,128)(2,1)S(1)} %compare_select_fusion, bf16[2,1024,256]{2,1,0:T(8,128)(2,1)S(1)} %bitcast.96), kind=kOutput, calls=%fused_computation.8 | convolution fusion | flops 1073741824 | bytes 6291456 | tf_op jit(solution)/shard_map/kda,kdb->ab/dot_general | solution.py:86
  58.9 1.3 %fusion = f32[1024,256]{1,0:T(8,128)S(1)} fusion(f32[1024,256]{1,0:T(8,128)S(1)} %convolution_bitcast_fusion, bf16[2,1024,1024]{1,2,0:T(8,128)(2,1)S(1)} %compare_select_fusion, bf16[2,1024,256]{2,1,0:T(8,128)(2,1)S(1)} %bitcast.97), kind=kOutput, calls=%fused_computation.10 | convolution fusion | flops 1074003968 | bytes 7340032 | tf_op jit(solution)/shard_map/kac,kcb->ab/dot_general | solution.py:84
  60.4 1.7 %collective-permute-start.16 = (f32[128,256]{1,0:T(8,128)S(1)}, f32[128,256]{1,0:T(8,128)S(1)}, u32[]{:S(2)}, u32[]{:S(2)}) collective-permute-start(f32[128,256]{1,0:T(8,128)S(1)} %get-tuple-element.8), channel_id=1, source_target_pairs={{0,48},{16,32},{32,16},{48,0},{64,112},{80,96},{96,80},{112,64},{1... | collective-permute-start | bytes 393224 | tf_op jit(solution)/shard_map/ppermute | solution.py:30
  62.0 3.1 %collective-permute-start.14 = (f32[128,256]{1,0:T(8,128)S(1)}, f32[128,256]{1,0:T(8,128)S(1)}, u32[]{:S(2)}, u32[]{:S(2)}) collective-permute-start(f32[128,256]{1,0:T(8,128)S(1)} %get-tuple-element.10), channel_id=1, source_target_pairs={{0,32},{16,48},{32,0},{48,16},{64,96},{80,112},{96,64},{112,80},{1... | collective-permute-start | bytes 393224 | tf_op jit(solution)/shard_map/ppermute | solution.py:30
  65.2 4.6 %collective-permute-start.13 = (f32[128,256]{1,0:T(8,128)S(1)}, f32[128,256]{1,0:T(8,128)S(1)}, u32[]{:S(2)}, u32[]{:S(2)}) collective-permute-start(f32[128,256]{1,0:T(8,128)S(1)} %get-tuple-element.11), channel_id=1, source_target_pairs={{0,112},{16,96},{32,80},{48,64},{64,48},{80,32},{96,16},{112,0},{1... | collective-permute-start | bytes 393224 | tf_op jit(solution)/shard_map/ppermute | solution.py:30
  69.7 5.5 %collective-permute-start.11 = (f32[128,256]{1,0:T(8,128)S(1)}, f32[128,256]{1,0:T(8,128)S(1)}, u32[]{:S(2)}, u32[]{:S(2)}) collective-permute-start(f32[128,256]{1,0:T(8,128)S(1)} %get-tuple-element.13), channel_id=1, source_target_pairs={{0,96},{16,112},{32,64},{48,80},{64,32},{80,48},{96,0},{112,16},{1... | collective-permute-start | bytes 393224 | tf_op jit(solution)/shard_map/ppermute | solution.py:30
  76.6 2.0 %collective-permute-done.12 = f32[128,256]{1,0:T(8,128)S(1)} collective-permute-done((f32[128,256]{1,0:T(8,128)S(1)}, f32[128,256]{1,0:T(8,128)S(1)}, u32[]{:S(2)}, u32[]{:S(2)}) %collective-permute-start.12) | collective-permute-done | bytes 131104 | tf_op jit(solution)/shard_map/ppermute | solution.py:30
  78.6 2.8 %collective-permute-done.11 = f32[128,256]{1,0:T(8,128)S(1)} collective-permute-done((f32[128,256]{1,0:T(8,128)S(1)}, f32[128,256]{1,0:T(8,128)S(1)}, u32[]{:S(2)}, u32[]{:S(2)}) %collective-permute-start.11) | collective-permute-done | bytes 131104 | tf_op jit(solution)/shard_map/ppermute | solution.py:30
  (57 shorter events, 14.8 us)
Async XLA Ops:
  6.8 21.9 %collective-permute-start.8 = (bf16[2,256,256]{2,1,0:T(8,128)(2,1)S(1)}, bf16[2,256,256]{2,1,0:T(8,128)(2,1)}, u32[]{:S(2)}, u32[]{:S(2)}) collective-permute-start(bf16[2,256,256]{2,1,0:T(8,128)(2,1)S(1)} %slice_add_fusion), channel_id=1, source_target_pairs={{0,12},{4,0},{8,4},{12,8},{1,13},{5,1},{9,5},{13,9},{2,14},{6,2},{... | collective-permute-start | bytes 786440 | tf_op jit(solution)/shard_map/ppermute | solution.py:26
  11.0 27.5 %collective-permute-start.7 = (bf16[2,256,256]{2,1,0:T(8,128)(2,1)S(1)}, bf16[2,256,256]{2,1,0:T(8,128)(2,1)}, u32[]{:S(2)}, u32[]{:S(2)}) collective-permute-start(bf16[2,256,256]{2,1,0:T(8,128)(2,1)S(1)} %slice_add_fusion), channel_id=1, source_target_pairs={{0,4},{4,8},{8,12},{12,0},{1,5},{5,9},{9,13},{13,1},{2,6},{6,10},{... | collective-permute-start | bytes 786440 | tf_op jit(solution)/shard_map/ppermute | solution.py:26
  14.5 8.7 %collective-permute-start = (bf16[2,128,256]{2,0,1:T(2,128)(2,1)S(1)}, bf16[2,128,256]{2,0,1:T(2,128)(2,1)S(1)}, u32[]{:S(2)}, u32[]{:S(2)}) collective-permute-start(bf16[2,128,256]{2,0,1:T(2,128)(2,1)S(1)} %get-tuple-element.16), channel_id=1, source_target_pairs={{0,0},{1,32},{2,64},{3,96},{16,16},{17,48},{18,80},{19,112},{32,1}... | collective-permute-start | bytes 393224 | tf_op jit(solution)/shard_map/ppermute | solution.py:61
  15.2 8.1 %collective-permute-start.1 = (bf16[2,128,256]{2,0,1:T(2,128)(2,1)S(1)}, bf16[2,128,256]{2,0,1:T(2,128)(2,1)S(1)}, u32[]{:S(2)}, u32[]{:S(2)}) collective-permute-start(bf16[2,128,256]{2,0,1:T(2,128)(2,1)S(1)} %get-tuple-element.17), channel_id=1, source_target_pairs={{0,16},{1,48},{2,80},{3,112},{16,0},{17,32},{18,64},{19,96},{32,17... | collective-permute-start | bytes 393224 | tf_op jit(solution)/shard_map/ppermute | solution.py:61
  17.6 24.2 %collective-permute-start.6 = (bf16[2,256,256]{2,1,0:T(8,128)(2,1)}, bf16[2,256,256]{2,1,0:T(8,128)(2,1)}, u32[]{:S(2)}, u32[]{:S(2)}) collective-permute-start(bf16[2,256,256]{2,1,0:T(8,128)(2,1)} %slice_add_fusion.3), channel_id=1, source_target_pairs={{0,12},{4,0},{8,4},{12,8},{1,13},{5,1},{9,5},{13,9},{2,14},{6,2},{... | collective-permute-start | bytes 786440 | tf_op jit(solution)/shard_map/ppermute | solution.py:26
  23.2 14.2 %collective-permute-start.4 = (bf16[2,256,256]{2,1,0:T(8,128)(2,1)}, bf16[2,256,256]{2,1,0:T(8,128)(2,1)}, u32[]{:S(2)}, u32[]{:S(2)}) collective-permute-start(bf16[2,256,256]{2,1,0:T(8,128)(2,1)} %slice_add_fusion.3), channel_id=1, source_target_pairs={{0,4},{4,8},{8,12},{12,0},{1,5},{5,9},{9,13},{13,1},{2,6},{6,10},{... | collective-permute-start | bytes 786440 | tf_op jit(solution)/shard_map/ppermute | solution.py:26
  23.9 11.0 %collective-permute-start.2 = (bf16[2,2,128,256]{3,1,2,0:T(2,128)(2,1)S(1)}, bf16[2,2,128,256]{3,1,2,0:T(2,128)(2,1)S(1)}, u32[]{:S(2)}, u32[]{:S(2)}) collective-permute-start(bf16[2,2,128,256]{3,1,2,0:T(2,128)(2,1)S(1)} %pad_maximum_fusion.2), channel_id=1, source_target_pairs={{0,2},{1,3},{2,0},{3,1},{4,6},{5,7},{6,4},{7,5},{8,10},{9,11},{10,... | collective-permute-start | bytes 786440 | tf_op jit(solution)/shard_map/ppermute | solution.py:30
  28.7 10.3 %collective-permute-start.9 = (bf16[2,256,256]{2,1,0:T(8,128)(2,1)}, bf16[2,256,256]{2,1,0:T(8,128)(2,1)S(1)}, u32[]{:S(2)}, u32[]{:S(2)}) collective-permute-start(bf16[2,256,256]{2,1,0:T(8,128)(2,1)} %collective-permute-done.8), channel_id=1, source_target_pairs={{0,12},{4,0},{8,4},{12,8},{1,13},{5,1},{9,5},{13,9},{2,14},{6,2},{... | collective-permute-start | bytes 786440 | tf_op jit(solution)/shard_map/ppermute | solution.py:26
  36.5 13.1 %collective-permute-start.3 = (bf16[2,2,2,128,256]{4,2,3,1,0:T(2,128)(2,1)}, bf16[2,2,2,128,256]{4,2,3,1,0:T(2,128)(2,1)}, u32[]{:S(2)}, u32[]{:S(2)}) collective-permute-start(bf16[2,2,2,128,256]{4,2,3,1,0:T(2,128)(2,1)} %broadcast_select_fusion.2), channel_id=1, source_target_pairs={{0,1},{1,0},{2,3},{3,2},{4,5},{5,4},{6,7},{7,6},{8,9},{9,8},{10,11... | collective-permute-start | bytes 1572872 | tf_op jit(solution)/shard_map/ppermute | solution.py:30
  37.5 10.2 %collective-permute-start.5 = (bf16[2,256,256]{2,1,0:T(8,128)(2,1)}, bf16[2,256,256]{2,1,0:T(8,128)(2,1)}, u32[]{:S(2)}, u32[]{:S(2)}) collective-permute-start(bf16[2,256,256]{2,1,0:T(8,128)(2,1)} %collective-permute-done.4), channel_id=1, source_target_pairs={{0,4},{4,8},{8,12},{12,0},{1,5},{5,9},{9,13},{13,1},{2,6},{6,10},{... | collective-permute-start | bytes 786440 | tf_op jit(solution)/shard_map/ppermute | solution.py:26
  54.2 3.5 %copy-start = (bf16[2,4,256,256]{3,2,1,0:T(8,128)(2,1)S(1)}, bf16[2,4,256,256]{3,2,1,0:T(8,128)(2,1)}, u32[]{:S(2)}) copy-start(bf16[2,4,256,256]{3,2,1,0:T(8,128)(2,1)} %copy.20) | copy-start | bytes 3145732
  60.4 9.4 %collective-permute-start.16 = (f32[128,256]{1,0:T(8,128)S(1)}, f32[128,256]{1,0:T(8,128)S(1)}, u32[]{:S(2)}, u32[]{:S(2)}) collective-permute-start(f32[128,256]{1,0:T(8,128)S(1)} %get-tuple-element.8), channel_id=1, source_target_pairs={{0,48},{16,32},{32,16},{48,0},{64,112},{80,96},{96,80},{112,64},{1... | collective-permute-start | bytes 393224 | tf_op jit(solution)/shard_map/ppermute | solution.py:30
  62.0 13.2 %collective-permute-start.15 = (f32[128,256]{1,0:T(8,128)S(1)}, f32[128,256]{1,0:T(8,128)S(1)}, u32[]{:S(2)}, u32[]{:S(2)}) collective-permute-start(f32[128,256]{1,0:T(8,128)S(1)} %get-tuple-element.9), channel_id=1, source_target_pairs={{0,16},{16,0},{32,48},{48,32},{64,80},{80,64},{96,112},{112,96},{1... | collective-permute-start | bytes 393224 | tf_op jit(solution)/shard_map/ppermute | solution.py:30
  62.0 14.5 %collective-permute-start.14 = (f32[128,256]{1,0:T(8,128)S(1)}, f32[128,256]{1,0:T(8,128)S(1)}, u32[]{:S(2)}, u32[]{:S(2)}) collective-permute-start(f32[128,256]{1,0:T(8,128)S(1)} %get-tuple-element.10), channel_id=1, source_target_pairs={{0,32},{16,48},{32,0},{48,16},{64,96},{80,112},{96,64},{112,80},{1... | collective-permute-start | bytes 393224 | tf_op jit(solution)/shard_map/ppermute | solution.py:30
  65.2 11.4 %collective-permute-start.13 = (f32[128,256]{1,0:T(8,128)S(1)}, f32[128,256]{1,0:T(8,128)S(1)}, u32[]{:S(2)}, u32[]{:S(2)}) collective-permute-start(f32[128,256]{1,0:T(8,128)S(1)} %get-tuple-element.11), channel_id=1, source_target_pairs={{0,112},{16,96},{32,80},{48,64},{64,48},{80,32},{96,16},{112,0},{1... | collective-permute-start | bytes 393224 | tf_op jit(solution)/shard_map/ppermute | solution.py:30
  69.7 8.8 %collective-permute-start.12 = (f32[128,256]{1,0:T(8,128)S(1)}, f32[128,256]{1,0:T(8,128)S(1)}, u32[]{:S(2)}, u32[]{:S(2)}) collective-permute-start(f32[128,256]{1,0:T(8,128)S(1)} %get-tuple-element.12), channel_id=1, source_target_pairs={{0,80},{16,64},{32,112},{48,96},{64,16},{80,0},{96,48},{112,32},{1... | collective-permute-start | bytes 393224 | tf_op jit(solution)/shard_map/ppermute | solution.py:30
  69.7 11.6 %collective-permute-start.11 = (f32[128,256]{1,0:T(8,128)S(1)}, f32[128,256]{1,0:T(8,128)S(1)}, u32[]{:S(2)}, u32[]{:S(2)}) collective-permute-start(f32[128,256]{1,0:T(8,128)S(1)} %get-tuple-element.13), channel_id=1, source_target_pairs={{0,96},{16,112},{32,64},{48,80},{64,32},{80,48},{96,0},{112,16},{1... | collective-permute-start | bytes 393224 | tf_op jit(solution)/shard_map/ppermute | solution.py:30
  75.2 6.5 %collective-permute-start.10 = (f32[128,256]{1,0:T(8,128)S(1)}, f32[128,256]{1,0:T(8,128)S(1)}, u32[]{:S(2)}, u32[]{:S(2)}) collective-permute-start(f32[128,256]{1,0:T(8,128)S(1)} %get-tuple-element.7), channel_id=1, source_target_pairs={{0,64},{16,80},{32,96},{48,112},{64,0},{80,16},{96,32},{112,48},{1... | collective-permute-start | bytes 393224 | tf_op jit(solution)/shard_map/ppermute | solution.py:30

commit v2 on v0

v2 whole, which is shorter than its diff:
```python
import functools

import jax
import jax.numpy as jnp
from jax import lax
from jax.experimental import pallas as pl
from jax.experimental.pallas import tpu as pltpu
from jax.sharding import PartitionSpec as P

FOLD = 256
SMEM = pl.BlockSpec(memory_space=pltpu.SMEM)
VMEM = pl.BlockSpec(memory_space=pltpu.VMEM)


def bounds_of(sizes_ref):
    total, bounds = sizes_ref[0], []
    for g in range(1, 8):
        bounds.append(total)
        total = total + sizes_ref[g]
    return bounds


def irrep(index, bounds):
    total = (index >= bounds[0]).astype(jnp.int32)
    for bound in bounds[1:]:
        total = total + (index >= bound).astype(jnp.int32)
    return total


def irrep_lanes(start, count, bounds):
    return irrep(lax.broadcasted_iota(jnp.int32, (1, count), 1) + start, bounds)


def irrep_rows(start, count, bounds):
    return irrep(lax.broadcasted_iota(jnp.int32, (count, 1), 0) + start, bounds)


def fold_of(load, want, lanes):
    total = None
    for at, irr in enumerate(lanes):
        kept = jnp.where(want == irr, load(at).astype(jnp.float32), 0.0)
        total = kept if total is None else total + kept
    return total


def fold_integrals(w_ref, u_ref, occ_ref, virt_ref, k_ref, j_ref, out_ref):
    ctr, row, col = lax.axis_index("ctr"), lax.axis_index("row"), lax.axis_index("col")
    occ, virt = bounds_of(occ_ref), bounds_of(virt_ref)
    lanes = [irrep_lanes(at * FOLD, FOLD, virt) for at in range(4)]
    rows = irrep_rows(row * 256, 256, virt)
    irr_j = irrep(j_ref[col], occ)
    for k in range(2):
        want = rows ^ (irr_j ^ irrep(k_ref[2 * ctr + k], occ))
        for n, ref in enumerate((w_ref, u_ref)):
            folded = fold_of(lambda at: ref[k, :, at * FOLD : (at + 1) * FOLD], want, lanes)
            out_ref[n, k] = folded.T.astype(out_ref.dtype)


def fold_amplitudes(t_ref, occ_ref, virt_ref, slab_ref, k_ref, out_ref):
    ctr, row, col = lax.axis_index("ctr"), lax.axis_index("row"), lax.axis_index("col")
    occ, virt = bounds_of(occ_ref), bounds_of(virt_ref)
    lanes = [irrep_lanes(at * FOLD, FOLD, virt) for at in range(4)]
    rows = irrep_rows(ctr * 128, 128, virt)
    irr_i = irrep(slab_ref[row], occ)
    for k in range(4):
        want = rows ^ (irr_i ^ irrep(k_ref[4 * col + k], occ))
        folded = fold_of(lambda at: t_ref[:, k, at * FOLD : (at + 1) * FOLD], want, lanes)
        out_ref[(ctr % 2) ^ (k // 2), k % 2] = folded.astype(out_ref.dtype)


def products(targets, *refs):
    (t0, t1, t2, t3, t4, own_ref, up_ref, down_ref, wfar_ref, ufar_ref, occ_ref, virt_ref, slab_ref, k_ref, out_ref, t_all) = refs
    ctr, row, col = lax.axis_index("ctr"), lax.axis_index("row"), lax.axis_index("col")
    occ, virt = bounds_of(occ_ref), bounds_of(virt_ref)
    odd, y = ctr % 2, ctr % 4
    for u in range(2):
        for k in range(2):
            t_all[k, 2 * col + (odd ^ u)] = (t0 if u == 0 else t1)[k]
            for flip, ref in ((2, t2), (1, t3), (3, t4)):
                t_all[k, 2 * (col ^ flip) + (odd ^ u)] = ref[u, k]
    irr_i = irrep(slab_ref[row], occ)
    away = [irr_i ^ irrep(k_ref[2 * ctr + k], occ) for k in range(2)]
    quarters = [row, (row + 3) % 4, (row + 1) % 4, (row + 2) % 4]
    w = [lambda k: own_ref[0, k], lambda k: up_ref[0, k], lambda k: down_ref[0, k], lambda k: wfar_ref[k]]
    u = [lambda k: own_ref[1, k], lambda k: up_ref[1, k], lambda k: down_ref[1, k], lambda k: ufar_ref[k]]
    q_lanes = [irrep_lanes(q * 256, 256, virt) for q in quarters]
    q_rows = [irrep_rows(q * 256, 256, virt) for q in quarters]
    dtype = t_all.dtype
    for at, ahead in enumerate(targets):
        to = (y + ahead) % 4
        a_rows = [irrep_rows((4 * h + to) * 128, 128, virt) for h in range(2)]
        a_lanes = [irrep_lanes((4 * h + to) * 128, 128, virt) for h in range(2)]
        total = jnp.zeros((FOLD, 256), jnp.float32)
        for k in range(2):
            left = [t_all[k, 4 * h + to].astype(jnp.float32) for h in range(2)]
            for n, q in enumerate(quarters):
                right = jnp.concatenate(
                    [jnp.where((a_rows[h] ^ away[k]) == q_lanes[n], left[h], 0.0) for h in range(2)], axis=0
                ).astype(dtype)
                total = total + lax.dot_general(
                    w[n](k), right, (((1,), (1,)), ((), ())), preferred_element_type=jnp.float32
                )
                both = t_all[k, pl.ds(2 * q, 2)].reshape(256, FOLD).astype(jnp.float32)
                half = jnp.where(to % 2 == 0, both[:, :128], both[:, 128:])
                right = jnp.concatenate(
                    [jnp.where((q_rows[n] ^ away[k]) == a_lanes[h], half, 0.0) for h in range(2)], axis=1
                ).astype(dtype)
                total = total + lax.dot_general(
                    u[n](k), right, (((1,), (0,)), ((), ())), preferred_element_type=jnp.float32
                )
        out_ref[at, 0] = total[:, :128]
        out_ref[at, 1] = total[:, 128:]


def finish(own_ref, up_ref, down_ref, across_ref, occ_ref, virt_ref, slab_ref, j_ref, out_ref):
    ctr, row, col = lax.axis_index("ctr"), lax.axis_index("row"), lax.axis_index("col")
    occ, virt = bounds_of(occ_ref), bounds_of(virt_ref)
    h = ctr // 4
    total = (own_ref[h] + up_ref[h] + down_ref[h] + across_ref[...]).T
    want = irrep_rows(ctr * 128, 128, virt) ^ (irrep(slab_ref[row], occ) ^ irrep(j_ref[col], occ))
    for at in range(4):
        kept = jnp.where(want == irrep_lanes(at * FOLD, FOLD, virt), total, 0.0)
        out_ref[:, at * FOLD : (at + 1) * FOLD] = kept.astype(out_ref.dtype)


def call(kernel, shape, dtype, arrays, scalars, scratch=(), flops=0, name=None):
    return pl.pallas_call(
        kernel,
        out_shape=jax.ShapeDtypeStruct(shape, dtype),
        in_specs=[VMEM] * len(arrays) + [SMEM] * len(scalars),
        out_specs=VMEM,
        scratch_shapes=scratch,
        compiler_params=pltpu.CompilerParams(vmem_limit_bytes=40 << 20),
        cost_estimate=pl.CostEstimate(flops=flops, bytes_accessed=1 << 20, transcendentals=0),
        name=name,
    )(*arrays, *scalars)


def shift(value, axis, count, step):
    return lax.ppermute(value, axis, [(at, (at + step) % count) for at in range(count)])


def shift_y(value, step):
    return lax.ppermute(value, "ctr", [(at, at // 4 * 4 + (at + step) % 4) for at in range(8)])


def swap(value, axis, count, mask):
    return lax.ppermute(value, axis, [(at, at ^ mask) for at in range(count)])


def on_device(amps, w_cycle, w_cross, occ_sizes, virt_sizes, slab_occ, k_occ, j_occ):
    bf16, f32 = jnp.bfloat16, jnp.float32
    own = call(
        fold_integrals, (2, 2, FOLD, 256), bf16, [w_cycle[:, :, 0], w_cross[:, :, 0]],
        [occ_sizes, virt_sizes, k_occ, j_occ], name="fold_integrals",
    )
    up, down = shift(own, "row", 4, 1), shift(own, "row", 4, -1)
    w_far, u_far = shift(up[0], "row", 4, 1), shift(down[1], "row", 4, -1)

    t = call(
        fold_amplitudes, (2, 2, 128, FOLD), bf16, [amps[0]],
        [occ_sizes, virt_sizes, slab_occ, k_occ], name="fold_amplitudes",
    )
    arrived = []
    for flip in range(2):
        pairs = [
            (x * 4 + q, (2 * q + (x % 2 ^ flip)) * 4 + x // 2) for x in range(8) for q in range(4)
        ]
        arrived.append(lax.ppermute(t[flip], ("ctr", "col"), pairs))
    quarter = jnp.stack(arrived)
    beside = swap(quarter, "col", 4, 2)
    there, beyond = swap(quarter, "col", 4, 1), swap(beside, "col", 4, 1)

    args = [*arrived, beside, there, beyond, own, up, down, w_far, u_far]
    scalars = [occ_sizes, virt_sizes, slab_occ, k_occ]

    def form(targets):
        return call(
            functools.partial(products, targets), (len(targets), 2, FOLD, 128), f32, args, scalars,
            [pltpu.VMEM((2, 8, 128, FOLD), bf16)], flops=len(targets) << 29, name="products",
        )

    far = form((2,))[0]
    near = form((1, 3, 0))
    from_below, from_above = shift_y(far[0], 1), shift_y(far[1], -1)
    low = shift_y(near[0].at[0].add(from_below), 1)
    high = shift_y(near[1].at[1].add(from_above), -1)
    other = 1 - lax.axis_index("ctr") // 4
    pick = lambda value: lax.dynamic_index_in_dim(value, other, 0, False)
    across = swap(pick(near[2]) + pick(low) + pick(high), "ctr", 8, 4)
    out = call(
        finish, (128, 4 * FOLD), bf16, [near[2], low, high, across],
        [occ_sizes, virt_sizes, slab_occ, j_occ], name="finish",
    )
    return out[None, :, None, :]


def solution(mesh):
    return jax.shard_map(
        on_device,
        mesh=mesh,
        in_specs=(
            P("row", "ctr", "col", None),
            P("ctr", "row", "col", None),
            P("ctr", "row", "col", None),
            P(),
            P(),
            P(),
            P(),
            P(),
        ),
        out_specs=P("row", "ctr", "col", None),
        check_vma=False,
    )
```

time: 265 us -> 65.7 us (0.25)
  waiting for transfers between devices: 199 us -> 24.9 us
  matrix products: 21.4 us -> 0 us
  starting transfers between devices: 6.53 us -> 26.9 us
  local copies, waits for them, and re-layouts: 18.1 us -> 3.3 us
  between operations: 13.2 us -> 0.12 us
  Pallas kernels: 0 us -> 9.36 us
  other arithmetic: 6.45 us -> 0.08 us
    reduce_scatter x1 -> x0, waiting for transfers between devices: 84 us -> none  [on_device(): lax.psum_scatter(cycle_part, 'ctr', scatter_dimension=1, tiled=True)]
    all_gather x3 -> x0, waiting for transfers between devices: 68.4 us -> none  [the longest x1 47.1 us: on_device(): gathered = lax.all_gather(amps, 'col', axis=2, tiled=True)]
    all_to_all x1 -> x0, waiting for transfers between devices: 44.7 us -> none  [on_device(): lax.all_to_all(gathered, 'ctr', split_axis=2, concat_axis=1, tiled=True)]
    ppermute x0 -> x14, starting transfers between devices: none -> 26.9 us  [the longest x4 14 us: swap(): return lax.ppermute(value, axis, [(at, at ^ mask) for at in range(count)])]
    ppermute x0 -> x14, waiting for transfers between devices: none -> 24.9 us  [the longest x4 7.91 us: shift_y(): lax.ppermute(value, 'ctr', [(at, at // 4 * 4 + (at + step) % 4) for at in...]
    dot_general x2 -> x0, matrix products: 21.4 us -> none  [the longest x1 11.3 us: on_device(): jnp.einsum('iakc,kcjb->iajb', t_sym, lax.all_gather(w_cycle, 'row', axis=...]
    all_to_all x2 -> x0, local copies, waits for them, and re-layouts: 14.2 us -> none  [on_device(): lax.all_to_all(gathered, 'ctr', split_axis=2, concat_axis=1, tiled=True)]
    pallas_call x0 -> x5, Pallas kernels: none -> 9.36 us  [call(): pl.pallas_call(kernel, out_shape=jax.ShapeDtypeStruct(shape, dtype), in_s...]
  transfers between devices with their start and end apart: 5 -> 14, of which waited for: 4 -> 8; matrix products, arithmetic and copies ran while one was open for 9% -> 0% of each run, Pallas kernels for 0% -> 7%
where the time goes in v2:
time: 65.7 us; the launch traced here: 64.7 us
  starting transfers between devices  26.9 us (41%)
  waiting for transfers between devices  24.9 us (38%)
  Pallas kernels  9.36 us (14%)
  local copies, waits for them, and re-layouts  3.3 us (5%)
    ppermute x4, starting transfers between devices, swap(): return lax.ppermute(value, axis, [(at, at ^ mask) for at in range(count)])  14 us
    pallas_call x5, Pallas kernels, call(): pl.pallas_call(kernel, out_shape=jax.ShapeDtypeStruct(shape, dtype), in_s...  9.36 us
    ppermute x4, waiting for transfers between devices, shift_y(): lax.ppermute(value, 'ctr', [(at, at // 4 * 4 + (at + step) % 4) for at in...  7.91 us
    ppermute x4, waiting for transfers between devices, shift(): lax.ppermute(value, axis, [(at, (at + step) % count) for at in range(coun...  7.5 us
    ppermute x4, waiting for transfers between devices, swap(): return lax.ppermute(value, axis, [(at, at ^ mask) for at in range(count)])  6.89 us
    ppermute x4, starting transfers between devices, shift(): lax.ppermute(value, axis, [(at, (at + step) % count) for at in range(coun...  6.43 us
    ppermute x4, starting transfers between devices, shift_y(): lax.ppermute(value, 'ctr', [(at, at // 4 * 4 + (at + step) % 4) for at in...  4.19 us
    unnamed x16, local copies, waits for them, and re-layouts  3.16 us
  transfers between devices with their start and end apart: 14, of which 8 were waited for; matrix products, arithmetic and copies ran while one was open for 0% of the time, Pallas kernels for 7%

profile of v2, /device:TPU:0, one launch (start us, length us, event | category | flops | bytes accessed | tf_op | source)
XLA Modules:
  0.0 64.7 jit_solution(15442361789442944862)
XLA Ops:
  0.7 1.2 %copy-done.1 = bf16[2,256,1,1024]{3,1,2,0:T(8,128)(2,1)S(1)} copy-done((bf16[2,256,1,1024]{3,1,2,0:T(8,128)(2,1)S(1)}, bf16[2,256,1,1024]{3,1,2,0:T(8,128)(2,1)}, u32[]{:S(2)}) %copy-start.1) | copy-done | bytes 1048600
  1.9 1.2 %copy-done.2 = bf16[2,256,1,1024]{3,1,2,0:T(8,128)(2,1)S(1)} copy-done((bf16[2,256,1,1024]{3,1,2,0:T(8,128)(2,1)S(1)}, bf16[2,256,1,1024]{3,1,2,0:T(8,128)(2,1)}, u32[]{:S(2)}) %copy-start.2) | copy-done | bytes 1048600
  3.2 1.3 %fold_integrals.1.refs_5_ = bf16[2,2,256,256]{3,2,1,0:T(8,128)(2,1)S(1)} custom-call(bf16[2,256,1024]{2,1,0:T(8,128)(2,1)S(1)} %bitcast.57, bf16[2,256,1024]{2,1,0:T(8,128)(2,1)S(1)} %bitcast.58, s32[8]{0:T(128)S(1)} %copy-done.3, s32[8]{0:T(128)S(1)} %copy-done.4, s32[16]{0:T(128)S(1)} %copy-done.5, s32[4]{0:T(128)S(1)} %copy-done.7), custom_call_target="tpu_custom_call" | custom-call | bytes 1048576 | tf_op jit(solution)/shard_map/fold_integrals/pallas_call | solution.py:127
  4.5 4.2 %collective-permute-start.6 = (bf16[2,2,256,256]{3,2,1,0:T(8,128)(2,1)S(1)}, bf16[2,2,256,256]{3,2,1,0:T(8,128)(2,1)S(1)}, u32[]{:S(2)}, u32[]{:S(2)}) collective-permute-start(bf16[2,2,256,256]{3,2,1,0:T(8,128)(2,1)S(1)} %fold_integrals.1.refs_5_), channel_id=1, source_target_pairs={{0,12},{4,0},{8,4},{12,8},{1,13},{5,1},{9,5},{13,9},{2,14},{6,2},{... | collective-permute-start | bytes 1572872 | tf_op jit(solution)/shard_map/ppermute | solution.py:140
  8.7 1.8 %fold_amplitudes.1 = bf16[2,2,128,256]{3,2,1,0:T(8,128)(2,1)S(1)} custom-call(bf16[128,4,1024]{2,1,0:T(4,128)(2,1)S(1)} %bitcast.56, s32[8]{0:T(128)S(1)} %copy-done.3, s32[8]{0:T(128)S(1)} %copy-done.4, s32[4]{0:T(128)S(1)} %copy-done.6, s32[16]{0:T(128)S(1)} %copy-done.5), custom_call_target="tpu_custom_call" | custom-call | bytes 1048576 | tf_op jit(solution)/shard_map/fold_amplitudes/pallas_call | solution.py:127
  10.5 1.7 %collective-permute-start.1 = (bf16[2,128,256]{2,1,0:T(8,128)(2,1)S(1)}, bf16[2,128,256]{2,1,0:T(8,128)(2,1)S(1)}, u32[]{:S(2)}, u32[]{:S(2)}) collective-permute-start(bf16[2,128,256]{2,1,0:T(8,128)(2,1)S(1)} %get-tuple-element.37), channel_id=1, source_target_pairs={{0,16},{1,48},{2,80},{3,112},{16,0},{17,32},{18,64},{19,96},{32,17... | collective-permute-start | bytes 393224 | tf_op jit(solution)/shard_map/ppermute | solution.py:169
  12.9 2.6 %collective-permute-done.1.refs_1_ = bf16[2,128,256]{2,1,0:T(8,128)(2,1)S(1)} collective-permute-done((bf16[2,128,256]{2,1,0:T(8,128)(2,1)S(1)}, bf16[2,128,256]{2,1,0:T(8,128)(2,1)S(1)}, u32[]{:S(2)}, u32[]{:S(2)}) %collective-permute-start.1) | collective-permute-done | bytes 131104 | tf_op jit(solution)/shard_map/ppermute | solution.py:169
  15.6 7.3 %collective-permute-start.2 = (bf16[2,2,128,256]{3,2,1,0:T(8,128)(2,1)S(1)}, bf16[2,2,128,256]{3,2,1,0:T(8,128)(2,1)S(1)}, u32[]{:S(2)}, u32[]{:S(2)}) collective-permute-start(bf16[2,2,128,256]{3,2,1,0:T(8,128)(2,1)S(1)} %pad_maximum_fusion), channel_id=1, source_target_pairs={{0,2},{1,3},{2,0},{3,1},{4,6},{5,7},{6,4},{7,5},{8,10},{9,11},{10,... | collective-permute-start | bytes 786440 | tf_op jit(solution)/shard_map/ppermute | solution.py:148
  22.8 1.8 %collective-permute-start.3 = (bf16[2,2,128,256]{3,2,1,0:T(8,128)(2,1)S(1)}, bf16[2,2,128,256]{3,2,1,0:T(8,128)(2,1)S(1)}, u32[]{:S(2)}, u32[]{:S(2)}) collective-permute-start(bf16[2,2,128,256]{3,2,1,0:T(8,128)(2,1)S(1)} %pad_maximum_fusion), channel_id=1, source_target_pairs={{0,1},{1,0},{2,3},{3,2},{4,5},{5,4},{6,7},{7,6},{8,9},{9,8},{10,11... | collective-permute-start | bytes 786440 | tf_op jit(solution)/shard_map/ppermute | solution.py:148
  24.6 3.9 %collective-permute-done.2.refs_2_ = bf16[2,2,128,256]{3,2,1,0:T(8,128)(2,1)S(1)} collective-permute-done((bf16[2,2,128,256]{3,2,1,0:T(8,128)(2,1)S(1)}, bf16[2,2,128,256]{3,2,1,0:T(8,128)(2,1)S(1)}, u32[]{:S(2)}, u32[]{:S(2)}) %collective-permute-start.2) | collective-permute-done | bytes 262176 | tf_op jit(solution)/shard_map/ppermute | solution.py:148
  28.6 1.3 %collective-permute-start.4 = (bf16[2,2,128,256]{3,2,1,0:T(8,128)(2,1)S(1)}, bf16[2,2,128,256]{3,2,1,0:T(8,128)(2,1)S(1)}, u32[]{:S(2)}, u32[]{:S(2)}) collective-permute-start(bf16[2,2,128,256]{3,2,1,0:T(8,128)(2,1)S(1)} %collective-permute-done.2.refs_2_), channel_id=1, source_target_pairs={{0,1},{1,0},{2,3},{3,2},{4,5},{5,4},{6,7},{7,6},{8,9},{9,8},{10,11... | collective-permute-start | bytes 786440 | tf_op jit(solution)/shard_map/ppermute | solution.py:148
  30.3 1.7 %collective-permute-start.7 = (bf16[2,256,256]{2,1,0:T(8,128)(2,1)S(1)}, bf16[2,256,256]{2,1,0:T(8,128)(2,1)S(1)}, u32[]{:S(2)}, u32[]{:S(2)}) collective-permute-start(bf16[2,256,256]{2,1,0:T(8,128)(2,1)S(1)} %slice_bitcast_fusion.3), channel_id=1, source_target_pairs={{0,4},{4,8},{8,12},{12,0},{1,5},{5,9},{9,13},{13,1},{2,6},{6,10},{... | collective-permute-start | bytes 786440 | tf_op jit(solution)/shard_map/ppermute | solution.py:140
  32.0 6.1 %collective-permute-done.8.refs_9_ = bf16[2,256,256]{2,1,0:T(8,128)(2,1)S(1)} collective-permute-done((bf16[2,256,256]{2,1,0:T(8,128)(2,1)S(1)}, bf16[2,256,256]{2,1,0:T(8,128)(2,1)S(1)}, u32[]{:S(2)}, u32[]{:S(2)}) %collective-permute-start.8) | collective-permute-done | bytes 262176 | tf_op jit(solution)/shard_map/ppermute | solution.py:140
  38.1 1.4 %collective-permute-done.7.refs_8_ = bf16[2,256,256]{2,1,0:T(8,128)(2,1)S(1)} collective-permute-done((bf16[2,256,256]{2,1,0:T(8,128)(2,1)S(1)}, bf16[2,256,256]{2,1,0:T(8,128)(2,1)S(1)}, u32[]{:S(2)}, u32[]{:S(2)}) %collective-permute-start.7) | collective-permute-done | bytes 262176 | tf_op jit(solution)/shard_map/ppermute | solution.py:140
  39.5 1.8 %products.3 = f32[1,2,256,128]{3,2,1,0:T(8,128)S(1)} custom-call(bf16[2,128,256]{2,1,0:T(8,128)(2,1)S(1)} %collective-permute-done.refs_0_, bf16[2,128,256]{2,1,0:T(8,128)(2,1)S(1)} %collective-permute-done.1.refs_1_, bf16[2,2,128,256]{3,2,1,0:T(8,128)(2,1)S(1)} %collective-permute-done.2.refs_2_, ...), custom_call_target="tpu_custom_call" | custom-call | flops 536870912 | bytes 1048576 | tf_op jit(solution)/shard_map/products/pallas_call | solution.py:127
  42.1 1.3 %collective-permute-start.9 = (f32[256,128]{1,0:T(8,128)S(1)}, f32[256,128]{1,0:T(8,128)S(1)}, u32[]{:S(2)}, u32[]{:S(2)}) collective-permute-start(f32[256,128]{1,0:T(8,128)S(1)} %get-tuple-element.36), channel_id=1, source_target_pairs={{0,16},{16,32},{32,48},{48,0},{64,80},{80,96},{96,112},{112,64},{1... | collective-permute-start | bytes 393224 | tf_op jit(solution)/shard_map/ppermute | solution.py:144
  43.5 3.1 %products.2 = f32[3,2,256,128]{3,2,1,0:T(8,128)S(1)} custom-call(bf16[2,128,256]{2,1,0:T(8,128)(2,1)S(1)} %collective-permute-done.refs_0_, bf16[2,128,256]{2,1,0:T(8,128)(2,1)S(1)} %collective-permute-done.1.refs_1_, bf16[2,2,128,256]{3,2,1,0:T(8,128)(2,1)S(1)} %collective-permute-done.2.refs_2_, ...), custom_call_target="tpu_custom_call" | custom-call | flops 1610612736 | bytes 1048576 | tf_op jit(solution)/shard_map/products/pallas_call | solution.py:127
  46.6 1.7 %collective-permute-done.9 = f32[256,128]{1,0:T(8,128)S(1)} collective-permute-done((f32[256,128]{1,0:T(8,128)S(1)}, f32[256,128]{1,0:T(8,128)S(1)}, u32[]{:S(2)}, u32[]{:S(2)}) %collective-permute-start.9) | collective-permute-done | bytes 131104 | tf_op jit(solution)/shard_map/ppermute | solution.py:144
  48.6 1.8 %collective-permute-start.10 = (f32[2,256,128]{2,1,0:T(8,128)S(1)}, f32[2,256,128]{2,1,0:T(8,128)S(1)}, u32[]{:S(2)}, u32[]{:S(2)}) collective-permute-start(f32[2,256,128]{2,1,0:T(8,128)S(1)} %get-tuple-element.34), channel_id=1, source_target_pairs={{0,16},{16,32},{32,48},{48,0},{64,80},{80,96},{96,112},{112,64},{1... | collective-permute-start | bytes 786440 | tf_op jit(solution)/shard_map/ppermute | solution.py:144
  50.5 4.3 %collective-permute-done.12.down_ref = f32[2,256,128]{2,1,0:T(8,128)S(1)} collective-permute-done((f32[2,256,128]{2,1,0:T(8,128)S(1)}, f32[2,256,128]{2,1,0:T(8,128)S(1)}, u32[]{:S(2)}, u32[]{:S(2)}) %collective-permute-start.12) | collective-permute-done | bytes 262176 | tf_op jit(solution)/shard_map/ppermute | solution.py:144
  54.8 1.8 %collective-permute-done.10.up_ref = f32[2,256,128]{2,1,0:T(8,128)S(1)} collective-permute-done((f32[2,256,128]{2,1,0:T(8,128)S(1)}, f32[2,256,128]{2,1,0:T(8,128)S(1)}, u32[]{:S(2)}, u32[]{:S(2)}) %collective-permute-start.10) | collective-permute-done | bytes 262176 | tf_op jit(solution)/shard_map/ppermute | solution.py:144
  56.7 3.7 %collective-permute-start.13 = (f32[256,128]{1,0:T(8,128)S(1)}, f32[256,128]{1,0:T(8,128)S(1)}, u32[]{:S(2)}, u32[]{:S(2)}) collective-permute-start(f32[256,128]{1,0:T(8,128)S(1)} %bitcast_add_fusion), channel_id=1, source_target_pairs={{0,64},{16,80},{32,96},{48,112},{64,0},{80,16},{96,32},{112,48},{1... | collective-permute-start | bytes 393224 | tf_op jit(solution)/shard_map/ppermute | solution.py:148
  60.4 2.9 %collective-permute-done.13.across_ref = f32[256,128]{1,0:T(8,128)S(1)} collective-permute-done((f32[256,128]{1,0:T(8,128)S(1)}, f32[256,128]{1,0:T(8,128)S(1)}, u32[]{:S(2)}, u32[]{:S(2)}) %collective-permute-start.13) | collective-permute-done | bytes 131104 | tf_op jit(solution)/shard_map/ppermute | solution.py:148
  63.3 1.4 %finish.1 = bf16[128,1024]{1,0:T(8,128)(2,1)} custom-call(f32[2,256,128]{2,1,0:T(8,128)S(1)} %get-tuple-element.30.own_ref, f32[2,256,128]{2,1,0:T(8,128)S(1)} %collective-permute-done.10.up_ref, f32[2,256,128]{2,1,0:T(8,128)S(1)} %collective-permute-done.12.down_ref, f32[256,128]{1,0:T(8,128)S(1)} %collective-permute-done.13.across_ref, s32[8]{0:T(128)S(1)} %copy-done.3, ...), custom_call_target="tpu_custom_call" | custom-call | bytes 1048576 | tf_op jit(solution)/shard_map/finish/pallas_call | solution.py:127
  (33 shorter events, 3.2 us)
Async XLA Ops:
  0.0 0.7 %copy-start.7 = (s32[4]{0:T(128)S(1)}, s32[4]{0:T(128)}, u32[]{:S(2)}) copy-start(s32[4]{0:T(128)} %j_ref.3) | copy-start | bytes 52
  0.0 0.7 %copy-start.3 = (s32[8]{0:T(128)S(1)}, s32[8]{0:T(128)}, u32[]{:S(2)}) copy-start(s32[8]{0:T(128)} %occ_ref.5) | copy-start | bytes 100
  0.0 0.7 %copy-start.4 = (s32[8]{0:T(128)S(1)}, s32[8]{0:T(128)}, u32[]{:S(2)}) copy-start(s32[8]{0:T(128)} %virt_ref.5) | copy-start | bytes 100
  0.0 0.7 %copy-start.5 = (s32[16]{0:T(128)S(1)}, s32[16]{0:T(128)}, u32[]{:S(2)}) copy-start(s32[16]{0:T(128)} %refs_13_.3) | copy-start | bytes 196
  0.7 1.2 %copy-start.1 = (bf16[2,256,1,1024]{3,1,2,0:T(8,128)(2,1)S(1)}, bf16[2,256,1,1024]{3,1,2,0:T(8,128)(2,1)}, u32[]{:S(2)}) copy-start(bf16[2,256,1,1024]{3,1,2,0:T(8,128)(2,1)} %param.13) | copy-start | bytes 3145732
  1.9 1.2 %copy-start.2 = (bf16[2,256,1,1024]{3,1,2,0:T(8,128)(2,1)S(1)}, bf16[2,256,1,1024]{3,1,2,0:T(8,128)(2,1)}, u32[]{:S(2)}) copy-start(bf16[2,256,1,1024]{3,1,2,0:T(8,128)(2,1)} %param.14) | copy-start | bytes 3145732
  3.2 5.5 %copy-start = (bf16[1,128,4,1024]{3,2,1,0:T(4,128)(2,1)S(1)}, bf16[1,128,4,1024]{3,2,1,0:T(4,128)(2,1)}, u32[]{:S(2)}) copy-start(bf16[1,128,4,1024]{3,2,1,0:T(4,128)(2,1)} %param.12) | copy-start | bytes 3145732
  4.5 4.2 %copy-start.6 = (s32[4]{0:T(128)S(1)}, s32[4]{0:T(128)}, u32[]{:S(2)}) copy-start(s32[4]{0:T(128)} %slab_ref.3) | copy-start | bytes 52
  4.5 25.3 %collective-permute-start.6 = (bf16[2,2,256,256]{3,2,1,0:T(8,128)(2,1)S(1)}, bf16[2,2,256,256]{3,2,1,0:T(8,128)(2,1)S(1)}, u32[]{:S(2)}, u32[]{:S(2)}) collective-permute-start(bf16[2,2,256,256]{3,2,1,0:T(8,128)(2,1)S(1)} %fold_integrals.1.refs_5_), channel_id=1, source_target_pairs={{0,12},{4,0},{8,4},{12,8},{1,13},{5,1},{9,5},{13,9},{2,14},{6,2},{... | collective-permute-start | bytes 1572872 | tf_op jit(solution)/shard_map/ppermute | solution.py:140
  10.5 5.0 %collective-permute-start.1 = (bf16[2,128,256]{2,1,0:T(8,128)(2,1)S(1)}, bf16[2,128,256]{2,1,0:T(8,128)(2,1)S(1)}, u32[]{:S(2)}, u32[]{:S(2)}) collective-permute-start(bf16[2,128,256]{2,1,0:T(8,128)(2,1)S(1)} %get-tuple-element.37), channel_id=1, source_target_pairs={{0,16},{1,48},{2,80},{3,112},{16,0},{17,32},{18,64},{19,96},{32,17... | collective-permute-start | bytes 393224 | tf_op jit(solution)/shard_map/ppermute | solution.py:169
  12.1 3.4 %collective-permute-start = (bf16[2,128,256]{2,1,0:T(8,128)(2,1)S(1)}, bf16[2,128,256]{2,1,0:T(8,128)(2,1)S(1)}, u32[]{:S(2)}, u32[]{:S(2)}) collective-permute-start(bf16[2,128,256]{2,1,0:T(8,128)(2,1)S(1)} %get-tuple-element.38), channel_id=1, source_target_pairs={{0,0},{1,32},{2,64},{3,96},{16,16},{17,48},{18,80},{19,112},{32,1}... | collective-permute-start | bytes 393224 | tf_op jit(solution)/shard_map/ppermute | solution.py:169
  12.8 17.5 %collective-permute-start.5 = (bf16[2,2,256,256]{3,2,1,0:T(8,128)(2,1)S(1)}, bf16[2,2,256,256]{3,2,1,0:T(8,128)(2,1)S(1)}, u32[]{:S(2)}, u32[]{:S(2)}) collective-permute-start(bf16[2,2,256,256]{3,2,1,0:T(8,128)(2,1)S(1)} %fold_integrals.1.refs_5_), channel_id=1, source_target_pairs={{0,4},{4,8},{8,12},{12,0},{1,5},{5,9},{9,13},{13,1},{2,6},{6,10},{... | collective-permute-start | bytes 1572872 | tf_op jit(solution)/shard_map/ppermute | solution.py:140
  15.6 13.0 %collective-permute-start.2 = (bf16[2,2,128,256]{3,2,1,0:T(8,128)(2,1)S(1)}, bf16[2,2,128,256]{3,2,1,0:T(8,128)(2,1)S(1)}, u32[]{:S(2)}, u32[]{:S(2)}) collective-permute-start(bf16[2,2,128,256]{3,2,1,0:T(8,128)(2,1)S(1)} %pad_maximum_fusion), channel_id=1, source_target_pairs={{0,2},{1,3},{2,0},{3,1},{4,6},{5,7},{6,4},{7,5},{8,10},{9,11},{10,... | collective-permute-start | bytes 786440 | tf_op jit(solution)/shard_map/ppermute | solution.py:148
  22.8 9.2 %collective-permute-start.3 = (bf16[2,2,128,256]{3,2,1,0:T(8,128)(2,1)S(1)}, bf16[2,2,128,256]{3,2,1,0:T(8,128)(2,1)S(1)}, u32[]{:S(2)}, u32[]{:S(2)}) collective-permute-start(bf16[2,2,128,256]{3,2,1,0:T(8,128)(2,1)S(1)} %pad_maximum_fusion), channel_id=1, source_target_pairs={{0,1},{1,0},{2,3},{3,2},{4,5},{5,4},{6,7},{7,6},{8,9},{9,8},{10,11... | collective-permute-start | bytes 786440 | tf_op jit(solution)/shard_map/ppermute | solution.py:148
  28.6 3.5 %collective-permute-start.4 = (bf16[2,2,128,256]{3,2,1,0:T(8,128)(2,1)S(1)}, bf16[2,2,128,256]{3,2,1,0:T(8,128)(2,1)S(1)}, u32[]{:S(2)}, u32[]{:S(2)}) collective-permute-start(bf16[2,2,128,256]{3,2,1,0:T(8,128)(2,1)S(1)} %collective-permute-done.2.refs_2_), channel_id=1, source_target_pairs={{0,1},{1,0},{2,3},{3,2},{4,5},{5,4},{6,7},{7,6},{8,9},{9,8},{10,11... | collective-permute-start | bytes 786440 | tf_op jit(solution)/shard_map/ppermute | solution.py:148
  29.8 8.3 %collective-permute-start.8 = (bf16[2,256,256]{2,1,0:T(8,128)(2,1)S(1)}, bf16[2,256,256]{2,1,0:T(8,128)(2,1)S(1)}, u32[]{:S(2)}, u32[]{:S(2)}) collective-permute-start(bf16[2,256,256]{2,1,0:T(8,128)(2,1)S(1)} %slice_bitcast_fusion.2), channel_id=1, source_target_pairs={{0,12},{4,0},{8,4},{12,8},{1,13},{5,1},{9,5},{13,9},{2,14},{6,2},{... | collective-permute-start | bytes 786440 | tf_op jit(solution)/shard_map/ppermute | solution.py:140
  30.3 9.2 %collective-permute-start.7 = (bf16[2,256,256]{2,1,0:T(8,128)(2,1)S(1)}, bf16[2,256,256]{2,1,0:T(8,128)(2,1)S(1)}, u32[]{:S(2)}, u32[]{:S(2)}) collective-permute-start(bf16[2,256,256]{2,1,0:T(8,128)(2,1)S(1)} %slice_bitcast_fusion.3), channel_id=1, source_target_pairs={{0,4},{4,8},{8,12},{12,0},{1,5},{5,9},{9,13},{13,1},{2,6},{6,10},{... | collective-permute-start | bytes 786440 | tf_op jit(solution)/shard_map/ppermute | solution.py:140
  41.4 5.2 %collective-permute-start.11 = (f32[256,128]{1,0:T(8,128)S(1)}, f32[256,128]{1,0:T(8,128)S(1)}, u32[]{:S(2)}, u32[]{:S(2)}) collective-permute-start(f32[256,128]{1,0:T(8,128)S(1)} %get-tuple-element.35), channel_id=1, source_target_pairs={{0,48},{16,0},{32,16},{48,32},{64,112},{80,64},{96,80},{112,96},{1... | collective-permute-start | bytes 393224 | tf_op jit(solution)/shard_map/ppermute | solution.py:144
  42.1 6.2 %collective-permute-start.9 = (f32[256,128]{1,0:T(8,128)S(1)}, f32[256,128]{1,0:T(8,128)S(1)}, u32[]{:S(2)}, u32[]{:S(2)}) collective-permute-start(f32[256,128]{1,0:T(8,128)S(1)} %get-tuple-element.36), channel_id=1, source_target_pairs={{0,16},{16,32},{32,48},{48,0},{64,80},{80,96},{96,112},{112,64},{1... | collective-permute-start | bytes 393224 | tf_op jit(solution)/shard_map/ppermute | solution.py:144
  48.4 6.4 %collective-permute-start.12 = (f32[2,256,128]{2,1,0:T(8,128)S(1)}, f32[2,256,128]{2,1,0:T(8,128)S(1)}, u32[]{:S(2)}, u32[]{:S(2)}) collective-permute-start(f32[2,256,128]{2,1,0:T(8,128)S(1)} %get-tuple-element.33), channel_id=1, source_target_pairs={{0,48},{16,0},{32,16},{48,32},{64,112},{80,64},{96,80},{112,96},{1... | collective-permute-start | bytes 786440 | tf_op jit(solution)/shard_map/ppermute | solution.py:144
  48.6 8.0 %collective-permute-start.10 = (f32[2,256,128]{2,1,0:T(8,128)S(1)}, f32[2,256,128]{2,1,0:T(8,128)S(1)}, u32[]{:S(2)}, u32[]{:S(2)}) collective-permute-start(f32[2,256,128]{2,1,0:T(8,128)S(1)} %get-tuple-element.34), channel_id=1, source_target_pairs={{0,16},{16,32},{32,48},{48,0},{64,80},{80,96},{96,112},{112,64},{1... | collective-permute-start | bytes 786440 | tf_op jit(solution)/shard_map/ppermute | solution.py:144
  56.7 6.7 %collective-permute-start.13 = (f32[256,128]{1,0:T(8,128)S(1)}, f32[256,128]{1,0:T(8,128)S(1)}, u32[]{:S(2)}, u32[]{:S(2)}) collective-permute-start(f32[256,128]{1,0:T(8,128)S(1)} %bitcast_add_fusion), channel_id=1, source_target_pairs={{0,64},{16,80},{32,96},{48,112},{64,0},{80,16},{96,32},{112,48},{1... | collective-permute-start | bytes 393224 | tf_op jit(solution)/shard_map/ppermute | solution.py:148

commit v3 on v2

v3 whole, which is shorter than its diff:
```python
import functools

import jax
import jax.numpy as jnp
from jax import lax
from jax.experimental import pallas as pl
from jax.experimental.pallas import tpu as pltpu
from jax.sharding import PartitionSpec as P

FOLD = 256
SMEM = pl.BlockSpec(memory_space=pltpu.SMEM)
VMEM = pl.BlockSpec(memory_space=pltpu.VMEM)


def bounds_of(sizes_ref):
    total, bounds = sizes_ref[0], []
    for g in range(1, 8):
        bounds.append(total)
        total = total + sizes_ref[g]
    return bounds


def irrep(index, bounds):
    total = (index >= bounds[0]).astype(jnp.int32)
    for bound in bounds[1:]:
        total = total + (index >= bound).astype(jnp.int32)
    return total


def irrep_lanes(start, count, bounds):
    return irrep(lax.broadcasted_iota(jnp.int32, (1, count), 1) + start, bounds)


def irrep_rows(start, count, bounds):
    return irrep(lax.broadcasted_iota(jnp.int32, (count, 1), 0) + start, bounds)


def fold_of(load, want, lanes):
    total = None
    for at, irr in enumerate(lanes):
        kept = jnp.where(want == irr, load(at).astype(jnp.float32), 0.0)
        total = kept if total is None else total + kept
    return total


def fold_integrals(w_hbm, u_hbm, *refs):
    small, (out_ref, w_ref, u_ref, *held, sems, small_sems) = refs[:4], refs[4:]
    fetch = [pltpu.make_async_copy(*pair, small_sems.at[n]) for n, pair in enumerate(zip(small, held))]
    copies = [
        [
            pltpu.make_async_copy(hbm.at[k], ref.at[k], sems.at[k, n])
            for n, (hbm, ref) in enumerate(((w_hbm, w_ref), (u_hbm, u_ref)))
        ]
        for k in range(2)
    ]
    for copy in [*fetch, *copies[0], *copies[1]]:
        copy.start()
    for copy in fetch:
        copy.wait()
    occ_ref, virt_ref, k_ref, j_ref = held
    ctr, row, col = lax.axis_index("ctr"), lax.axis_index("row"), lax.axis_index("col")
    occ, virt = bounds_of(occ_ref), bounds_of(virt_ref)
    lanes = [irrep_lanes(at * FOLD, FOLD, virt) for at in range(4)]
    rows = irrep_rows(row * 256, 256, virt)
    irr_j = irrep(j_ref[col], occ)
    for k in range(2):
        want = rows ^ (irr_j ^ irrep(k_ref[2 * ctr + k], occ))
        for n, ref in enumerate((w_ref, u_ref)):
            copies[k][n].wait()
            folded = fold_of(lambda at: ref[k, :, at * FOLD : (at + 1) * FOLD], want, lanes)
            out_ref[n, k] = folded.T.astype(out_ref.dtype)


def fold_amplitudes(t_ref, occ_ref, virt_ref, slab_ref, k_ref, out_ref):
    ctr, row, col = lax.axis_index("ctr"), lax.axis_index("row"), lax.axis_index("col")
    occ, virt = bounds_of(occ_ref), bounds_of(virt_ref)
    lanes = [irrep_lanes(at * FOLD, FOLD, virt) for at in range(4)]
    rows = irrep_rows(ctr * 128, 128, virt)
    irr_i = irrep(slab_ref[row], occ)
    for k in range(4):
        want = rows ^ (irr_i ^ irrep(k_ref[4 * col + k], occ))
        folded = fold_of(lambda at: t_ref[:, k, at * FOLD : (at + 1) * FOLD], want, lanes)
        out_ref[(ctr % 2) ^ (k // 2), k % 2] = folded.astype(out_ref.dtype)


def assemble(pieces, t_all):
    col, odd = lax.axis_index("col"), lax.axis_index("ctr") % 2
    for n, piece in enumerate(pieces):
        flip, u = (0, 2, 1, 3)[n // 2], n % 2
        for k in range(2):
            t_all[k, 2 * (col ^ flip) + (odd ^ u)] = piece[k]


def products(ahead, t_all, w, u, scalars):
    occ_ref, virt_ref, slab_ref, k_ref = scalars
    ctr, row = lax.axis_index("ctr"), lax.axis_index("row")
    occ, virt = bounds_of(occ_ref), bounds_of(virt_ref)
    irr_i = irrep(slab_ref[row], occ)
    away = [irr_i ^ irrep(k_ref[2 * ctr + k], occ) for k in range(2)]
    quarters = [row, (row + 3) % 4, (row + 1) % 4, (row + 2) % 4]
    at = [4 * h + (ctr + ahead) % 4 for h in range(2)]
    a_rows = [irrep_rows(block * 128, 128, virt) for block in at]
    a_lanes = [irrep_lanes(block * 128, 128, virt) for block in at]
    total = jnp.zeros((FOLD, 256), jnp.float32)
    for k in range(2):
        left = [t_all[k, block].astype(jnp.float32) for block in at]
        for n, q in enumerate(quarters):
            c_lanes = irrep_lanes(q * 256, 256, virt)
            right = jnp.concatenate(
                [jnp.where((a_rows[m] ^ away[k]) == c_lanes, left[m], 0.0) for m in range(2)], axis=0
            ).astype(t_all.dtype)
            total = total + lax.dot_general(
                w[n][k], right, (((1,), (1,)), ((), ())), preferred_element_type=jnp.float32
            )
            d_rows = irrep_rows(q * 256, 256, virt) ^ away[k]
            both = t_all[k, pl.ds(2 * q, 2)].reshape(256, FOLD).astype(jnp.float32)
            half = jnp.where(at[0] % 2 == 0, both[:, :128], both[:, 128:])
            right = jnp.concatenate(
                [jnp.where(d_rows == a_lanes[m], half, 0.0) for m in range(2)], axis=1
            ).astype(t_all.dtype)
            total = total + lax.dot_general(
                u[n][k], right, (((1,), (0,)), ((), ())), preferred_element_type=jnp.float32
            )
    return total


def split(refs):
    held = refs[1:6]
    w, u = [*(ref.at[0] for ref in held[:3]), held[3]], [*(ref.at[1] for ref in held[:3]), held[4]]
    return refs[0], w, u, refs[6:10], refs[10:]


def far_products(*refs):
    pieces, (_, w, u, scalars, (out, t_all)) = refs[:8], split(refs[7:])
    assemble(pieces, t_all)
    total = products(2, t_all, w, u, scalars)
    out[0], out[1] = total[:, :128], total[:, 128:]


def near_products(*refs):
    t_all, w, u, scalars, (out,) = split(refs)
    for n, ahead in enumerate((1, 3, 0)):
        total = products(ahead, t_all, w, u, scalars)
        out[n, 0], out[n, 1] = total[:, :128], total[:, 128:]


def finish(here, low, high, across_ref, occ_ref, virt_ref, slab_ref, j_ref, out_ref):
    ctr, row, col = lax.axis_index("ctr"), lax.axis_index("row"), lax.axis_index("col")
    occ, virt = bounds_of(occ_ref), bounds_of(virt_ref)
    h = ctr // 4
    total = (here[h] + low[h] + high[h] + across_ref[...]).T
    want = irrep_rows(ctr * 128, 128, virt) ^ (irrep(slab_ref[row], occ) ^ irrep(j_ref[col], occ))
    for at in range(4):
        kept = jnp.where(want == irrep_lanes(at * FOLD, FOLD, virt), total, 0.0)
        out_ref[:, at * FOLD : (at + 1) * FOLD] = kept.astype(out_ref.dtype)


def call(kernel, outs, arrays, scalars, scratch=(), place=VMEM, place_scalars=SMEM, mib=16, name=None):
    return pl.pallas_call(
        kernel,
        out_shape=[jax.ShapeDtypeStruct(*out) for out in outs],
        in_specs=[place] * len(arrays) + [place_scalars] * len(scalars),
        out_specs=[VMEM] * len(outs),
        scratch_shapes=scratch,
        compiler_params=pltpu.CompilerParams(vmem_limit_bytes=mib << 20),
        cost_estimate=pl.CostEstimate(flops=1 << 10, bytes_accessed=1 << 10, transcendentals=0),
        name=name,
    )(*arrays, *scalars)


def shift(value, axis, count, step):
    return lax.ppermute(value, axis, [(at, (at + step) % count) for at in range(count)])


def shift_y(value, step):
    return lax.ppermute(value, "ctr", [(at, at // 4 * 4 + (at + step) % 4) for at in range(8)])


def swap(value, axis, count, mask):
    return lax.ppermute(value, axis, [(at, at ^ mask) for at in range(count)])


def on_device(amps, w_cycle, w_cross, occ_sizes, virt_sizes, slab_occ, k_occ, j_occ):
    bf16, f32 = jnp.bfloat16, jnp.float32
    hbm = pl.BlockSpec(memory_space=pltpu.HBM)
    small = [occ_sizes, virt_sizes, k_occ, j_occ]
    own = call(
        fold_integrals, [((2, 2, FOLD, 256), bf16)], [w_cycle[:, :, 0], w_cross[:, :, 0]], small,
        [pltpu.VMEM((2, 256, 1024), bf16)] * 2
        + [pltpu.SMEM(value.shape, value.dtype) for value in small]
        + [pltpu.SemaphoreType.DMA((2, 2)), pltpu.SemaphoreType.DMA((4,))],
        place=hbm, place_scalars=hbm, mib=62, name="fold_integrals",
    )[0]
    up, down = shift(own, "row", 4, 1), shift(own, "row", 4, -1)
    integrals = [own, up, down, shift(up[0], "row", 4, 1), shift(down[1], "row", 4, -1)]

    t = call(
        fold_amplitudes, [((2, 2, 128, FOLD), bf16)], [amps[0]],
        [occ_sizes, virt_sizes, slab_occ, k_occ], name="fold_amplitudes",
    )[0]

    def spread(value, flip):
        pairs = [(x * 4 + q, (2 * q + (x % 2 ^ flip)) * 4 + x // 2) for x in range(8) for q in range(4)]
        return lax.ppermute(value, ("ctr", "col"), pairs)

    arrived = [spread(t[flip], flip) for flip in range(2)]
    beside = [swap(piece, "col", 4, 2) for piece in arrived]
    there = [swap(piece, "col", 4, 1) for piece in arrived]
    beyond = [swap(piece, "col", 4, 1) for piece in beside]
    pieces = [*arrived, *beside, *there, *beyond]
    scalars = [occ_sizes, virt_sizes, slab_occ, k_occ]

    far, t_all = call(
        far_products, [((2, FOLD, 128), f32), ((2, 8, 128, FOLD), bf16)], [*pieces, *integrals], scalars,
        name="far_products",
    )
    below, above = shift_y(far[0], 1), shift_y(far[1], -1)
    near = call(near_products, [((3, 2, FOLD, 128), f32)], [t_all, *integrals], scalars, name="near_products")[0]
    low = shift_y(near[0].at[0].add(below), 1)
    high = shift_y(near[1].at[1].add(above), -1)
    other = 1 - lax.axis_index("ctr") // 4
    pick = lambda value: lax.dynamic_index_in_dim(value, other, 0, False)
    across = swap(pick(near[2]) + pick(low) + pick(high), "ctr", 8, 4)
    out = call(
        finish, [((128, 4 * FOLD), bf16)], [near[2], low, high, across],
        [occ_sizes, virt_sizes, slab_occ, j_occ], name="finish",
    )[0]
    return out[None, :, None, :]


def solution(mesh):
    return jax.shard_map(
        on_device,
        mesh=mesh,
        in_specs=(
            P("row", "ctr", "col", None),
            P("ctr", "row", "col", None),
            P("ctr", "row", "col", None),
            P(),
            P(),
            P(),
            P(),
            P(),
        ),
        out_specs=P("row", "ctr", "col", None),
        check_vma=False,
    )
```

time: 65.7 us -> 57.5 us (0.88); the launches traced: 64.7 us -> 57.4 us
  waiting for transfers between devices: 24.9 us -> 15.5 us
  starting transfers between devices: 26.9 us -> 30.2 us
  local copies, waits for them, and re-layouts: 3.3 us -> 0.18 us
  Pallas kernels: 9.36 us -> 11.3 us
    ppermute x4, waiting for transfers between devices: 7.5 us -> 3.26 us  [shift(): lax.ppermute(value, axis, [(at, (at + step) % count) for at in range(coun...]
    unnamed x16 -> x14, local copies, waits for them, and re-layouts: 3.16 us -> 0.04 us
    ppermute x2, waiting for transfers between devices: 2.65 us -> 0.01 us  [spread(): return lax.ppermute(value, ('ctr', 'col'), pairs)]
    ppermute x4, starting transfers between devices: 4.19 us -> 6.6 us  [shift_y(): lax.ppermute(value, 'ctr', [(at, at // 4 * 4 + (at + step) % 4) for at in...]
    ppermute x4, waiting for transfers between devices: 7.91 us -> 5.99 us  [shift_y(): lax.ppermute(value, 'ctr', [(at, at // 4 * 4 + (at + step) % 4) for at in...]
    pallas_call x5, Pallas kernels: 9.36 us -> 11.3 us  [call(): pl.pallas_call(kernel, out_shape=[jax.ShapeDtypeStruct(*out) for out in o...]
    ppermute x4, starting transfers between devices: 6.43 us -> 7.62 us  [shift(): lax.ppermute(value, axis, [(at, (at + step) % count) for at in range(coun...]
    ppermute x4 -> x7, waiting for transfers between devices: 6.89 us -> 6.22 us  [swap(): return lax.ppermute(value, axis, [(at, at ^ mask) for at in range(count)])]
  transfers between devices with their start and end apart: 14 -> 17, of which waited for: 8 -> 7; matrix products, arithmetic and copies ran while one was open for 0% -> 0% of each run, Pallas kernels for 7% -> 9%
where the time goes in v3:
time: 57.5 us; the launch traced here: 57.4 us
  starting transfers between devices  30.2 us (53%)
  waiting for transfers between devices  15.5 us (27%)
  Pallas kernels  11.3 us (20%)
    ppermute x7, starting transfers between devices, swap(): return lax.ppermute(value, axis, [(at, at ^ mask) for at in range(count)])  13.7 us
    pallas_call x5, Pallas kernels, call(): pl.pallas_call(kernel, out_shape=[jax.ShapeDtypeStruct(*out) for out in o...  11.3 us
    ppermute x4, starting transfers between devices, shift(): lax.ppermute(value, axis, [(at, (at + step) % count) for at in range(coun...  7.62 us
    ppermute x4, starting transfers between devices, shift_y(): lax.ppermute(value, 'ctr', [(at, at // 4 * 4 + (at + step) % 4) for at in...  6.6 us
    ppermute x7, waiting for transfers between devices, swap(): return lax.ppermute(value, axis, [(at, at ^ mask) for at in range(count)])  6.22 us
    ppermute x4, waiting for transfers between devices, shift_y(): lax.ppermute(value, 'ctr', [(at, at // 4 * 4 + (at + step) % 4) for at in...  5.99 us
    ppermute x4, waiting for transfers between devices, shift(): lax.ppermute(value, axis, [(at, (at + step) % count) for at in range(coun...  3.26 us
    ppermute x2, starting transfers between devices, spread(): return lax.ppermute(value, ('ctr', 'col'), pairs)  2.32 us
  transfers between devices with their start and end apart: 17, of which 7 were waited for; matrix products, arithmetic and copies ran while one was open for 0% of the time, Pallas kernels for 9%

profile of v3, /device:TPU:0, one launch (start us, length us, event | category | flops | bytes accessed | tf_op | source)
XLA Modules:
  0.0 57.4 jit_solution(3157454436845702065)
XLA Ops:
  0.0 2.8 %fold_integrals.1.refs_8_.refs_1_ = bf16[2,2,256,256]{3,2,1,0:T(8,128)(2,1)} custom-call(bf16[2,256,1024]{2,1,0:T(8,128)(2,1)} %bitcast.55, bf16[2,256,1024]{2,1,0:T(8,128)(2,1)} %bitcast.56, s32[8]{0:T(128)} %occ_ref.3, s32[8]{0:T(128)} %virt_ref.3, s32[16]{0:T(128)} %refs_9_.1, s32[4]{0:T(128)} %j_ref.1), custom_call_target="tpu_custom_call" | custom-call | flops 1024 | bytes 1024 | tf_op jit(solution)/shard_map/fold_integrals/pallas_call | solution.py:159
  2.9 2.1 %collective-permute-start.8 = (bf16[2,2,256,256]{3,2,1,0:T(8,128)(2,1)}, bf16[2,2,256,256]{3,2,1,0:T(8,128)(2,1)S(1)}, u32[]{:S(2)}, u32[]{:S(2)}) collective-permute-start(bf16[2,2,256,256]{3,2,1,0:T(8,128)(2,1)} %fold_integrals.1.refs_8_.refs_1_), channel_id=1, source_target_pairs={{0,4},{4,8},{8,12},{12,0},{1,5},{5,9},{9,13},{13,1},{2,6},{6,10},{... | collective-permute-start | bytes 1572872 | tf_op jit(solution)/shard_map/ppermute | solution.py:172
  4.9 2.2 %collective-permute-start.9 = (bf16[2,2,256,256]{3,2,1,0:T(8,128)(2,1)}, bf16[2,2,256,256]{3,2,1,0:T(8,128)(2,1)S(1)}, u32[]{:S(2)}, u32[]{:S(2)}) collective-permute-start(bf16[2,2,256,256]{3,2,1,0:T(8,128)(2,1)} %fold_integrals.1.refs_8_.refs_1_), channel_id=1, source_target_pairs={{0,12},{4,0},{8,4},{12,8},{1,13},{5,1},{9,5},{13,9},{2,14},{6,2},{... | collective-permute-start | bytes 1572872 | tf_op jit(solution)/shard_map/ppermute | solution.py:172
  7.2 1.8 %fold_amplitudes.1 = bf16[2,2,128,256]{3,2,1,0:T(8,128)(2,1)S(1)} custom-call(bf16[128,4,1024]{2,1,0:T(4,128)(2,1)S(1)} %bitcast.54, s32[8]{0:T(128)S(1)} %copy-done.2, s32[8]{0:T(128)S(1)} %copy-done.3, s32[4]{0:T(128)S(1)} %copy-done.5, s32[16]{0:T(128)S(1)} %copy-done.4), custom_call_target="tpu_custom_call" | custom-call | flops 1024 | bytes 1024 | tf_op jit(solution)/shard_map/fold_amplitudes/pallas_call | solution.py:159
  9.0 0.7 %collective-permute-start = (bf16[2,128,256]{2,1,0:T(8,128)(2,1)S(1)}, bf16[2,128,256]{2,1,0:T(8,128)(2,1)S(1)}, u32[]{:S(2)}, u32[]{:S(2)}) collective-permute-start(bf16[2,128,256]{2,1,0:T(8,128)(2,1)S(1)} %get-tuple-element.42), channel_id=1, source_target_pairs={{0,0},{1,32},{2,64},{3,96},{16,16},{17,48},{18,80},{19,112},{32,1}... | collective-permute-start | bytes 393224 | tf_op jit(solution)/shard_map/ppermute | solution.py:204
  9.7 1.7 %collective-permute-start.1 = (bf16[2,128,256]{2,1,0:T(8,128)(2,1)S(1)}, bf16[2,128,256]{2,1,0:T(8,128)(2,1)S(1)}, u32[]{:S(2)}, u32[]{:S(2)}) collective-permute-start(bf16[2,128,256]{2,1,0:T(8,128)(2,1)S(1)} %get-tuple-element.41), channel_id=1, source_target_pairs={{0,16},{1,48},{2,80},{3,112},{16,0},{17,32},{18,64},{19,96},{32,17... | collective-permute-start | bytes 393224 | tf_op jit(solution)/shard_map/ppermute | solution.py:204
  11.3 6.0 %collective-permute-start.2 = (bf16[2,128,256]{2,1,0:T(8,128)(2,1)S(1)}, bf16[2,128,256]{2,1,0:T(8,128)(2,1)S(1)}, u32[]{:S(2)}, u32[]{:S(2)}) collective-permute-start(bf16[2,128,256]{2,1,0:T(8,128)(2,1)S(1)} %collective-permute-done.refs_0_), channel_id=1, source_target_pairs={{0,2},{1,3},{2,0},{3,1},{4,6},{5,7},{6,4},{7,5},{8,10},{9,11},{10,... | collective-permute-start | bytes 393224 | tf_op jit(solution)/shard_map/ppermute | solution.py:180
  17.3 2.9 %collective-permute-start.4 = (bf16[2,128,256]{2,1,0:T(8,128)(2,1)S(1)}, bf16[2,128,256]{2,1,0:T(8,128)(2,1)S(1)}, u32[]{:S(2)}, u32[]{:S(2)}) collective-permute-start(bf16[2,128,256]{2,1,0:T(8,128)(2,1)S(1)} %collective-permute-done.refs_0_), channel_id=1, source_target_pairs={{0,1},{1,0},{2,3},{3,2},{4,5},{5,4},{6,7},{7,6},{8,9},{9,8},{10,11... | collective-permute-start | bytes 393224 | tf_op jit(solution)/shard_map/ppermute | solution.py:180
  20.2 1.1 %collective-permute-start.3 = (bf16[2,128,256]{2,1,0:T(8,128)(2,1)S(1)}, bf16[2,128,256]{2,1,0:T(8,128)(2,1)S(1)}, u32[]{:S(2)}, u32[]{:S(2)}) collective-permute-start(bf16[2,128,256]{2,1,0:T(8,128)(2,1)S(1)} %collective-permute-done.1.refs_1_), channel_id=1, source_target_pairs={{0,2},{1,3},{2,0},{3,1},{4,6},{5,7},{6,4},{7,5},{8,10},{9,11},{10,... | collective-permute-start | bytes 393224 | tf_op jit(solution)/shard_map/ppermute | solution.py:180
  21.5 3.3 %collective-permute-start.11 = (bf16[2,256,256]{2,1,0:T(8,128)(2,1)S(1)}, bf16[2,256,256]{2,1,0:T(8,128)(2,1)S(1)}, u32[]{:S(2)}, u32[]{:S(2)}) collective-permute-start(bf16[2,256,256]{2,1,0:T(8,128)(2,1)S(1)} %slice_bitcast_fusion.2), channel_id=1, source_target_pairs={{0,12},{4,0},{8,4},{12,8},{1,13},{5,1},{9,5},{13,9},{2,14},{6,2},{... | collective-permute-start | bytes 786440 | tf_op jit(solution)/shard_map/ppermute | solution.py:172
  24.8 1.0 %collective-permute-start.5 = (bf16[2,128,256]{2,1,0:T(8,128)(2,1)S(1)}, bf16[2,128,256]{2,1,0:T(8,128)(2,1)S(1)}, u32[]{:S(2)}, u32[]{:S(2)}) collective-permute-start(bf16[2,128,256]{2,1,0:T(8,128)(2,1)S(1)} %collective-permute-done.1.refs_1_), channel_id=1, source_target_pairs={{0,1},{1,0},{2,3},{3,2},{4,5},{5,4},{6,7},{7,6},{8,9},{9,8},{10,11... | collective-permute-start | bytes 393224 | tf_op jit(solution)/shard_map/ppermute | solution.py:180
  25.8 0.5 collective-permute-done.3.refs_3_
  26.3 0.4 collective-permute-start.6
  26.9 0.8 %collective-permute-done.6.refs_6_ = bf16[2,128,256]{2,1,0:T(8,128)(2,1)S(1)} collective-permute-done((bf16[2,128,256]{2,1,0:T(8,128)(2,1)S(1)}, bf16[2,128,256]{2,1,0:T(8,128)(2,1)S(1)}, u32[]{:S(2)}, u32[]{:S(2)}) %collective-permute-start.6) | collective-permute-done | bytes 131104 | tf_op jit(solution)/shard_map/ppermute | solution.py:180
  28.1 3.3 %collective-permute-done.10.refs_11_.refs_4_ = bf16[2,256,256]{2,1,0:T(8,128)(2,1)S(1)} collective-permute-done((bf16[2,256,256]{2,1,0:T(8,128)(2,1)S(1)}, bf16[2,256,256]{2,1,0:T(8,128)(2,1)S(1)}, u32[]{:S(2)}, u32[]{:S(2)}) %collective-permute-start.10) | collective-permute-done | bytes 262176 | tf_op jit(solution)/shard_map/ppermute | solution.py:172
  31.3 1.8 %far_products.1 = (f32[2,256,128]{2,1,0:T(8,128)S(1)}, bf16[2,8,128,256]{3,2,1,0:T(8,128)(2,1)S(1)}) custom-call(bf16[2,128,256]{2,1,0:T(8,128)(2,1)S(1)} %collective-permute-done.refs_0_, bf16[2,128,256]{2,1,0:T(8,128)(2,1)S(1)} %collective-permute-done.1.refs_1_, bf16[2,128,256]{2,1,0:T(8,128)(2,1)S(1)} %collective-permute-done.2.refs_2_, ...), custom_call_target="tpu_custom_call" | custom-call | flops 1024 | bytes 1024 | tf_op jit(solution)/shard_map/far_products/pallas_call | solution.py:159
  33.2 0.9 %collective-permute-start.12 = (f32[256,128]{1,0:T(8,128)S(1)}, f32[256,128]{1,0:T(8,128)S(1)}, u32[]{:S(2)}, u32[]{:S(2)}) collective-permute-start(f32[256,128]{1,0:T(8,128)S(1)} %get-tuple-element.40), channel_id=1, source_target_pairs={{0,16},{16,32},{32,48},{48,0},{64,80},{80,96},{96,112},{112,64},{1... | collective-permute-start | bytes 393224 | tf_op jit(solution)/shard_map/ppermute | solution.py:176
  34.1 2.4 %collective-permute-start.14 = (f32[256,128]{1,0:T(8,128)S(1)}, f32[256,128]{1,0:T(8,128)S(1)}, u32[]{:S(2)}, u32[]{:S(2)}) collective-permute-start(f32[256,128]{1,0:T(8,128)S(1)} %get-tuple-element.39), channel_id=1, source_target_pairs={{0,48},{16,0},{32,16},{48,32},{64,112},{80,64},{96,80},{112,96},{1... | collective-permute-start | bytes 393224 | tf_op jit(solution)/shard_map/ppermute | solution.py:176
  36.5 3.4 %near_products.1 = f32[3,2,256,128]{3,2,1,0:T(8,128)S(1)} custom-call(bf16[2,8,128,256]{3,2,1,0:T(8,128)(2,1)S(1)} %get-tuple-element.31.refs_0_, bf16[2,2,256,256]{3,2,1,0:T(8,128)(2,1)S(1)} %copy-done, bf16[2,2,256,256]{3,2,1,0:T(8,128)(2,1)S(1)} %collective-permute-done.8.refs_9_.refs_2_, ...), custom_call_target="tpu_custom_call" | custom-call | flops 1024 | bytes 1024 | tf_op jit(solution)/shard_map/near_products/pallas_call | solution.py:159
  40.4 3.2 %collective-permute-start.15 = (f32[2,256,128]{2,1,0:T(8,128)S(1)}, f32[2,256,128]{2,1,0:T(8,128)S(1)}, u32[]{:S(2)}, u32[]{:S(2)}) collective-permute-start(f32[2,256,128]{2,1,0:T(8,128)S(1)} %get-tuple-element.37), channel_id=1, source_target_pairs={{0,48},{16,0},{32,16},{48,32},{64,112},{80,64},{96,80},{112,96},{1... | collective-permute-start | bytes 786440 | tf_op jit(solution)/shard_map/ppermute | solution.py:176
  43.6 5.8 %collective-permute-done.13.low = f32[2,256,128]{2,1,0:T(8,128)S(1)} collective-permute-done((f32[2,256,128]{2,1,0:T(8,128)S(1)}, f32[2,256,128]{2,1,0:T(8,128)S(1)}, u32[]{:S(2)}, u32[]{:S(2)}) %collective-permute-start.13) | collective-permute-done | bytes 262176 | tf_op jit(solution)/shard_map/ppermute | solution.py:176
  49.4 2.1 %collective-permute-start.16 = (f32[256,128]{1,0:T(8,128)S(1)}, f32[256,128]{1,0:T(8,128)S(1)}, u32[]{:S(2)}, u32[]{:S(2)}) collective-permute-start(f32[256,128]{1,0:T(8,128)S(1)} %bitcast_add_fusion), channel_id=1, source_target_pairs={{0,64},{16,80},{32,96},{48,112},{64,0},{80,16},{96,32},{112,48},{1... | collective-permute-start | bytes 393224 | tf_op jit(solution)/shard_map/ppermute | solution.py:180
  51.5 4.5 %collective-permute-done.16.across_ref = f32[256,128]{1,0:T(8,128)S(1)} collective-permute-done((f32[256,128]{1,0:T(8,128)S(1)}, f32[256,128]{1,0:T(8,128)S(1)}, u32[]{:S(2)}, u32[]{:S(2)}) %collective-permute-start.16) | collective-permute-done | bytes 131104 | tf_op jit(solution)/shard_map/ppermute | solution.py:180
  55.9 1.4 %finish.1 = bf16[128,1024]{1,0:T(8,128)(2,1)} custom-call(f32[2,256,128]{2,1,0:T(8,128)S(1)} %get-tuple-element.34.here, f32[2,256,128]{2,1,0:T(8,128)S(1)} %collective-permute-done.13.low, f32[2,256,128]{2,1,0:T(8,128)S(1)} %collective-permute-done.15.high, f32[256,128]{1,0:T(8,128)S(1)} %collective-permute-done.16.across_ref, s32[8]{0:T(128)S(1)} %copy-done.2, ...), custom_call_target="tpu_custom_call" | custom-call | flops 1024 | bytes 1024 | tf_op jit(solution)/shard_map/finish/pallas_call | solution.py:159
  (36 shorter events, 1.1 us)
Async XLA Ops:
  0.0 7.2 %copy-start.1 = (bf16[1,128,4,1024]{3,2,1,0:T(4,128)(2,1)S(1)}, bf16[1,128,4,1024]{3,2,1,0:T(4,128)(2,1)}, u32[]{:S(2)}) copy-start(bf16[1,128,4,1024]{3,2,1,0:T(4,128)(2,1)} %param.12) | copy-start | bytes 3145732
  0.0 7.2 %copy-start.5 = (s32[4]{0:T(128)S(1)}, s32[4]{0:T(128)}, u32[]{:S(2)}) copy-start(s32[4]{0:T(128)} %slab_ref.3) | copy-start | bytes 52
  2.8 4.3 %copy-start.2 = (s32[8]{0:T(128)S(1)}, s32[8]{0:T(128)}, u32[]{:S(2)}) copy-start(s32[8]{0:T(128)} %occ_ref.3) | copy-start | bytes 100
  2.9 4.3 %copy-start.3 = (s32[8]{0:T(128)S(1)}, s32[8]{0:T(128)}, u32[]{:S(2)}) copy-start(s32[8]{0:T(128)} %virt_ref.3) | copy-start | bytes 100
  2.9 4.3 %copy-start.4 = (s32[16]{0:T(128)S(1)}, s32[16]{0:T(128)}, u32[]{:S(2)}) copy-start(s32[16]{0:T(128)} %refs_9_.1) | copy-start | bytes 196
  2.9 18.5 %collective-permute-start.8 = (bf16[2,2,256,256]{3,2,1,0:T(8,128)(2,1)}, bf16[2,2,256,256]{3,2,1,0:T(8,128)(2,1)S(1)}, u32[]{:S(2)}, u32[]{:S(2)}) collective-permute-start(bf16[2,2,256,256]{3,2,1,0:T(8,128)(2,1)} %fold_integrals.1.refs_8_.refs_1_), channel_id=1, source_target_pairs={{0,4},{4,8},{8,12},{12,0},{1,5},{5,9},{9,13},{13,1},{2,6},{6,10},{... | collective-permute-start | bytes 1572872 | tf_op jit(solution)/shard_map/ppermute | solution.py:172
  4.9 16.5 %collective-permute-start.9 = (bf16[2,2,256,256]{3,2,1,0:T(8,128)(2,1)}, bf16[2,2,256,256]{3,2,1,0:T(8,128)(2,1)S(1)}, u32[]{:S(2)}, u32[]{:S(2)}) collective-permute-start(bf16[2,2,256,256]{3,2,1,0:T(8,128)(2,1)} %fold_integrals.1.refs_8_.refs_1_), channel_id=1, source_target_pairs={{0,12},{4,0},{8,4},{12,8},{1,13},{5,1},{9,5},{13,9},{2,14},{6,2},{... | collective-permute-start | bytes 1572872 | tf_op jit(solution)/shard_map/ppermute | solution.py:172
  9.0 2.3 %collective-permute-start = (bf16[2,128,256]{2,1,0:T(8,128)(2,1)S(1)}, bf16[2,128,256]{2,1,0:T(8,128)(2,1)S(1)}, u32[]{:S(2)}, u32[]{:S(2)}) collective-permute-start(bf16[2,128,256]{2,1,0:T(8,128)(2,1)S(1)} %get-tuple-element.42), channel_id=1, source_target_pairs={{0,0},{1,32},{2,64},{3,96},{16,16},{17,48},{18,80},{19,112},{32,1}... | collective-permute-start | bytes 393224 | tf_op jit(solution)/shard_map/ppermute | solution.py:204
  9.6 21.7 %copy-start = (bf16[2,2,256,256]{3,2,1,0:T(8,128)(2,1)S(1)}, bf16[2,2,256,256]{3,2,1,0:T(8,128)(2,1)}, u32[]{:S(2)}) copy-start(bf16[2,2,256,256]{3,2,1,0:T(8,128)(2,1)} %fold_integrals.1.refs_8_.refs_1_) | copy-start | bytes 1572868
  9.7 10.6 %collective-permute-start.1 = (bf16[2,128,256]{2,1,0:T(8,128)(2,1)S(1)}, bf16[2,128,256]{2,1,0:T(8,128)(2,1)S(1)}, u32[]{:S(2)}, u32[]{:S(2)}) collective-permute-start(bf16[2,128,256]{2,1,0:T(8,128)(2,1)S(1)} %get-tuple-element.41), channel_id=1, source_target_pairs={{0,16},{1,48},{2,80},{3,112},{16,0},{17,32},{18,64},{19,96},{32,17... | collective-permute-start | bytes 393224 | tf_op jit(solution)/shard_map/ppermute | solution.py:204
  11.3 13.5 %collective-permute-start.2 = (bf16[2,128,256]{2,1,0:T(8,128)(2,1)S(1)}, bf16[2,128,256]{2,1,0:T(8,128)(2,1)S(1)}, u32[]{:S(2)}, u32[]{:S(2)}) collective-permute-start(bf16[2,128,256]{2,1,0:T(8,128)(2,1)S(1)} %collective-permute-done.refs_0_), channel_id=1, source_target_pairs={{0,2},{1,3},{2,0},{3,1},{4,6},{5,7},{6,4},{7,5},{8,10},{9,11},{10,... | collective-permute-start | bytes 393224 | tf_op jit(solution)/shard_map/ppermute | solution.py:180
  17.3 9.4 %collective-permute-start.4 = (bf16[2,128,256]{2,1,0:T(8,128)(2,1)S(1)}, bf16[2,128,256]{2,1,0:T(8,128)(2,1)S(1)}, u32[]{:S(2)}, u32[]{:S(2)}) collective-permute-start(bf16[2,128,256]{2,1,0:T(8,128)(2,1)S(1)} %collective-permute-done.refs_0_), channel_id=1, source_target_pairs={{0,1},{1,0},{2,3},{3,2},{4,5},{5,4},{6,7},{7,6},{8,9},{9,8},{10,11... | collective-permute-start | bytes 393224 | tf_op jit(solution)/shard_map/ppermute | solution.py:180
  20.2 6.1 %collective-permute-start.3 = (bf16[2,128,256]{2,1,0:T(8,128)(2,1)S(1)}, bf16[2,128,256]{2,1,0:T(8,128)(2,1)S(1)}, u32[]{:S(2)}, u32[]{:S(2)}) collective-permute-start(bf16[2,128,256]{2,1,0:T(8,128)(2,1)S(1)} %collective-permute-done.1.refs_1_), channel_id=1, source_target_pairs={{0,2},{1,3},{2,0},{3,1},{4,6},{5,7},{6,4},{7,5},{8,10},{9,11},{10,... | collective-permute-start | bytes 393224 | tf_op jit(solution)/shard_map/ppermute | solution.py:180
  21.4 9.9 %collective-permute-start.10 = (bf16[2,256,256]{2,1,0:T(8,128)(2,1)S(1)}, bf16[2,256,256]{2,1,0:T(8,128)(2,1)S(1)}, u32[]{:S(2)}, u32[]{:S(2)}) collective-permute-start(bf16[2,256,256]{2,1,0:T(8,128)(2,1)S(1)} %slice_bitcast_fusion.3), channel_id=1, source_target_pairs={{0,4},{4,8},{8,12},{12,0},{1,5},{5,9},{9,13},{13,1},{2,6},{6,10},{... | collective-permute-start | bytes 786440 | tf_op jit(solution)/shard_map/ppermute | solution.py:172
  21.5 9.8 %collective-permute-start.11 = (bf16[2,256,256]{2,1,0:T(8,128)(2,1)S(1)}, bf16[2,256,256]{2,1,0:T(8,128)(2,1)S(1)}, u32[]{:S(2)}, u32[]{:S(2)}) collective-permute-start(bf16[2,256,256]{2,1,0:T(8,128)(2,1)S(1)} %slice_bitcast_fusion.2), channel_id=1, source_target_pairs={{0,12},{4,0},{8,4},{12,8},{1,13},{5,1},{9,5},{13,9},{2,14},{6,2},{... | collective-permute-start | bytes 786440 | tf_op jit(solution)/shard_map/ppermute | solution.py:172
  24.8 2.1 %collective-permute-start.5 = (bf16[2,128,256]{2,1,0:T(8,128)(2,1)S(1)}, bf16[2,128,256]{2,1,0:T(8,128)(2,1)S(1)}, u32[]{:S(2)}, u32[]{:S(2)}) collective-permute-start(bf16[2,128,256]{2,1,0:T(8,128)(2,1)S(1)} %collective-permute-done.1.refs_1_), channel_id=1, source_target_pairs={{0,1},{1,0},{2,3},{3,2},{4,5},{5,4},{6,7},{7,6},{8,9},{9,8},{10,11... | collective-permute-start | bytes 393224 | tf_op jit(solution)/shard_map/ppermute | solution.py:180
  26.3 1.4 %collective-permute-start.6 = (bf16[2,128,256]{2,1,0:T(8,128)(2,1)S(1)}, bf16[2,128,256]{2,1,0:T(8,128)(2,1)S(1)}, u32[]{:S(2)}, u32[]{:S(2)}) collective-permute-start(bf16[2,128,256]{2,1,0:T(8,128)(2,1)S(1)} %collective-permute-done.2.refs_2_), channel_id=1, source_target_pairs={{0,1},{1,0},{2,3},{3,2},{4,5},{5,4},{6,7},{7,6},{8,9},{9,8},{10,11... | collective-permute-start | bytes 393224 | tf_op jit(solution)/shard_map/ppermute | solution.py:180
  26.7 1.3 %collective-permute-start.7 = (bf16[2,128,256]{2,1,0:T(8,128)(2,1)S(1)}, bf16[2,128,256]{2,1,0:T(8,128)(2,1)S(1)}, u32[]{:S(2)}, u32[]{:S(2)}) collective-permute-start(bf16[2,128,256]{2,1,0:T(8,128)(2,1)S(1)} %collective-permute-done.3.refs_3_), channel_id=1, source_target_pairs={{0,1},{1,0},{2,3},{3,2},{4,5},{5,4},{6,7},{7,6},{8,9},{9,8},{10,11... | collective-permute-start | bytes 393224 | tf_op jit(solution)/shard_map/ppermute | solution.py:180
  33.2 7.0 %collective-permute-start.12 = (f32[256,128]{1,0:T(8,128)S(1)}, f32[256,128]{1,0:T(8,128)S(1)}, u32[]{:S(2)}, u32[]{:S(2)}) collective-permute-start(f32[256,128]{1,0:T(8,128)S(1)} %get-tuple-element.40), channel_id=1, source_target_pairs={{0,16},{16,32},{32,48},{48,0},{64,80},{80,96},{96,112},{112,64},{1... | collective-permute-start | bytes 393224 | tf_op jit(solution)/shard_map/ppermute | solution.py:176
  34.1 6.2 %collective-permute-start.14 = (f32[256,128]{1,0:T(8,128)S(1)}, f32[256,128]{1,0:T(8,128)S(1)}, u32[]{:S(2)}, u32[]{:S(2)}) collective-permute-start(f32[256,128]{1,0:T(8,128)S(1)} %get-tuple-element.39), channel_id=1, source_target_pairs={{0,48},{16,0},{32,16},{48,32},{64,112},{80,64},{96,80},{112,96},{1... | collective-permute-start | bytes 393224 | tf_op jit(solution)/shard_map/ppermute | solution.py:176
  40.3 9.1 %collective-permute-start.13 = (f32[2,256,128]{2,1,0:T(8,128)S(1)}, f32[2,256,128]{2,1,0:T(8,128)S(1)}, u32[]{:S(2)}, u32[]{:S(2)}) collective-permute-start(f32[2,256,128]{2,1,0:T(8,128)S(1)} %get-tuple-element.38), channel_id=1, source_target_pairs={{0,16},{16,32},{32,48},{48,0},{64,80},{80,96},{96,112},{112,64},{1... | collective-permute-start | bytes 786440 | tf_op jit(solution)/shard_map/ppermute | solution.py:176
  40.4 9.0 %collective-permute-start.15 = (f32[2,256,128]{2,1,0:T(8,128)S(1)}, f32[2,256,128]{2,1,0:T(8,128)S(1)}, u32[]{:S(2)}, u32[]{:S(2)}) collective-permute-start(f32[2,256,128]{2,1,0:T(8,128)S(1)} %get-tuple-element.37), channel_id=1, source_target_pairs={{0,48},{16,0},{32,16},{48,32},{64,112},{80,64},{96,80},{112,96},{1... | collective-permute-start | bytes 786440 | tf_op jit(solution)/shard_map/ppermute | solution.py:176
  49.4 6.6 %copy-start.6 = (s32[4]{0:T(128)S(1)}, s32[4]{0:T(128)}, u32[]{:S(2)}) copy-start(s32[4]{0:T(128)} %j_ref.1) | copy-start | bytes 52
  49.4 6.6 %collective-permute-start.16 = (f32[256,128]{1,0:T(8,128)S(1)}, f32[256,128]{1,0:T(8,128)S(1)}, u32[]{:S(2)}, u32[]{:S(2)}) collective-permute-start(f32[256,128]{1,0:T(8,128)S(1)} %bitcast_add_fusion), channel_id=1, source_target_pairs={{0,64},{16,80},{32,96},{48,112},{64,0},{80,16},{96,32},{112,48},{1... | collective-permute-start | bytes 393224 | tf_op jit(solution)/shard_map/ppermute | solution.py:180

commit v4 on v3

--- a/solution.py
+++ b/solution.py
@@ -20,6 +20,10 @@
     return bounds
 
 
+def bounds_in(table):
+    return [table[g : g + 1, :1] for g in range(7)]
+
+
 def irrep(index, bounds):
     total = (index >= bounds[0]).astype(jnp.int32)
     for bound in bounds[1:]:
@@ -44,7 +48,7 @@
 
 
 def fold_integrals(w_hbm, u_hbm, *refs):
-    small, (out_ref, w_ref, u_ref, *held, sems, small_sems) = refs[:4], refs[4:]
+    small, (out_ref, table, w_ref, u_ref, *held, sems, small_sems) = refs[:5], refs[5:]
     fetch = [pltpu.make_async_copy(*pair, small_sems.at[n]) for n, pair in enumerate(zip(small, held))]
     copies = [
         [
@@ -57,9 +61,16 @@
         copy.start()
     for copy in fetch:
         copy.wait()
-    occ_ref, virt_ref, k_ref, j_ref = held
+    occ_ref, virt_ref, slab_ref, k_ref, j_ref = held
     ctr, row, col = lax.axis_index("ctr"), lax.axis_index("row"), lax.axis_index("col")
     occ, virt = bounds_of(occ_ref), bounds_of(virt_ref)
+    irr_i = irrep(slab_ref[row], occ)
+    entries = [*virt, *(irr_i ^ irrep(k_ref[2 * ctr + k], occ) for k in range(2)), irr_i ^ irrep(j_ref[col], occ)]
+    line = lax.broadcasted_iota(jnp.int32, table.shape, 0)
+    held_table = jnp.zeros(table.shape, jnp.int32)
+    for n, entry in enumerate(entries):
+        held_table = jnp.where(line == n, entry, held_table)
+    table[...] = held_table
     lanes = [irrep_lanes(at * FOLD, FOLD, virt) for at in range(4)]
     rows = irrep_rows(row * 256, 256, virt)
     irr_j = irrep(j_ref[col], occ)
@@ -91,71 +102,71 @@
             t_all[k, 2 * (col ^ flip) + (odd ^ u)] = piece[k]
 
 
-def products(ahead, t_all, w, u, scalars):
-    occ_ref, virt_ref, slab_ref, k_ref = scalars
+def products(ahead, t_all, w, u, table):
     ctr, row = lax.axis_index("ctr"), lax.axis_index("row")
-    occ, virt = bounds_of(occ_ref), bounds_of(virt_ref)
-    irr_i = irrep(slab_ref[row], occ)
-    away = [irr_i ^ irrep(k_ref[2 * ctr + k], occ) for k in range(2)]
+    virt = bounds_in(table)
     quarters = [row, (row + 3) % 4, (row + 1) % 4, (row + 2) % 4]
     at = [4 * h + (ctr + ahead) % 4 for h in range(2)]
-    a_rows = [irrep_rows(block * 128, 128, virt) for block in at]
-    a_lanes = [irrep_lanes(block * 128, 128, virt) for block in at]
-    total = jnp.zeros((FOLD, 256), jnp.float32)
+    dtype = t_all.dtype
+    small = lambda value: value.astype(jnp.float32).astype(dtype)
+    a_lanes = [small(irrep_lanes(block * 128, 128, virt)) for block in at]
+    q_lanes = [small(irrep_lanes(q * 256, 256, virt)) for q in quarters]
+    zero = jnp.zeros((), dtype)
+    total = None
     for k in range(2):
-        left = [t_all[k, block].astype(jnp.float32) for block in at]
-        for n, q in enumerate(quarters):
-            c_lanes = irrep_lanes(q * 256, 256, virt)
-            right = jnp.concatenate(
-                [jnp.where((a_rows[m] ^ away[k]) == c_lanes, left[m], 0.0) for m in range(2)], axis=0
-            ).astype(t_all.dtype)
-            total = total + lax.dot_general(
-                w[n][k], right, (((1,), (1,)), ((), ())), preferred_element_type=jnp.float32
-            )
-            d_rows = irrep_rows(q * 256, 256, virt) ^ away[k]
-            both = t_all[k, pl.ds(2 * q, 2)].reshape(256, FOLD).astype(jnp.float32)
-            half = jnp.where(at[0] % 2 == 0, both[:, :128], both[:, 128:])
-            right = jnp.concatenate(
-                [jnp.where(d_rows == a_lanes[m], half, 0.0) for m in range(2)], axis=1
-            ).astype(t_all.dtype)
-            total = total + lax.dot_general(
-                u[n][k], right, (((1,), (0,)), ((), ())), preferred_element_type=jnp.float32
-            )
+        away = table[7 + k : 8 + k, :1]
+        a_rows = jnp.concatenate([small(irrep_rows(block * 128, 128, virt) ^ away) for block in at], axis=0)
+        left = jnp.concatenate([t_all[k, block] for block in at], axis=0)
+        right = jnp.concatenate([jnp.where(a_rows == lanes, left, zero) for lanes in q_lanes], axis=1)
+        part = lax.dot_general(
+            jnp.concatenate([w[n][k] for n in range(4)], axis=1), right, (((1,), (1,)), ((), ())),
+            preferred_element_type=jnp.float32,
+        )
+        total = part if total is None else total + part
+        right = []
+        for q in quarters:
+            d_rows = small(irrep_rows(q * 256, 256, virt) ^ away)
+            half = t_all[k, pl.ds(2 * q, 2)].reshape(256, FOLD)
+            half = jnp.where(at[0] % 2 == 0, half[:, :128], half[:, 128:])
+            right.append(jnp.concatenate([jnp.where(d_rows == lanes, half, zero) for lanes in a_lanes], axis=1))
+        total = total + lax.dot_general(
+            jnp.concatenate([u[n][k] for n in range(4)], axis=1), jnp.concatenate(right, axis=0),
+            (((1,), (0,)), ((), ())), preferred_element_type=jnp.float32,
+        )
     return total
 
 
 def split(refs):
     held = refs[1:6]
     w, u = [*(ref.at[0] for ref in held[:3]), held[3]], [*(ref.at[1] for ref in held[:3]), held[4]]
-    return refs[0], w, u, refs[6:10], refs[10:]
+    return refs[0], w, u, refs[6], refs[7:]
 
 
 def far_products(*refs):
-    pieces, (_, w, u, scalars, (out, t_all)) = refs[:8], split(refs[7:])
+    pieces, (_, w, u, table, (out, t_all)) = refs[:8], split(refs[7:])
     assemble(pieces, t_all)
-    total = products(2, t_all, w, u, scalars)
+    total = products(2, t_all, w, u, table)
     out[0], out[1] = total[:, :128], total[:, 128:]
 
 
 def near_products(*refs):
-    t_all, w, u, scalars, (out,) = split(refs)
+    t_all, w, u, table, (out,) = split(refs)
     for n, ahead in enumerate((1, 3, 0)):
-        total = products(ahead, t_all, w, u, scalars)
+        total = products(ahead, t_all, w, u, table)
         out[n, 0], out[n, 1] = total[:, :128], total[:, 128:]
 
 
-def finish(here, low, high, across_ref, occ_ref, virt_ref, slab_ref, j_ref, out_ref):
-    ctr, row, col = lax.axis_index("ctr"), lax.axis_index("row"), lax.axis_index("col")
-    occ, virt = bounds_of(occ_ref), bounds_of(virt_ref)
+def finish(here, low, high, across_ref, table, out_ref):
+    virt, ctr = bounds_in(table), lax.axis_index("ctr")
     h = ctr // 4
     total = (here[h] + low[h] + high[h] + across_ref[...]).T
-    want = irrep_rows(ctr * 128, 128, virt) ^ (irrep(slab_ref[row], occ) ^ irrep(j_ref[col], occ))
+    want = irrep_rows(ctr * 128, 128, virt) ^ table[9:10, :1]
     for at in range(4):
         kept = jnp.where(want == irrep_lanes(at * FOLD, FOLD, virt), total, 0.0)
         out_ref[:, at * FOLD : (at + 1) * FOLD] = kept.astype(out_ref.dtype)
 
 
-def call(kernel, outs, arrays, scalars, scratch=(), place=VMEM, place_scalars=SMEM, mib=16, name=None):
+def call(kernel, outs, arrays, scalars, scratch=(), place=VMEM, place_scalars=SMEM, mib=16, flops=1 << 10, name=None):
     return pl.pallas_call(
         kernel,
         out_shape=[jax.ShapeDtypeStruct(*out) for out in outs],
@@ -163,7 +174,7 @@
         out_specs=[VMEM] * len(outs),
         scratch_shapes=scratch,
         compiler_params=pltpu.CompilerParams(vmem_limit_bytes=mib << 20),
-        cost_estimate=pl.CostEstimate(flops=1 << 10, bytes_accessed=1 << 10, transcendentals=0),
+        cost_estimate=pl.CostEstimate(flops=flops, bytes_accessed=1 << 10, transcendentals=0),
         name=name,
     )(*arrays, *scalars)
 
@@ -183,16 +194,17 @@
 def on_device(amps, w_cycle, w_cross, occ_sizes, virt_sizes, slab_occ, k_occ, j_occ):
     bf16, f32 = jnp.bfloat16, jnp.float32
     hbm = pl.BlockSpec(memory_space=pltpu.HBM)
-    small = [occ_sizes, virt_sizes, k_occ, j_occ]
-    own = call(
-        fold_integrals, [((2, 2, FOLD, 256), bf16)], [w_cycle[:, :, 0], w_cross[:, :, 0]], small,
+    small = [occ_sizes, virt_sizes, slab_occ, k_occ, j_occ]
+    own, table = call(
+        fold_integrals, [((2, 2, FOLD, 256), bf16), ((16, 128), jnp.int32)], [w_cycle[:, :, 0], w_cross[:, :, 0]], small,
         [pltpu.VMEM((2, 256, 1024), bf16)] * 2
         + [pltpu.SMEM(value.shape, value.dtype) for value in small]
-        + [pltpu.SemaphoreType.DMA((2, 2)), pltpu.SemaphoreType.DMA((4,))],
+        + [pltpu.SemaphoreType.DMA((2, 2)), pltpu.SemaphoreType.DMA((5,))],
         place=hbm, place_scalars=hbm, mib=62, name="fold_integrals",
-    )[0]
+    )
     up, down = shift(own, "row", 4, 1), shift(own, "row", 4, -1)
-    integrals = [own, up, down, shift(up[0], "row", 4, 1), shift(down[1], "row", 4, -1)]
+    w_far, u_far = shift(up[0], "row", 4, 1), shift(down[1], "row", 4, -1)
+    integrals = [own, up, down, w_far, u_far]
 
     t = call(
         fold_amplitudes, [((2, 2, 128, FOLD), bf16)], [amps[0]],
@@ -208,23 +220,19 @@
     there = [swap(piece, "col", 4, 1) for piece in arrived]
     beyond = [swap(piece, "col", 4, 1) for piece in beside]
     pieces = [*arrived, *beside, *there, *beyond]
-    scalars = [occ_sizes, virt_sizes, slab_occ, k_occ]
 
     far, t_all = call(
-        far_products, [((2, FOLD, 128), f32), ((2, 8, 128, FOLD), bf16)], [*pieces, *integrals], scalars,
+        far_products, [((2, FOLD, 128), f32), ((2, 8, 128, FOLD), bf16)], [*pieces, *integrals, table], [],
         name="far_products",
     )
     below, above = shift_y(far[0], 1), shift_y(far[1], -1)
-    near = call(near_products, [((3, 2, FOLD, 128), f32)], [t_all, *integrals], scalars, name="near_products")[0]
+    near = call(near_products, [((3, 2, FOLD, 128), f32)], [t_all, *integrals, table], [], name="near_products")[0]
     low = shift_y(near[0].at[0].add(below), 1)
     high = shift_y(near[1].at[1].add(above), -1)
     other = 1 - lax.axis_index("ctr") // 4
     pick = lambda value: lax.dynamic_index_in_dim(value, other, 0, False)
     across = swap(pick(near[2]) + pick(low) + pick(high), "ctr", 8, 4)
-    out = call(
-        finish, [((128, 4 * FOLD), bf16)], [near[2], low, high, across],
-        [occ_sizes, virt_sizes, slab_occ, j_occ], name="finish",
-    )[0]
+    out = call(finish, [((128, 4 * FOLD), bf16)], [near[2], low, high, across, table], [], name="finish")[0]
     return out[None, :, None, :]
 
 

time: 57.5 us -> 56.4 us (0.981)
  Pallas kernels: 11.3 us -> 10 us
    pallas_call x5, Pallas kernels: 11.3 us -> 10 us  [call(): pl.pallas_call(kernel, out_shape=[jax.ShapeDtypeStruct(*out) for out in o...]
where the time goes in v4:
time: 56.4 us; the launch traced here: 56.3 us
  starting transfers between devices  30 us (53%)
  waiting for transfers between devices  15.9 us (28%)
  Pallas kernels  10 us (18%)
    ppermute x7, starting transfers between devices, swap(): return lax.ppermute(value, axis, [(at, at ^ mask) for at in range(count)])  13.5 us
    pallas_call x5, Pallas kernels, call(): pl.pallas_call(kernel, out_shape=[jax.ShapeDtypeStruct(*out) for out in o...  10 us
    ppermute x4, starting transfers between devices, shift(): lax.ppermute(value, axis, [(at, (at + step) % count) for at in range(coun...  7.62 us
    ppermute x4, starting transfers between devices, shift_y(): lax.ppermute(value, 'ctr', [(at, at // 4 * 4 + (at + step) % 4) for at in...  6.6 us
    ppermute x7, waiting for transfers between devices, swap(): return lax.ppermute(value, axis, [(at, at ^ mask) for at in range(count)])  6.4 us
    ppermute x4, waiting for transfers between devices, shift_y(): lax.ppermute(value, 'ctr', [(at, at // 4 * 4 + (at + step) % 4) for at in...  6.19 us
    ppermute x4, waiting for transfers between devices, shift(): lax.ppermute(value, axis, [(at, (at + step) % count) for at in range(coun...  3.27 us
    ppermute x2, starting transfers between devices, spread(): return lax.ppermute(value, ('ctr', 'col'), pairs)  2.32 us
  transfers between devices with their start and end apart: 17, of which 7 were waited for; matrix products, arithmetic and copies ran while one was open for 0% of the time, Pallas kernels for 9%

profile of v4, /device:TPU:0, one launch (start us, length us, event | category | flops | bytes accessed | tf_op | source)
XLA Modules:
  0.0 56.3 jit_solution(10969224334915394387)
XLA Ops:
  0.0 2.8 %fold_integrals.1 = (bf16[2,2,256,256]{3,2,1,0:T(8,128)(2,1)}, s32[16,128]{1,0:T(8,128)}) custom-call(bf16[2,256,1024]{2,1,0:T(8,128)(2,1)} %bitcast.55, bf16[2,256,1024]{2,1,0:T(8,128)(2,1)} %bitcast.56, s32[8]{0:T(128)} %refs_0_.1, s32[8]{0:T(128)} %refs_1_.1, s32[4]{0:T(128)} %refs_2_.1, s32[16]{0:T(128)} %refs_3_.1, s32[4]{0:T(128)} %refs_4_.1), custom_call_target="tpu_custom_call" | custom-call | flops 1024 | bytes 1024 | tf_op jit(solution)/shard_map/fold_integrals/pallas_call | solution.py:170
  2.9 2.1 %collective-permute-start.8 = (bf16[2,2,256,256]{3,2,1,0:T(8,128)(2,1)}, bf16[2,2,256,256]{3,2,1,0:T(8,128)(2,1)S(1)}, u32[]{:S(2)}, u32[]{:S(2)}) collective-permute-start(bf16[2,2,256,256]{3,2,1,0:T(8,128)(2,1)} %get-tuple-element.33.refs_8_.refs_1_), channel_id=1, source_target_pairs={{0,4},{4,8},{8,12},{12,0},{1,5},{5,9},{9,13},{13,1},{2,6},{6,10},{... | collective-permute-start | bytes 1572872 | tf_op jit(solution)/shard_map/ppermute | solution.py:183
  5.0 2.2 %collective-permute-start.9 = (bf16[2,2,256,256]{3,2,1,0:T(8,128)(2,1)}, bf16[2,2,256,256]{3,2,1,0:T(8,128)(2,1)S(1)}, u32[]{:S(2)}, u32[]{:S(2)}) collective-permute-start(bf16[2,2,256,256]{3,2,1,0:T(8,128)(2,1)} %get-tuple-element.33.refs_8_.refs_1_), channel_id=1, source_target_pairs={{0,12},{4,0},{8,4},{12,8},{1,13},{5,1},{9,5},{13,9},{2,14},{6,2},{... | collective-permute-start | bytes 1572872 | tf_op jit(solution)/shard_map/ppermute | solution.py:183
  7.2 1.8 %fold_amplitudes.1 = bf16[2,2,128,256]{3,2,1,0:T(8,128)(2,1)S(1)} custom-call(bf16[128,4,1024]{2,1,0:T(4,128)(2,1)S(1)} %bitcast.54, s32[8]{0:T(128)S(1)} %copy-done.3, s32[8]{0:T(128)S(1)} %copy-done.4, s32[4]{0:T(128)S(1)} %copy-done.5, s32[16]{0:T(128)S(1)} %copy-done.6), custom_call_target="tpu_custom_call" | custom-call | flops 1024 | bytes 1024 | tf_op jit(solution)/shard_map/fold_amplitudes/pallas_call | solution.py:170
  9.0 0.7 %collective-permute-start = (bf16[2,128,256]{2,1,0:T(8,128)(2,1)S(1)}, bf16[2,128,256]{2,1,0:T(8,128)(2,1)S(1)}, u32[]{:S(2)}, u32[]{:S(2)}) collective-permute-start(bf16[2,128,256]{2,1,0:T(8,128)(2,1)S(1)} %get-tuple-element.46), channel_id=1, source_target_pairs={{0,0},{1,32},{2,64},{3,96},{16,16},{17,48},{18,80},{19,112},{32,1}... | collective-permute-start | bytes 393224 | tf_op jit(solution)/shard_map/ppermute | solution.py:216
  9.7 1.7 %collective-permute-start.1 = (bf16[2,128,256]{2,1,0:T(8,128)(2,1)S(1)}, bf16[2,128,256]{2,1,0:T(8,128)(2,1)S(1)}, u32[]{:S(2)}, u32[]{:S(2)}) collective-permute-start(bf16[2,128,256]{2,1,0:T(8,128)(2,1)S(1)} %get-tuple-element.45), channel_id=1, source_target_pairs={{0,16},{1,48},{2,80},{3,112},{16,0},{17,32},{18,64},{19,96},{32,17... | collective-permute-start | bytes 393224 | tf_op jit(solution)/shard_map/ppermute | solution.py:216
  11.3 6.0 %collective-permute-start.2 = (bf16[2,128,256]{2,1,0:T(8,128)(2,1)S(1)}, bf16[2,128,256]{2,1,0:T(8,128)(2,1)S(1)}, u32[]{:S(2)}, u32[]{:S(2)}) collective-permute-start(bf16[2,128,256]{2,1,0:T(8,128)(2,1)S(1)} %collective-permute-done.refs_0_), channel_id=1, source_target_pairs={{0,2},{1,3},{2,0},{3,1},{4,6},{5,7},{6,4},{7,5},{8,10},{9,11},{10,... | collective-permute-start | bytes 393224 | tf_op jit(solution)/shard_map/ppermute | solution.py:191
  17.3 2.9 %collective-permute-start.4 = (bf16[2,128,256]{2,1,0:T(8,128)(2,1)S(1)}, bf16[2,128,256]{2,1,0:T(8,128)(2,1)S(1)}, u32[]{:S(2)}, u32[]{:S(2)}) collective-permute-start(bf16[2,128,256]{2,1,0:T(8,128)(2,1)S(1)} %collective-permute-done.refs_0_), channel_id=1, source_target_pairs={{0,1},{1,0},{2,3},{3,2},{4,5},{5,4},{6,7},{7,6},{8,9},{9,8},{10,11... | collective-permute-start | bytes 393224 | tf_op jit(solution)/shard_map/ppermute | solution.py:191
  20.3 1.1 %collective-permute-start.3 = (bf16[2,128,256]{2,1,0:T(8,128)(2,1)S(1)}, bf16[2,128,256]{2,1,0:T(8,128)(2,1)S(1)}, u32[]{:S(2)}, u32[]{:S(2)}) collective-permute-start(bf16[2,128,256]{2,1,0:T(8,128)(2,1)S(1)} %collective-permute-done.1.refs_1_), channel_id=1, source_target_pairs={{0,2},{1,3},{2,0},{3,1},{4,6},{5,7},{6,4},{7,5},{8,10},{9,11},{10,... | collective-permute-start | bytes 393224 | tf_op jit(solution)/shard_map/ppermute | solution.py:191
  21.5 3.3 %collective-permute-start.11 = (bf16[2,256,256]{2,1,0:T(8,128)(2,1)S(1)}, bf16[2,256,256]{2,1,0:T(8,128)(2,1)S(1)}, u32[]{:S(2)}, u32[]{:S(2)}) collective-permute-start(bf16[2,256,256]{2,1,0:T(8,128)(2,1)S(1)} %slice_bitcast_fusion.2), channel_id=1, source_target_pairs={{0,12},{4,0},{8,4},{12,8},{1,13},{5,1},{9,5},{13,9},{2,14},{6,2},{... | collective-permute-start | bytes 786440 | tf_op jit(solution)/shard_map/ppermute | solution.py:183
  24.8 1.0 %collective-permute-start.5 = (bf16[2,128,256]{2,1,0:T(8,128)(2,1)S(1)}, bf16[2,128,256]{2,1,0:T(8,128)(2,1)S(1)}, u32[]{:S(2)}, u32[]{:S(2)}) collective-permute-start(bf16[2,128,256]{2,1,0:T(8,128)(2,1)S(1)} %collective-permute-done.1.refs_1_), channel_id=1, source_target_pairs={{0,1},{1,0},{2,3},{3,2},{4,5},{5,4},{6,7},{7,6},{8,9},{9,8},{10,11... | collective-permute-start | bytes 393224 | tf_op jit(solution)/shard_map/ppermute | solution.py:191
  25.8 0.5 collective-permute-done.3.refs_3_
  26.9 0.8 %collective-permute-done.6.refs_6_ = bf16[2,128,256]{2,1,0:T(8,128)(2,1)S(1)} collective-permute-done((bf16[2,128,256]{2,1,0:T(8,128)(2,1)S(1)}, bf16[2,128,256]{2,1,0:T(8,128)(2,1)S(1)}, u32[]{:S(2)}, u32[]{:S(2)}) %collective-permute-start.6) | collective-permute-done | bytes 131104 | tf_op jit(solution)/shard_map/ppermute | solution.py:191
  28.1 3.3 %collective-permute-done.10.refs_11_.refs_4_ = bf16[2,256,256]{2,1,0:T(8,128)(2,1)S(1)} collective-permute-done((bf16[2,256,256]{2,1,0:T(8,128)(2,1)S(1)}, bf16[2,256,256]{2,1,0:T(8,128)(2,1)S(1)}, u32[]{:S(2)}, u32[]{:S(2)}) %collective-permute-start.10) | collective-permute-done | bytes 262176 | tf_op jit(solution)/shard_map/ppermute | solution.py:183
  31.4 1.4 %far_products.1 = (f32[2,256,128]{2,1,0:T(8,128)S(1)}, bf16[2,8,128,256]{3,2,1,0:T(8,128)(2,1)S(1)}) custom-call(bf16[2,128,256]{2,1,0:T(8,128)(2,1)S(1)} %collective-permute-done.refs_0_, bf16[2,128,256]{2,1,0:T(8,128)(2,1)S(1)} %collective-permute-done.1.refs_1_, bf16[2,128,256]{2,1,0:T(8,128)(2,1)S(1)} %collective-permute-done.2.refs_2_, ...), custom_call_target="tpu_custom_call" | custom-call | flops 1024 | bytes 1024 | tf_op jit(solution)/shard_map/far_products/pallas_call | solution.py:170
  32.8 0.9 %collective-permute-start.12 = (f32[256,128]{1,0:T(8,128)S(1)}, f32[256,128]{1,0:T(8,128)S(1)}, u32[]{:S(2)}, u32[]{:S(2)}) collective-permute-start(f32[256,128]{1,0:T(8,128)S(1)} %get-tuple-element.44), channel_id=1, source_target_pairs={{0,16},{16,32},{32,48},{48,0},{64,80},{80,96},{96,112},{112,64},{1... | collective-permute-start | bytes 393224 | tf_op jit(solution)/shard_map/ppermute | solution.py:187
  33.7 2.4 %collective-permute-start.14 = (f32[256,128]{1,0:T(8,128)S(1)}, f32[256,128]{1,0:T(8,128)S(1)}, u32[]{:S(2)}, u32[]{:S(2)}) collective-permute-start(f32[256,128]{1,0:T(8,128)S(1)} %get-tuple-element.43), channel_id=1, source_target_pairs={{0,48},{16,0},{32,16},{48,32},{64,112},{80,64},{96,80},{112,96},{1... | collective-permute-start | bytes 393224 | tf_op jit(solution)/shard_map/ppermute | solution.py:187
  36.1 3.2 %near_products.1 = f32[3,2,256,128]{3,2,1,0:T(8,128)S(1)} custom-call(bf16[2,8,128,256]{3,2,1,0:T(8,128)(2,1)S(1)} %get-tuple-element.35.refs_0_, bf16[2,2,256,256]{3,2,1,0:T(8,128)(2,1)S(1)} %copy-done, bf16[2,2,256,256]{3,2,1,0:T(8,128)(2,1)S(1)} %collective-permute-done.8.refs_9_.refs_2_, ...), custom_call_target="tpu_custom_call" | custom-call | flops 1024 | bytes 1024 | tf_op jit(solution)/shard_map/near_products/pallas_call | solution.py:170
  39.4 0.5 collective-permute-done.12
  39.9 3.2 %collective-permute-start.15 = (f32[2,256,128]{2,1,0:T(8,128)S(1)}, f32[2,256,128]{2,1,0:T(8,128)S(1)}, u32[]{:S(2)}, u32[]{:S(2)}) collective-permute-start(f32[2,256,128]{2,1,0:T(8,128)S(1)} %get-tuple-element.41), channel_id=1, source_target_pairs={{0,48},{16,0},{32,16},{48,32},{64,112},{80,64},{96,80},{112,96},{1... | collective-permute-start | bytes 786440 | tf_op jit(solution)/shard_map/ppermute | solution.py:187
  43.1 5.7 %collective-permute-done.13.low = f32[2,256,128]{2,1,0:T(8,128)S(1)} collective-permute-done((f32[2,256,128]{2,1,0:T(8,128)S(1)}, f32[2,256,128]{2,1,0:T(8,128)S(1)}, u32[]{:S(2)}, u32[]{:S(2)}) %collective-permute-start.13) | collective-permute-done | bytes 262176 | tf_op jit(solution)/shard_map/ppermute | solution.py:187
  48.9 1.9 %collective-permute-start.16 = (f32[256,128]{1,0:T(8,128)S(1)}, f32[256,128]{1,0:T(8,128)S(1)}, u32[]{:S(2)}, u32[]{:S(2)}) collective-permute-start(f32[256,128]{1,0:T(8,128)S(1)} %bitcast_add_fusion), channel_id=1, source_target_pairs={{0,64},{16,80},{32,96},{48,112},{64,0},{80,16},{96,32},{112,48},{1... | collective-permute-start | bytes 393224 | tf_op jit(solution)/shard_map/ppermute | solution.py:191
  50.8 4.6 %collective-permute-done.16.across_ref = f32[256,128]{1,0:T(8,128)S(1)} collective-permute-done((f32[256,128]{1,0:T(8,128)S(1)}, f32[256,128]{1,0:T(8,128)S(1)}, u32[]{:S(2)}, u32[]{:S(2)}) %collective-permute-start.16) | collective-permute-done | bytes 131104 | tf_op jit(solution)/shard_map/ppermute | solution.py:191
  55.5 0.9 %finish.1 = bf16[128,1024]{1,0:T(8,128)(2,1)} custom-call(f32[2,256,128]{2,1,0:T(8,128)S(1)} %get-tuple-element.38.here, f32[2,256,128]{2,1,0:T(8,128)S(1)} %collective-permute-done.13.low, f32[2,256,128]{2,1,0:T(8,128)S(1)} %collective-permute-done.15.high, f32[256,128]{1,0:T(8,128)S(1)} %collective-permute-done.16.across_ref, s32[16,128]{1,0:T(8,128)S(1)} %copy-done.2), custom_call_target="tpu_custom_call" | custom-call | flops 1024 | bytes 1024 | tf_op jit(solution)/shard_map/finish/pallas_call | solution.py:170
  (36 shorter events, 1.3 us)
Async XLA Ops:
  0.0 7.2 %copy-start.1 = (bf16[1,128,4,1024]{3,2,1,0:T(4,128)(2,1)S(1)}, bf16[1,128,4,1024]{3,2,1,0:T(4,128)(2,1)}, u32[]{:S(2)}) copy-start(bf16[1,128,4,1024]{3,2,1,0:T(4,128)(2,1)} %param.12) | copy-start | bytes 3145732
  2.9 4.3 %copy-start.6 = (s32[16]{0:T(128)S(1)}, s32[16]{0:T(128)}, u32[]{:S(2)}) copy-start(s32[16]{0:T(128)} %refs_3_.1) | copy-start | bytes 196
  2.9 4.3 %copy-start.3 = (s32[8]{0:T(128)S(1)}, s32[8]{0:T(128)}, u32[]{:S(2)}) copy-start(s32[8]{0:T(128)} %refs_0_.1) | copy-start | bytes 100
  2.9 4.3 %copy-start.4 = (s32[8]{0:T(128)S(1)}, s32[8]{0:T(128)}, u32[]{:S(2)}) copy-start(s32[8]{0:T(128)} %refs_1_.1) | copy-start | bytes 100
  2.9 4.3 %copy-start.5 = (s32[4]{0:T(128)S(1)}, s32[4]{0:T(128)}, u32[]{:S(2)}) copy-start(s32[4]{0:T(128)} %refs_2_.1) | copy-start | bytes 52
  2.9 18.5 %collective-permute-start.8 = (bf16[2,2,256,256]{3,2,1,0:T(8,128)(2,1)}, bf16[2,2,256,256]{3,2,1,0:T(8,128)(2,1)S(1)}, u32[]{:S(2)}, u32[]{:S(2)}) collective-permute-start(bf16[2,2,256,256]{3,2,1,0:T(8,128)(2,1)} %get-tuple-element.33.refs_8_.refs_1_), channel_id=1, source_target_pairs={{0,4},{4,8},{8,12},{12,0},{1,5},{5,9},{9,13},{13,1},{2,6},{6,10},{... | collective-permute-start | bytes 1572872 | tf_op jit(solution)/shard_map/ppermute | solution.py:183
  5.0 16.5 %collective-permute-start.9 = (bf16[2,2,256,256]{3,2,1,0:T(8,128)(2,1)}, bf16[2,2,256,256]{3,2,1,0:T(8,128)(2,1)S(1)}, u32[]{:S(2)}, u32[]{:S(2)}) collective-permute-start(bf16[2,2,256,256]{3,2,1,0:T(8,128)(2,1)} %get-tuple-element.33.refs_8_.refs_1_), channel_id=1, source_target_pairs={{0,12},{4,0},{8,4},{12,8},{1,13},{5,1},{9,5},{13,9},{2,14},{6,2},{... | collective-permute-start | bytes 1572872 | tf_op jit(solution)/shard_map/ppermute | solution.py:183
  9.0 2.3 %collective-permute-start = (bf16[2,128,256]{2,1,0:T(8,128)(2,1)S(1)}, bf16[2,128,256]{2,1,0:T(8,128)(2,1)S(1)}, u32[]{:S(2)}, u32[]{:S(2)}) collective-permute-start(bf16[2,128,256]{2,1,0:T(8,128)(2,1)S(1)} %get-tuple-element.46), channel_id=1, source_target_pairs={{0,0},{1,32},{2,64},{3,96},{16,16},{17,48},{18,80},{19,112},{32,1}... | collective-permute-start | bytes 393224 | tf_op jit(solution)/shard_map/ppermute | solution.py:216
  9.7 21.7 %copy-start = (bf16[2,2,256,256]{3,2,1,0:T(8,128)(2,1)S(1)}, bf16[2,2,256,256]{3,2,1,0:T(8,128)(2,1)}, u32[]{:S(2)}) copy-start(bf16[2,2,256,256]{3,2,1,0:T(8,128)(2,1)} %get-tuple-element.33.refs_8_.refs_1_) | copy-start | bytes 1572868
  9.7 10.6 %collective-permute-start.1 = (bf16[2,128,256]{2,1,0:T(8,128)(2,1)S(1)}, bf16[2,128,256]{2,1,0:T(8,128)(2,1)S(1)}, u32[]{:S(2)}, u32[]{:S(2)}) collective-permute-start(bf16[2,128,256]{2,1,0:T(8,128)(2,1)S(1)} %get-tuple-element.45), channel_id=1, source_target_pairs={{0,16},{1,48},{2,80},{3,112},{16,0},{17,32},{18,64},{19,96},{32,17... | collective-permute-start | bytes 393224 | tf_op jit(solution)/shard_map/ppermute | solution.py:216
  11.3 13.5 %collective-permute-start.2 = (bf16[2,128,256]{2,1,0:T(8,128)(2,1)S(1)}, bf16[2,128,256]{2,1,0:T(8,128)(2,1)S(1)}, u32[]{:S(2)}, u32[]{:S(2)}) collective-permute-start(bf16[2,128,256]{2,1,0:T(8,128)(2,1)S(1)} %collective-permute-done.refs_0_), channel_id=1, source_target_pairs={{0,2},{1,3},{2,0},{3,1},{4,6},{5,7},{6,4},{7,5},{8,10},{9,11},{10,... | collective-permute-start | bytes 393224 | tf_op jit(solution)/shard_map/ppermute | solution.py:191
  17.3 9.4 %collective-permute-start.4 = (bf16[2,128,256]{2,1,0:T(8,128)(2,1)S(1)}, bf16[2,128,256]{2,1,0:T(8,128)(2,1)S(1)}, u32[]{:S(2)}, u32[]{:S(2)}) collective-permute-start(bf16[2,128,256]{2,1,0:T(8,128)(2,1)S(1)} %collective-permute-done.refs_0_), channel_id=1, source_target_pairs={{0,1},{1,0},{2,3},{3,2},{4,5},{5,4},{6,7},{7,6},{8,9},{9,8},{10,11... | collective-permute-start | bytes 393224 | tf_op jit(solution)/shard_map/ppermute | solution.py:191
  20.3 6.1 %collective-permute-start.3 = (bf16[2,128,256]{2,1,0:T(8,128)(2,1)S(1)}, bf16[2,128,256]{2,1,0:T(8,128)(2,1)S(1)}, u32[]{:S(2)}, u32[]{:S(2)}) collective-permute-start(bf16[2,128,256]{2,1,0:T(8,128)(2,1)S(1)} %collective-permute-done.1.refs_1_), channel_id=1, source_target_pairs={{0,2},{1,3},{2,0},{3,1},{4,6},{5,7},{6,4},{7,5},{8,10},{9,11},{10,... | collective-permute-start | bytes 393224 | tf_op jit(solution)/shard_map/ppermute | solution.py:191
  21.4 10.0 %copy-start.2 = (s32[16,128]{1,0:T(8,128)S(1)}, s32[16,128]{1,0:T(8,128)}, u32[]{:S(2)}) copy-start(s32[16,128]{1,0:T(8,128)} %get-tuple-element.34.refs_13_.refs_6_.table) | copy-start | bytes 24580
  21.4 9.9 %collective-permute-start.10 = (bf16[2,256,256]{2,1,0:T(8,128)(2,1)S(1)}, bf16[2,256,256]{2,1,0:T(8,128)(2,1)S(1)}, u32[]{:S(2)}, u32[]{:S(2)}) collective-permute-start(bf16[2,256,256]{2,1,0:T(8,128)(2,1)S(1)} %slice_bitcast_fusion.3), channel_id=1, source_target_pairs={{0,4},{4,8},{8,12},{12,0},{1,5},{5,9},{9,13},{13,1},{2,6},{6,10},{... | collective-permute-start | bytes 786440 | tf_op jit(solution)/shard_map/ppermute | solution.py:183
  21.5 9.8 %collective-permute-start.11 = (bf16[2,256,256]{2,1,0:T(8,128)(2,1)S(1)}, bf16[2,256,256]{2,1,0:T(8,128)(2,1)S(1)}, u32[]{:S(2)}, u32[]{:S(2)}) collective-permute-start(bf16[2,256,256]{2,1,0:T(8,128)(2,1)S(1)} %slice_bitcast_fusion.2), channel_id=1, source_target_pairs={{0,12},{4,0},{8,4},{12,8},{1,13},{5,1},{9,5},{13,9},{2,14},{6,2},{... | collective-permute-start | bytes 786440 | tf_op jit(solution)/shard_map/ppermute | solution.py:183
  24.8 2.0 %collective-permute-start.5 = (bf16[2,128,256]{2,1,0:T(8,128)(2,1)S(1)}, bf16[2,128,256]{2,1,0:T(8,128)(2,1)S(1)}, u32[]{:S(2)}, u32[]{:S(2)}) collective-permute-start(bf16[2,128,256]{2,1,0:T(8,128)(2,1)S(1)} %collective-permute-done.1.refs_1_), channel_id=1, source_target_pairs={{0,1},{1,0},{2,3},{3,2},{4,5},{5,4},{6,7},{7,6},{8,9},{9,8},{10,11... | collective-permute-start | bytes 393224 | tf_op jit(solution)/shard_map/ppermute | solution.py:191
  26.4 1.4 %collective-permute-start.6 = (bf16[2,128,256]{2,1,0:T(8,128)(2,1)S(1)}, bf16[2,128,256]{2,1,0:T(8,128)(2,1)S(1)}, u32[]{:S(2)}, u32[]{:S(2)}) collective-permute-start(bf16[2,128,256]{2,1,0:T(8,128)(2,1)S(1)} %collective-permute-done.2.refs_2_), channel_id=1, source_target_pairs={{0,1},{1,0},{2,3},{3,2},{4,5},{5,4},{6,7},{7,6},{8,9},{9,8},{10,11... | collective-permute-start | bytes 393224 | tf_op jit(solution)/shard_map/ppermute | solution.py:191
  26.7 1.3 %collective-permute-start.7 = (bf16[2,128,256]{2,1,0:T(8,128)(2,1)S(1)}, bf16[2,128,256]{2,1,0:T(8,128)(2,1)S(1)}, u32[]{:S(2)}, u32[]{:S(2)}) collective-permute-start(bf16[2,128,256]{2,1,0:T(8,128)(2,1)S(1)} %collective-permute-done.3.refs_3_), channel_id=1, source_target_pairs={{0,1},{1,0},{2,3},{3,2},{4,5},{5,4},{6,7},{7,6},{8,9},{9,8},{10,11... | collective-permute-start | bytes 393224 | tf_op jit(solution)/shard_map/ppermute | solution.py:191
  32.8 7.0 %collective-permute-start.12 = (f32[256,128]{1,0:T(8,128)S(1)}, f32[256,128]{1,0:T(8,128)S(1)}, u32[]{:S(2)}, u32[]{:S(2)}) collective-permute-start(f32[256,128]{1,0:T(8,128)S(1)} %get-tuple-element.44), channel_id=1, source_target_pairs={{0,16},{16,32},{32,48},{48,0},{64,80},{80,96},{96,112},{112,64},{1... | collective-permute-start | bytes 393224 | tf_op jit(solution)/shard_map/ppermute | solution.py:187
  33.7 6.2 %collective-permute-start.14 = (f32[256,128]{1,0:T(8,128)S(1)}, f32[256,128]{1,0:T(8,128)S(1)}, u32[]{:S(2)}, u32[]{:S(2)}) collective-permute-start(f32[256,128]{1,0:T(8,128)S(1)} %get-tuple-element.43), channel_id=1, source_target_pairs={{0,48},{16,0},{32,16},{48,32},{64,112},{80,64},{96,80},{112,96},{1... | collective-permute-start | bytes 393224 | tf_op jit(solution)/shard_map/ppermute | solution.py:187
  39.8 9.0 %collective-permute-start.13 = (f32[2,256,128]{2,1,0:T(8,128)S(1)}, f32[2,256,128]{2,1,0:T(8,128)S(1)}, u32[]{:S(2)}, u32[]{:S(2)}) collective-permute-start(f32[2,256,128]{2,1,0:T(8,128)S(1)} %get-tuple-element.42), channel_id=1, source_target_pairs={{0,16},{16,32},{32,48},{48,0},{64,80},{80,96},{96,112},{112,64},{1... | collective-permute-start | bytes 786440 | tf_op jit(solution)/shard_map/ppermute | solution.py:187
  39.9 9.0 %collective-permute-start.15 = (f32[2,256,128]{2,1,0:T(8,128)S(1)}, f32[2,256,128]{2,1,0:T(8,128)S(1)}, u32[]{:S(2)}, u32[]{:S(2)}) collective-permute-start(f32[2,256,128]{2,1,0:T(8,128)S(1)} %get-tuple-element.41), channel_id=1, source_target_pairs={{0,48},{16,0},{32,16},{48,32},{64,112},{80,64},{96,80},{112,96},{1... | collective-permute-start | bytes 786440 | tf_op jit(solution)/shard_map/ppermute | solution.py:187
  48.9 6.6 %collective-permute-start.16 = (f32[256,128]{1,0:T(8,128)S(1)}, f32[256,128]{1,0:T(8,128)S(1)}, u32[]{:S(2)}, u32[]{:S(2)}) collective-permute-start(f32[256,128]{1,0:T(8,128)S(1)} %bitcast_add_fusion), channel_id=1, source_target_pairs={{0,64},{16,80},{32,96},{48,112},{64,0},{80,16},{96,32},{112,48},{1... | collective-permute-start | bytes 393224 | tf_op jit(solution)/shard_map/ppermute | solution.py:191

commit v5 on v4

--- a/solution.py
+++ b/solution.py
@@ -71,15 +71,20 @@
     for n, entry in enumerate(entries):
         held_table = jnp.where(line == n, entry, held_table)
     table[...] = held_table
-    lanes = [irrep_lanes(at * FOLD, FOLD, virt) for at in range(4)]
+    dtype = w_ref.dtype
+    small = lambda value: value.astype(jnp.float32).astype(dtype)
+    lanes = [small(irrep_lanes(at * FOLD, FOLD, virt)) for at in range(4)]
     rows = irrep_rows(row * 256, 256, virt)
     irr_j = irrep(j_ref[col], occ)
     for k in range(2):
-        want = rows ^ (irr_j ^ irrep(k_ref[2 * ctr + k], occ))
+        want = small(rows ^ (irr_j ^ irrep(k_ref[2 * ctr + k], occ)))
         for n, ref in enumerate((w_ref, u_ref)):
             copies[k][n].wait()
-            folded = fold_of(lambda at: ref[k, :, at * FOLD : (at + 1) * FOLD], want, lanes)
-            out_ref[n, k] = folded.T.astype(out_ref.dtype)
+            total = None
+            for at, irr in enumerate(lanes):
+                kept = jnp.where(want == irr, ref[k, :, at * FOLD : (at + 1) * FOLD], jnp.zeros((), dtype))
+                total = kept if total is None else total + kept
+            out_ref[n, k] = total.T
 
 
 def fold_amplitudes(t_ref, occ_ref, virt_ref, slab_ref, k_ref, out_ref):

time: 56.4 us -> 56.2 us (level)
  no operation moved by 1% of the time
where the time goes in v5:
time: 56.2 us; the launch traced here: 56.1 us
  starting transfers between devices  30 us (53%)
  waiting for transfers between devices  15.9 us (28%)
  Pallas kernels  9.8 us (17%)
    ppermute x7, starting transfers between devices, swap(): return lax.ppermute(value, axis, [(at, at ^ mask) for at in range(count)])  13.5 us
    pallas_call x5, Pallas kernels, call(): pl.pallas_call(kernel, out_shape=[jax.ShapeDtypeStruct(*out) for out in o...  9.8 us
    ppermute x4, starting transfers between devices, shift(): lax.ppermute(value, axis, [(at, (at + step) % count) for at in range(coun...  7.62 us
    ppermute x4, starting transfers between devices, shift_y(): lax.ppermute(value, 'ctr', [(at, at // 4 * 4 + (at + step) % 4) for at in...  6.6 us
    ppermute x7, waiting for transfers between devices, swap(): return lax.ppermute(value, axis, [(at, at ^ mask) for at in range(count)])  6.4 us
    ppermute x4, waiting for transfers between devices, shift_y(): lax.ppermute(value, 'ctr', [(at, at // 4 * 4 + (at + step) % 4) for at in...  6.19 us
    ppermute x4, waiting for transfers between devices, shift(): lax.ppermute(value, axis, [(at, (at + step) % count) for at in range(coun...  3.27 us
    ppermute x2, starting transfers between devices, spread(): return lax.ppermute(value, ('ctr', 'col'), pairs)  2.32 us
  transfers between devices with their start and end apart: 17, of which 7 were waited for; matrix products, arithmetic and copies ran while one was open for 0% of the time, Pallas kernels for 9%

profile of v5, /device:TPU:0, one launch (start us, length us, event | category | flops | bytes accessed | tf_op | source)
XLA Modules:
  0.0 56.1 jit_solution(3539232865676078711)
XLA Ops:
  0.0 2.6 %fold_integrals.1 = (bf16[2,2,256,256]{3,2,1,0:T(8,128)(2,1)}, s32[16,128]{1,0:T(8,128)}) custom-call(bf16[2,256,1024]{2,1,0:T(8,128)(2,1)} %bitcast.55, bf16[2,256,1024]{2,1,0:T(8,128)(2,1)} %bitcast.56, s32[8]{0:T(128)} %refs_0_.1, s32[8]{0:T(128)} %refs_1_.1, s32[4]{0:T(128)} %refs_2_.1, s32[16]{0:T(128)} %refs_3_.1, s32[4]{0:T(128)} %refs_4_.1), custom_call_target="tpu_custom_call" | custom-call | flops 1024 | bytes 1024 | tf_op jit(solution)/shard_map/fold_integrals/pallas_call | solution.py:175
  2.7 2.1 %collective-permute-start.8 = (bf16[2,2,256,256]{3,2,1,0:T(8,128)(2,1)}, bf16[2,2,256,256]{3,2,1,0:T(8,128)(2,1)S(1)}, u32[]{:S(2)}, u32[]{:S(2)}) collective-permute-start(bf16[2,2,256,256]{3,2,1,0:T(8,128)(2,1)} %get-tuple-element.33.refs_8_.refs_1_), channel_id=1, source_target_pairs={{0,4},{4,8},{8,12},{12,0},{1,5},{5,9},{9,13},{13,1},{2,6},{6,10},{... | collective-permute-start | bytes 1572872 | tf_op jit(solution)/shard_map/ppermute | solution.py:188
  4.7 2.2 %collective-permute-start.9 = (bf16[2,2,256,256]{3,2,1,0:T(8,128)(2,1)}, bf16[2,2,256,256]{3,2,1,0:T(8,128)(2,1)S(1)}, u32[]{:S(2)}, u32[]{:S(2)}) collective-permute-start(bf16[2,2,256,256]{3,2,1,0:T(8,128)(2,1)} %get-tuple-element.33.refs_8_.refs_1_), channel_id=1, source_target_pairs={{0,12},{4,0},{8,4},{12,8},{1,13},{5,1},{9,5},{13,9},{2,14},{6,2},{... | collective-permute-start | bytes 1572872 | tf_op jit(solution)/shard_map/ppermute | solution.py:188
  7.0 1.8 %fold_amplitudes.1 = bf16[2,2,128,256]{3,2,1,0:T(8,128)(2,1)S(1)} custom-call(bf16[128,4,1024]{2,1,0:T(4,128)(2,1)S(1)} %bitcast.54, s32[8]{0:T(128)S(1)} %copy-done.3, s32[8]{0:T(128)S(1)} %copy-done.4, s32[4]{0:T(128)S(1)} %copy-done.5, s32[16]{0:T(128)S(1)} %copy-done.6), custom_call_target="tpu_custom_call" | custom-call | flops 1024 | bytes 1024 | tf_op jit(solution)/shard_map/fold_amplitudes/pallas_call | solution.py:175
  8.8 0.7 %collective-permute-start = (bf16[2,128,256]{2,1,0:T(8,128)(2,1)S(1)}, bf16[2,128,256]{2,1,0:T(8,128)(2,1)S(1)}, u32[]{:S(2)}, u32[]{:S(2)}) collective-permute-start(bf16[2,128,256]{2,1,0:T(8,128)(2,1)S(1)} %get-tuple-element.46), channel_id=1, source_target_pairs={{0,0},{1,32},{2,64},{3,96},{16,16},{17,48},{18,80},{19,112},{32,1}... | collective-permute-start | bytes 393224 | tf_op jit(solution)/shard_map/ppermute | solution.py:221
  9.4 1.7 %collective-permute-start.1 = (bf16[2,128,256]{2,1,0:T(8,128)(2,1)S(1)}, bf16[2,128,256]{2,1,0:T(8,128)(2,1)S(1)}, u32[]{:S(2)}, u32[]{:S(2)}) collective-permute-start(bf16[2,128,256]{2,1,0:T(8,128)(2,1)S(1)} %get-tuple-element.45), channel_id=1, source_target_pairs={{0,16},{1,48},{2,80},{3,112},{16,0},{17,32},{18,64},{19,96},{32,17... | collective-permute-start | bytes 393224 | tf_op jit(solution)/shard_map/ppermute | solution.py:221
  11.1 6.0 %collective-permute-start.2 = (bf16[2,128,256]{2,1,0:T(8,128)(2,1)S(1)}, bf16[2,128,256]{2,1,0:T(8,128)(2,1)S(1)}, u32[]{:S(2)}, u32[]{:S(2)}) collective-permute-start(bf16[2,128,256]{2,1,0:T(8,128)(2,1)S(1)} %collective-permute-done.refs_0_), channel_id=1, source_target_pairs={{0,2},{1,3},{2,0},{3,1},{4,6},{5,7},{6,4},{7,5},{8,10},{9,11},{10,... | collective-permute-start | bytes 393224 | tf_op jit(solution)/shard_map/ppermute | solution.py:196
  17.1 2.9 %collective-permute-start.4 = (bf16[2,128,256]{2,1,0:T(8,128)(2,1)S(1)}, bf16[2,128,256]{2,1,0:T(8,128)(2,1)S(1)}, u32[]{:S(2)}, u32[]{:S(2)}) collective-permute-start(bf16[2,128,256]{2,1,0:T(8,128)(2,1)S(1)} %collective-permute-done.refs_0_), channel_id=1, source_target_pairs={{0,1},{1,0},{2,3},{3,2},{4,5},{5,4},{6,7},{7,6},{8,9},{9,8},{10,11... | collective-permute-start | bytes 393224 | tf_op jit(solution)/shard_map/ppermute | solution.py:196
  20.0 1.1 %collective-permute-start.3 = (bf16[2,128,256]{2,1,0:T(8,128)(2,1)S(1)}, bf16[2,128,256]{2,1,0:T(8,128)(2,1)S(1)}, u32[]{:S(2)}, u32[]{:S(2)}) collective-permute-start(bf16[2,128,256]{2,1,0:T(8,128)(2,1)S(1)} %collective-permute-done.1.refs_1_), channel_id=1, source_target_pairs={{0,2},{1,3},{2,0},{3,1},{4,6},{5,7},{6,4},{7,5},{8,10},{9,11},{10,... | collective-permute-start | bytes 393224 | tf_op jit(solution)/shard_map/ppermute | solution.py:196
  21.3 3.3 %collective-permute-start.11 = (bf16[2,256,256]{2,1,0:T(8,128)(2,1)S(1)}, bf16[2,256,256]{2,1,0:T(8,128)(2,1)S(1)}, u32[]{:S(2)}, u32[]{:S(2)}) collective-permute-start(bf16[2,256,256]{2,1,0:T(8,128)(2,1)S(1)} %slice_bitcast_fusion.2), channel_id=1, source_target_pairs={{0,12},{4,0},{8,4},{12,8},{1,13},{5,1},{9,5},{13,9},{2,14},{6,2},{... | collective-permute-start | bytes 786440 | tf_op jit(solution)/shard_map/ppermute | solution.py:188
  24.6 1.0 %collective-permute-start.5 = (bf16[2,128,256]{2,1,0:T(8,128)(2,1)S(1)}, bf16[2,128,256]{2,1,0:T(8,128)(2,1)S(1)}, u32[]{:S(2)}, u32[]{:S(2)}) collective-permute-start(bf16[2,128,256]{2,1,0:T(8,128)(2,1)S(1)} %collective-permute-done.1.refs_1_), channel_id=1, source_target_pairs={{0,1},{1,0},{2,3},{3,2},{4,5},{5,4},{6,7},{7,6},{8,9},{9,8},{10,11... | collective-permute-start | bytes 393224 | tf_op jit(solution)/shard_map/ppermute | solution.py:196
  25.6 0.5 collective-permute-done.3.refs_3_
  26.7 0.8 %collective-permute-done.6.refs_6_ = bf16[2,128,256]{2,1,0:T(8,128)(2,1)S(1)} collective-permute-done((bf16[2,128,256]{2,1,0:T(8,128)(2,1)S(1)}, bf16[2,128,256]{2,1,0:T(8,128)(2,1)S(1)}, u32[]{:S(2)}, u32[]{:S(2)}) %collective-permute-start.6) | collective-permute-done | bytes 131104 | tf_op jit(solution)/shard_map/ppermute | solution.py:196
  27.9 3.3 %collective-permute-done.10.refs_11_.refs_4_ = bf16[2,256,256]{2,1,0:T(8,128)(2,1)S(1)} collective-permute-done((bf16[2,256,256]{2,1,0:T(8,128)(2,1)S(1)}, bf16[2,256,256]{2,1,0:T(8,128)(2,1)S(1)}, u32[]{:S(2)}, u32[]{:S(2)}) %collective-permute-start.10) | collective-permute-done | bytes 262176 | tf_op jit(solution)/shard_map/ppermute | solution.py:188
  31.1 1.4 %far_products.1 = (f32[2,256,128]{2,1,0:T(8,128)S(1)}, bf16[2,8,128,256]{3,2,1,0:T(8,128)(2,1)S(1)}) custom-call(bf16[2,128,256]{2,1,0:T(8,128)(2,1)S(1)} %collective-permute-done.refs_0_, bf16[2,128,256]{2,1,0:T(8,128)(2,1)S(1)} %collective-permute-done.1.refs_1_, bf16[2,128,256]{2,1,0:T(8,128)(2,1)S(1)} %collective-permute-done.2.refs_2_, ...), custom_call_target="tpu_custom_call" | custom-call | flops 1024 | bytes 1024 | tf_op jit(solution)/shard_map/far_products/pallas_call | solution.py:175
  32.6 0.9 %collective-permute-start.12 = (f32[256,128]{1,0:T(8,128)S(1)}, f32[256,128]{1,0:T(8,128)S(1)}, u32[]{:S(2)}, u32[]{:S(2)}) collective-permute-start(f32[256,128]{1,0:T(8,128)S(1)} %get-tuple-element.44), channel_id=1, source_target_pairs={{0,16},{16,32},{32,48},{48,0},{64,80},{80,96},{96,112},{112,64},{1... | collective-permute-start | bytes 393224 | tf_op jit(solution)/shard_map/ppermute | solution.py:192
  33.4 2.4 %collective-permute-start.14 = (f32[256,128]{1,0:T(8,128)S(1)}, f32[256,128]{1,0:T(8,128)S(1)}, u32[]{:S(2)}, u32[]{:S(2)}) collective-permute-start(f32[256,128]{1,0:T(8,128)S(1)} %get-tuple-element.43), channel_id=1, source_target_pairs={{0,48},{16,0},{32,16},{48,32},{64,112},{80,64},{96,80},{112,96},{1... | collective-permute-start | bytes 393224 | tf_op jit(solution)/shard_map/ppermute | solution.py:192
  35.9 3.2 %near_products.1 = f32[3,2,256,128]{3,2,1,0:T(8,128)S(1)} custom-call(bf16[2,8,128,256]{3,2,1,0:T(8,128)(2,1)S(1)} %get-tuple-element.35.refs_0_, bf16[2,2,256,256]{3,2,1,0:T(8,128)(2,1)S(1)} %copy-done, bf16[2,2,256,256]{3,2,1,0:T(8,128)(2,1)S(1)} %collective-permute-done.8.refs_9_.refs_2_, ...), custom_call_target="tpu_custom_call" | custom-call | flops 1024 | bytes 1024 | tf_op jit(solution)/shard_map/near_products/pallas_call | solution.py:175
  39.1 0.5 collective-permute-done.12
  39.7 3.2 %collective-permute-start.15 = (f32[2,256,128]{2,1,0:T(8,128)S(1)}, f32[2,256,128]{2,1,0:T(8,128)S(1)}, u32[]{:S(2)}, u32[]{:S(2)}) collective-permute-start(f32[2,256,128]{2,1,0:T(8,128)S(1)} %get-tuple-element.41), channel_id=1, source_target_pairs={{0,48},{16,0},{32,16},{48,32},{64,112},{80,64},{96,80},{112,96},{1... | collective-permute-start | bytes 786440 | tf_op jit(solution)/shard_map/ppermute | solution.py:192
  42.9 5.7 %collective-permute-done.13.low = f32[2,256,128]{2,1,0:T(8,128)S(1)} collective-permute-done((f32[2,256,128]{2,1,0:T(8,128)S(1)}, f32[2,256,128]{2,1,0:T(8,128)S(1)}, u32[]{:S(2)}, u32[]{:S(2)}) %collective-permute-start.13) | collective-permute-done | bytes 262176 | tf_op jit(solution)/shard_map/ppermute | solution.py:192
  48.7 1.9 %collective-permute-start.16 = (f32[256,128]{1,0:T(8,128)S(1)}, f32[256,128]{1,0:T(8,128)S(1)}, u32[]{:S(2)}, u32[]{:S(2)}) collective-permute-start(f32[256,128]{1,0:T(8,128)S(1)} %bitcast_add_fusion), channel_id=1, source_target_pairs={{0,64},{16,80},{32,96},{48,112},{64,0},{80,16},{96,32},{112,48},{1... | collective-permute-start | bytes 393224 | tf_op jit(solution)/shard_map/ppermute | solution.py:196
  50.6 4.7 %collective-permute-done.16.across_ref = f32[256,128]{1,0:T(8,128)S(1)} collective-permute-done((f32[256,128]{1,0:T(8,128)S(1)}, f32[256,128]{1,0:T(8,128)S(1)}, u32[]{:S(2)}, u32[]{:S(2)}) %collective-permute-start.16) | collective-permute-done | bytes 131104 | tf_op jit(solution)/shard_map/ppermute | solution.py:196
  55.2 0.9 %finish.1 = bf16[128,1024]{1,0:T(8,128)(2,1)} custom-call(f32[2,256,128]{2,1,0:T(8,128)S(1)} %get-tuple-element.38.here, f32[2,256,128]{2,1,0:T(8,128)S(1)} %collective-permute-done.13.low, f32[2,256,128]{2,1,0:T(8,128)S(1)} %collective-permute-done.15.high, f32[256,128]{1,0:T(8,128)S(1)} %collective-permute-done.16.across_ref, s32[16,128]{1,0:T(8,128)S(1)} %copy-done.2), custom_call_target="tpu_custom_call" | custom-call | flops 1024 | bytes 1024 | tf_op jit(solution)/shard_map/finish/pallas_call | solution.py:175
  (36 shorter events, 1.3 us)
Async XLA Ops:
  0.0 6.9 %copy-start.1 = (bf16[1,128,4,1024]{3,2,1,0:T(4,128)(2,1)S(1)}, bf16[1,128,4,1024]{3,2,1,0:T(4,128)(2,1)}, u32[]{:S(2)}) copy-start(bf16[1,128,4,1024]{3,2,1,0:T(4,128)(2,1)} %param.12) | copy-start | bytes 3145732
  2.6 4.3 %copy-start.6 = (s32[16]{0:T(128)S(1)}, s32[16]{0:T(128)}, u32[]{:S(2)}) copy-start(s32[16]{0:T(128)} %refs_3_.1) | copy-start | bytes 196
  2.6 4.3 %copy-start.3 = (s32[8]{0:T(128)S(1)}, s32[8]{0:T(128)}, u32[]{:S(2)}) copy-start(s32[8]{0:T(128)} %refs_0_.1) | copy-start | bytes 100
  2.6 4.3 %copy-start.4 = (s32[8]{0:T(128)S(1)}, s32[8]{0:T(128)}, u32[]{:S(2)}) copy-start(s32[8]{0:T(128)} %refs_1_.1) | copy-start | bytes 100
  2.7 4.3 %copy-start.5 = (s32[4]{0:T(128)S(1)}, s32[4]{0:T(128)}, u32[]{:S(2)}) copy-start(s32[4]{0:T(128)} %refs_2_.1) | copy-start | bytes 52
  2.7 18.5 %collective-permute-start.8 = (bf16[2,2,256,256]{3,2,1,0:T(8,128)(2,1)}, bf16[2,2,256,256]{3,2,1,0:T(8,128)(2,1)S(1)}, u32[]{:S(2)}, u32[]{:S(2)}) collective-permute-start(bf16[2,2,256,256]{3,2,1,0:T(8,128)(2,1)} %get-tuple-element.33.refs_8_.refs_1_), channel_id=1, source_target_pairs={{0,4},{4,8},{8,12},{12,0},{1,5},{5,9},{9,13},{13,1},{2,6},{6,10},{... | collective-permute-start | bytes 1572872 | tf_op jit(solution)/shard_map/ppermute | solution.py:188
  4.7 16.5 %collective-permute-start.9 = (bf16[2,2,256,256]{3,2,1,0:T(8,128)(2,1)}, bf16[2,2,256,256]{3,2,1,0:T(8,128)(2,1)S(1)}, u32[]{:S(2)}, u32[]{:S(2)}) collective-permute-start(bf16[2,2,256,256]{3,2,1,0:T(8,128)(2,1)} %get-tuple-element.33.refs_8_.refs_1_), channel_id=1, source_target_pairs={{0,12},{4,0},{8,4},{12,8},{1,13},{5,1},{9,5},{13,9},{2,14},{6,2},{... | collective-permute-start | bytes 1572872 | tf_op jit(solution)/shard_map/ppermute | solution.py:188
  8.8 2.3 %collective-permute-start = (bf16[2,128,256]{2,1,0:T(8,128)(2,1)S(1)}, bf16[2,128,256]{2,1,0:T(8,128)(2,1)S(1)}, u32[]{:S(2)}, u32[]{:S(2)}) collective-permute-start(bf16[2,128,256]{2,1,0:T(8,128)(2,1)S(1)} %get-tuple-element.46), channel_id=1, source_target_pairs={{0,0},{1,32},{2,64},{3,96},{16,16},{17,48},{18,80},{19,112},{32,1}... | collective-permute-start | bytes 393224 | tf_op jit(solution)/shard_map/ppermute | solution.py:221
  9.4 21.7 %copy-start = (bf16[2,2,256,256]{3,2,1,0:T(8,128)(2,1)S(1)}, bf16[2,2,256,256]{3,2,1,0:T(8,128)(2,1)}, u32[]{:S(2)}) copy-start(bf16[2,2,256,256]{3,2,1,0:T(8,128)(2,1)} %get-tuple-element.33.refs_8_.refs_1_) | copy-start | bytes 1572868
  9.4 10.6 %collective-permute-start.1 = (bf16[2,128,256]{2,1,0:T(8,128)(2,1)S(1)}, bf16[2,128,256]{2,1,0:T(8,128)(2,1)S(1)}, u32[]{:S(2)}, u32[]{:S(2)}) collective-permute-start(bf16[2,128,256]{2,1,0:T(8,128)(2,1)S(1)} %get-tuple-element.45), channel_id=1, source_target_pairs={{0,16},{1,48},{2,80},{3,112},{16,0},{17,32},{18,64},{19,96},{32,17... | collective-permute-start | bytes 393224 | tf_op jit(solution)/shard_map/ppermute | solution.py:221
  11.1 13.5 %collective-permute-start.2 = (bf16[2,128,256]{2,1,0:T(8,128)(2,1)S(1)}, bf16[2,128,256]{2,1,0:T(8,128)(2,1)S(1)}, u32[]{:S(2)}, u32[]{:S(2)}) collective-permute-start(bf16[2,128,256]{2,1,0:T(8,128)(2,1)S(1)} %collective-permute-done.refs_0_), channel_id=1, source_target_pairs={{0,2},{1,3},{2,0},{3,1},{4,6},{5,7},{6,4},{7,5},{8,10},{9,11},{10,... | collective-permute-start | bytes 393224 | tf_op jit(solution)/shard_map/ppermute | solution.py:196
  17.1 9.4 %collective-permute-start.4 = (bf16[2,128,256]{2,1,0:T(8,128)(2,1)S(1)}, bf16[2,128,256]{2,1,0:T(8,128)(2,1)S(1)}, u32[]{:S(2)}, u32[]{:S(2)}) collective-permute-start(bf16[2,128,256]{2,1,0:T(8,128)(2,1)S(1)} %collective-permute-done.refs_0_), channel_id=1, source_target_pairs={{0,1},{1,0},{2,3},{3,2},{4,5},{5,4},{6,7},{7,6},{8,9},{9,8},{10,11... | collective-permute-start | bytes 393224 | tf_op jit(solution)/shard_map/ppermute | solution.py:196
  20.0 6.1 %collective-permute-start.3 = (bf16[2,128,256]{2,1,0:T(8,128)(2,1)S(1)}, bf16[2,128,256]{2,1,0:T(8,128)(2,1)S(1)}, u32[]{:S(2)}, u32[]{:S(2)}) collective-permute-start(bf16[2,128,256]{2,1,0:T(8,128)(2,1)S(1)} %collective-permute-done.1.refs_1_), channel_id=1, source_target_pairs={{0,2},{1,3},{2,0},{3,1},{4,6},{5,7},{6,4},{7,5},{8,10},{9,11},{10,... | collective-permute-start | bytes 393224 | tf_op jit(solution)/shard_map/ppermute | solution.py:196
  21.2 10.0 %copy-start.2 = (s32[16,128]{1,0:T(8,128)S(1)}, s32[16,128]{1,0:T(8,128)}, u32[]{:S(2)}) copy-start(s32[16,128]{1,0:T(8,128)} %get-tuple-element.34.refs_13_.refs_6_.table) | copy-start | bytes 24580
  21.2 9.9 %collective-permute-start.10 = (bf16[2,256,256]{2,1,0:T(8,128)(2,1)S(1)}, bf16[2,256,256]{2,1,0:T(8,128)(2,1)S(1)}, u32[]{:S(2)}, u32[]{:S(2)}) collective-permute-start(bf16[2,256,256]{2,1,0:T(8,128)(2,1)S(1)} %slice_bitcast_fusion.3), channel_id=1, source_target_pairs={{0,4},{4,8},{8,12},{12,0},{1,5},{5,9},{9,13},{13,1},{2,6},{6,10},{... | collective-permute-start | bytes 786440 | tf_op jit(solution)/shard_map/ppermute | solution.py:188
  21.3 9.8 %collective-permute-start.11 = (bf16[2,256,256]{2,1,0:T(8,128)(2,1)S(1)}, bf16[2,256,256]{2,1,0:T(8,128)(2,1)S(1)}, u32[]{:S(2)}, u32[]{:S(2)}) collective-permute-start(bf16[2,256,256]{2,1,0:T(8,128)(2,1)S(1)} %slice_bitcast_fusion.2), channel_id=1, source_target_pairs={{0,12},{4,0},{8,4},{12,8},{1,13},{5,1},{9,5},{13,9},{2,14},{6,2},{... | collective-permute-start | bytes 786440 | tf_op jit(solution)/shard_map/ppermute | solution.py:188
  24.6 2.0 %collective-permute-start.5 = (bf16[2,128,256]{2,1,0:T(8,128)(2,1)S(1)}, bf16[2,128,256]{2,1,0:T(8,128)(2,1)S(1)}, u32[]{:S(2)}, u32[]{:S(2)}) collective-permute-start(bf16[2,128,256]{2,1,0:T(8,128)(2,1)S(1)} %collective-permute-done.1.refs_1_), channel_id=1, source_target_pairs={{0,1},{1,0},{2,3},{3,2},{4,5},{5,4},{6,7},{7,6},{8,9},{9,8},{10,11... | collective-permute-start | bytes 393224 | tf_op jit(solution)/shard_map/ppermute | solution.py:196
  26.1 1.4 %collective-permute-start.6 = (bf16[2,128,256]{2,1,0:T(8,128)(2,1)S(1)}, bf16[2,128,256]{2,1,0:T(8,128)(2,1)S(1)}, u32[]{:S(2)}, u32[]{:S(2)}) collective-permute-start(bf16[2,128,256]{2,1,0:T(8,128)(2,1)S(1)} %collective-permute-done.2.refs_2_), channel_id=1, source_target_pairs={{0,1},{1,0},{2,3},{3,2},{4,5},{5,4},{6,7},{7,6},{8,9},{9,8},{10,11... | collective-permute-start | bytes 393224 | tf_op jit(solution)/shard_map/ppermute | solution.py:196
  26.5 1.3 %collective-permute-start.7 = (bf16[2,128,256]{2,1,0:T(8,128)(2,1)S(1)}, bf16[2,128,256]{2,1,0:T(8,128)(2,1)S(1)}, u32[]{:S(2)}, u32[]{:S(2)}) collective-permute-start(bf16[2,128,256]{2,1,0:T(8,128)(2,1)S(1)} %collective-permute-done.3.refs_3_), channel_id=1, source_target_pairs={{0,1},{1,0},{2,3},{3,2},{4,5},{5,4},{6,7},{7,6},{8,9},{9,8},{10,11... | collective-permute-start | bytes 393224 | tf_op jit(solution)/shard_map/ppermute | solution.py:196
  32.6 7.0 %collective-permute-start.12 = (f32[256,128]{1,0:T(8,128)S(1)}, f32[256,128]{1,0:T(8,128)S(1)}, u32[]{:S(2)}, u32[]{:S(2)}) collective-permute-start(f32[256,128]{1,0:T(8,128)S(1)} %get-tuple-element.44), channel_id=1, source_target_pairs={{0,16},{16,32},{32,48},{48,0},{64,80},{80,96},{96,112},{112,64},{1... | collective-permute-start | bytes 393224 | tf_op jit(solution)/shard_map/ppermute | solution.py:192
  33.4 6.2 %collective-permute-start.14 = (f32[256,128]{1,0:T(8,128)S(1)}, f32[256,128]{1,0:T(8,128)S(1)}, u32[]{:S(2)}, u32[]{:S(2)}) collective-permute-start(f32[256,128]{1,0:T(8,128)S(1)} %get-tuple-element.43), channel_id=1, source_target_pairs={{0,48},{16,0},{32,16},{48,32},{64,112},{80,64},{96,80},{112,96},{1... | collective-permute-start | bytes 393224 | tf_op jit(solution)/shard_map/ppermute | solution.py:192
  39.6 9.0 %collective-permute-start.13 = (f32[2,256,128]{2,1,0:T(8,128)S(1)}, f32[2,256,128]{2,1,0:T(8,128)S(1)}, u32[]{:S(2)}, u32[]{:S(2)}) collective-permute-start(f32[2,256,128]{2,1,0:T(8,128)S(1)} %get-tuple-element.42), channel_id=1, source_target_pairs={{0,16},{16,32},{32,48},{48,0},{64,80},{80,96},{96,112},{112,64},{1... | collective-permute-start | bytes 786440 | tf_op jit(solution)/shard_map/ppermute | solution.py:192
  39.7 9.0 %collective-permute-start.15 = (f32[2,256,128]{2,1,0:T(8,128)S(1)}, f32[2,256,128]{2,1,0:T(8,128)S(1)}, u32[]{:S(2)}, u32[]{:S(2)}) collective-permute-start(f32[2,256,128]{2,1,0:T(8,128)S(1)} %get-tuple-element.41), channel_id=1, source_target_pairs={{0,48},{16,0},{32,16},{48,32},{64,112},{80,64},{96,80},{112,96},{1... | collective-permute-start | bytes 786440 | tf_op jit(solution)/shard_map/ppermute | solution.py:192
  48.7 6.6 %collective-permute-start.16 = (f32[256,128]{1,0:T(8,128)S(1)}, f32[256,128]{1,0:T(8,128)S(1)}, u32[]{:S(2)}, u32[]{:S(2)}) collective-permute-start(f32[256,128]{1,0:T(8,128)S(1)} %bitcast_add_fusion), channel_id=1, source_target_pairs={{0,64},{16,80},{32,96},{48,112},{64,0},{80,16},{96,32},{112,48},{1... | collective-permute-start | bytes 393224 | tf_op jit(solution)/shard_map/ppermute | solution.py:196

commit v6 on v5

--- a/solution.py
+++ b/solution.py
@@ -164,7 +164,7 @@
 def finish(here, low, high, across_ref, table, out_ref):
     virt, ctr = bounds_in(table), lax.axis_index("ctr")
     h = ctr // 4
-    total = (here[h] + low[h] + high[h] + across_ref[...]).T
+    total = (here[h] + low[...] + high[...] + across_ref[...]).T
     want = irrep_rows(ctr * 128, 128, virt) ^ table[9:10, :1]
     for at in range(4):
         kept = jnp.where(want == irrep_lanes(at * FOLD, FOLD, virt), total, 0.0)
@@ -232,12 +232,13 @@
     )
     below, above = shift_y(far[0], 1), shift_y(far[1], -1)
     near = call(near_products, [((3, 2, FOLD, 128), f32)], [t_all, *integrals, table], [], name="near_products")[0]
-    low = shift_y(near[0].at[0].add(below), 1)
-    high = shift_y(near[1].at[1].add(above), -1)
-    other = 1 - lax.axis_index("ctr") // 4
-    pick = lambda value: lax.dynamic_index_in_dim(value, other, 0, False)
-    across = swap(pick(near[2]) + pick(low) + pick(high), "ctr", 8, 4)
-    out = call(finish, [((128, 4 * FOLD), bf16)], [near[2], low, high, across, table], [], name="finish")[0]
+    low1, high0 = shift_y(near[0, 1], 1), shift_y(near[1, 0], -1)
+    low0, high1 = shift_y(near[0, 0] + below, 1), shift_y(near[1, 1] + above, -1)
+    first = lax.axis_index("ctr") // 4 == 0
+    mine = [jnp.where(first, low0, low1), jnp.where(first, high0, high1)]
+    across = near[2, 0] + low0 + high0, near[2, 1] + low1 + high1
+    across = swap(jnp.where(first, across[1], across[0]), "ctr", 8, 4)
+    out = call(finish, [((128, 4 * FOLD), bf16)], [near[2], *mine, across, table], [], name="finish")[0]
     return out[None, :, None, :]
 
 

time: 56.2 us -> 56.4 us (level)
  starting transfers between devices: 30 us -> 34.2 us
  waiting for transfers between devices: 15.9 us -> 11.8 us
    ppermute x4 -> x6, starting transfers between devices: 6.6 us -> 9.9 us  [shift_y(): lax.ppermute(value, 'ctr', [(at, at // 4 * 4 + (at + step) % 4) for at in...]
    ppermute x4 -> x6, waiting for transfers between devices: 6.19 us -> 2.95 us  [shift_y(): lax.ppermute(value, 'ctr', [(at, at // 4 * 4 + (at + step) % 4) for at in...]
    ppermute x7, waiting for transfers between devices: 6.4 us -> 5.53 us  [swap(): return lax.ppermute(value, axis, [(at, at ^ mask) for at in range(count)])]
    ppermute x7, starting transfers between devices: 13.5 us -> 14.3 us  [swap(): return lax.ppermute(value, axis, [(at, at ^ mask) for at in range(count)])]
  transfers between devices with their start and end apart: 17 -> 19, of which waited for: 7 -> 6; matrix products, arithmetic and copies ran while one was open for 0% -> 0% of each run, Pallas kernels for 9% -> 9%
where the time goes in v6:
time: 56.4 us; the launch traced here: 56.2 us
  starting transfers between devices  34.2 us (61%)
  waiting for transfers between devices  11.8 us (21%)
  Pallas kernels  9.8 us (17%)
    ppermute x7, starting transfers between devices, swap(): return lax.ppermute(value, axis, [(at, at ^ mask) for at in range(count)])  14.3 us
    ppermute x6, starting transfers between devices, shift_y(): lax.ppermute(value, 'ctr', [(at, at // 4 * 4 + (at + step) % 4) for at in...  9.9 us
    pallas_call x5, Pallas kernels, call(): pl.pallas_call(kernel, out_shape=[jax.ShapeDtypeStruct(*out) for out in o...  9.8 us
    ppermute x4, starting transfers between devices, shift(): lax.ppermute(value, axis, [(at, (at + step) % count) for at in range(coun...  7.62 us
    ppermute x7, waiting for transfers between devices, swap(): return lax.ppermute(value, axis, [(at, at ^ mask) for at in range(count)])  5.53 us
    ppermute x4, waiting for transfers between devices, shift(): lax.ppermute(value, axis, [(at, (at + step) % count) for at in range(coun...  3.27 us
    ppermute x6, waiting for transfers between devices, shift_y(): lax.ppermute(value, 'ctr', [(at, at // 4 * 4 + (at + step) % 4) for at in...  2.95 us
    ppermute x2, starting transfers between devices, spread(): return lax.ppermute(value, ('ctr', 'col'), pairs)  2.32 us
  transfers between devices with their start and end apart: 19, of which 6 were waited for; matrix products, arithmetic and copies ran while one was open for 0% of the time, Pallas kernels for 9%

profile of v6, /device:TPU:0, one launch (start us, length us, event | category | flops | bytes accessed | tf_op | source)
XLA Modules:
  0.0 56.2 jit_solution(1135550727602846144)
XLA Ops:
  0.0 2.6 %fold_integrals.1 = (bf16[2,2,256,256]{3,2,1,0:T(8,128)(2,1)}, s32[16,128]{1,0:T(8,128)}) custom-call(bf16[2,256,1024]{2,1,0:T(8,128)(2,1)} %bitcast.47, bf16[2,256,1024]{2,1,0:T(8,128)(2,1)} %bitcast.48, s32[8]{0:T(128)} %refs_0_.1, s32[8]{0:T(128)} %refs_1_.1, s32[4]{0:T(128)} %refs_2_.1, s32[16]{0:T(128)} %refs_3_.1, s32[4]{0:T(128)} %refs_4_.1), custom_call_target="tpu_custom_call" | custom-call | flops 1024 | bytes 1024 | tf_op jit(solution)/shard_map/fold_integrals/pallas_call | solution.py:175
  2.7 2.1 %collective-permute-start.8 = (bf16[2,2,256,256]{3,2,1,0:T(8,128)(2,1)}, bf16[2,2,256,256]{3,2,1,0:T(8,128)(2,1)S(1)}, u32[]{:S(2)}, u32[]{:S(2)}) collective-permute-start(bf16[2,2,256,256]{3,2,1,0:T(8,128)(2,1)} %get-tuple-element.9.refs_8_.refs_1_), channel_id=1, source_target_pairs={{0,4},{4,8},{8,12},{12,0},{1,5},{5,9},{9,13},{13,1},{2,6},{6,10},{... | collective-permute-start | bytes 1572872 | tf_op jit(solution)/shard_map/ppermute | solution.py:188
  4.7 2.2 %collective-permute-start.9 = (bf16[2,2,256,256]{3,2,1,0:T(8,128)(2,1)}, bf16[2,2,256,256]{3,2,1,0:T(8,128)(2,1)S(1)}, u32[]{:S(2)}, u32[]{:S(2)}) collective-permute-start(bf16[2,2,256,256]{3,2,1,0:T(8,128)(2,1)} %get-tuple-element.9.refs_8_.refs_1_), channel_id=1, source_target_pairs={{0,12},{4,0},{8,4},{12,8},{1,13},{5,1},{9,5},{13,9},{2,14},{6,2},{... | collective-permute-start | bytes 1572872 | tf_op jit(solution)/shard_map/ppermute | solution.py:188
  7.0 1.8 %fold_amplitudes.1 = bf16[2,2,128,256]{3,2,1,0:T(8,128)(2,1)S(1)} custom-call(bf16[128,4,1024]{2,1,0:T(4,128)(2,1)S(1)} %bitcast.46, s32[8]{0:T(128)S(1)} %copy-done.3, s32[8]{0:T(128)S(1)} %copy-done.4, s32[4]{0:T(128)S(1)} %copy-done.5, s32[16]{0:T(128)S(1)} %copy-done.6), custom_call_target="tpu_custom_call" | custom-call | flops 1024 | bytes 1024 | tf_op jit(solution)/shard_map/fold_amplitudes/pallas_call | solution.py:175
  8.8 0.7 %collective-permute-start = (bf16[2,128,256]{2,1,0:T(8,128)(2,1)S(1)}, bf16[2,128,256]{2,1,0:T(8,128)(2,1)S(1)}, u32[]{:S(2)}, u32[]{:S(2)}) collective-permute-start(bf16[2,128,256]{2,1,0:T(8,128)(2,1)S(1)} %get-tuple-element.23), channel_id=1, source_target_pairs={{0,0},{1,32},{2,64},{3,96},{16,16},{17,48},{18,80},{19,112},{32,1}... | collective-permute-start | bytes 393224 | tf_op jit(solution)/shard_map/ppermute | solution.py:221
  9.4 1.7 %collective-permute-start.1 = (bf16[2,128,256]{2,1,0:T(8,128)(2,1)S(1)}, bf16[2,128,256]{2,1,0:T(8,128)(2,1)S(1)}, u32[]{:S(2)}, u32[]{:S(2)}) collective-permute-start(bf16[2,128,256]{2,1,0:T(8,128)(2,1)S(1)} %get-tuple-element.22), channel_id=1, source_target_pairs={{0,16},{1,48},{2,80},{3,112},{16,0},{17,32},{18,64},{19,96},{32,17... | collective-permute-start | bytes 393224 | tf_op jit(solution)/shard_map/ppermute | solution.py:221
  11.1 6.0 %collective-permute-start.2 = (bf16[2,128,256]{2,1,0:T(8,128)(2,1)S(1)}, bf16[2,128,256]{2,1,0:T(8,128)(2,1)S(1)}, u32[]{:S(2)}, u32[]{:S(2)}) collective-permute-start(bf16[2,128,256]{2,1,0:T(8,128)(2,1)S(1)} %collective-permute-done.refs_0_), channel_id=1, source_target_pairs={{0,2},{1,3},{2,0},{3,1},{4,6},{5,7},{6,4},{7,5},{8,10},{9,11},{10,... | collective-permute-start | bytes 393224 | tf_op jit(solution)/shard_map/ppermute | solution.py:196
  17.1 2.9 %collective-permute-start.4 = (bf16[2,128,256]{2,1,0:T(8,128)(2,1)S(1)}, bf16[2,128,256]{2,1,0:T(8,128)(2,1)S(1)}, u32[]{:S(2)}, u32[]{:S(2)}) collective-permute-start(bf16[2,128,256]{2,1,0:T(8,128)(2,1)S(1)} %collective-permute-done.refs_0_), channel_id=1, source_target_pairs={{0,1},{1,0},{2,3},{3,2},{4,5},{5,4},{6,7},{7,6},{8,9},{9,8},{10,11... | collective-permute-start | bytes 393224 | tf_op jit(solution)/shard_map/ppermute | solution.py:196
  20.0 1.1 %collective-permute-start.3 = (bf16[2,128,256]{2,1,0:T(8,128)(2,1)S(1)}, bf16[2,128,256]{2,1,0:T(8,128)(2,1)S(1)}, u32[]{:S(2)}, u32[]{:S(2)}) collective-permute-start(bf16[2,128,256]{2,1,0:T(8,128)(2,1)S(1)} %collective-permute-done.1.refs_1_), channel_id=1, source_target_pairs={{0,2},{1,3},{2,0},{3,1},{4,6},{5,7},{6,4},{7,5},{8,10},{9,11},{10,... | collective-permute-start | bytes 393224 | tf_op jit(solution)/shard_map/ppermute | solution.py:196
  21.3 3.3 %collective-permute-start.11 = (bf16[2,256,256]{2,1,0:T(8,128)(2,1)S(1)}, bf16[2,256,256]{2,1,0:T(8,128)(2,1)S(1)}, u32[]{:S(2)}, u32[]{:S(2)}) collective-permute-start(bf16[2,256,256]{2,1,0:T(8,128)(2,1)S(1)} %slice_bitcast_fusion.1), channel_id=1, source_target_pairs={{0,12},{4,0},{8,4},{12,8},{1,13},{5,1},{9,5},{13,9},{2,14},{6,2},{... | collective-permute-start | bytes 786440 | tf_op jit(solution)/shard_map/ppermute | solution.py:188
  24.6 1.0 %collective-permute-start.5 = (bf16[2,128,256]{2,1,0:T(8,128)(2,1)S(1)}, bf16[2,128,256]{2,1,0:T(8,128)(2,1)S(1)}, u32[]{:S(2)}, u32[]{:S(2)}) collective-permute-start(bf16[2,128,256]{2,1,0:T(8,128)(2,1)S(1)} %collective-permute-done.1.refs_1_), channel_id=1, source_target_pairs={{0,1},{1,0},{2,3},{3,2},{4,5},{5,4},{6,7},{7,6},{8,9},{9,8},{10,11... | collective-permute-start | bytes 393224 | tf_op jit(solution)/shard_map/ppermute | solution.py:196
  25.6 0.5 collective-permute-done.3.refs_3_
  26.7 0.8 %collective-permute-done.6.refs_6_ = bf16[2,128,256]{2,1,0:T(8,128)(2,1)S(1)} collective-permute-done((bf16[2,128,256]{2,1,0:T(8,128)(2,1)S(1)}, bf16[2,128,256]{2,1,0:T(8,128)(2,1)S(1)}, u32[]{:S(2)}, u32[]{:S(2)}) %collective-permute-start.6) | collective-permute-done | bytes 131104 | tf_op jit(solution)/shard_map/ppermute | solution.py:196
  27.9 3.3 %collective-permute-done.10.refs_11_.refs_4_ = bf16[2,256,256]{2,1,0:T(8,128)(2,1)S(1)} collective-permute-done((bf16[2,256,256]{2,1,0:T(8,128)(2,1)S(1)}, bf16[2,256,256]{2,1,0:T(8,128)(2,1)S(1)}, u32[]{:S(2)}, u32[]{:S(2)}) %collective-permute-start.10) | collective-permute-done | bytes 262176 | tf_op jit(solution)/shard_map/ppermute | solution.py:188
  31.1 1.4 %far_products.1 = (f32[2,256,128]{2,1,0:T(8,128)S(1)}, bf16[2,8,128,256]{3,2,1,0:T(8,128)(2,1)S(1)}) custom-call(bf16[2,128,256]{2,1,0:T(8,128)(2,1)S(1)} %collective-permute-done.refs_0_, bf16[2,128,256]{2,1,0:T(8,128)(2,1)S(1)} %collective-permute-done.1.refs_1_, bf16[2,128,256]{2,1,0:T(8,128)(2,1)S(1)} %collective-permute-done.2.refs_2_, ...), custom_call_target="tpu_custom_call" | custom-call | flops 1024 | bytes 1024 | tf_op jit(solution)/shard_map/far_products/pallas_call | solution.py:175
  32.6 0.9 %collective-permute-start.12 = (f32[256,128]{1,0:T(8,128)S(1)}, f32[256,128]{1,0:T(8,128)S(1)}, u32[]{:S(2)}, u32[]{:S(2)}) collective-permute-start(f32[256,128]{1,0:T(8,128)S(1)} %get-tuple-element.21), channel_id=1, source_target_pairs={{0,16},{16,32},{32,48},{48,0},{64,80},{80,96},{96,112},{112,64},{1... | collective-permute-start | bytes 393224 | tf_op jit(solution)/shard_map/ppermute | solution.py:192
  33.4 2.4 %collective-permute-start.16 = (f32[256,128]{1,0:T(8,128)S(1)}, f32[256,128]{1,0:T(8,128)S(1)}, u32[]{:S(2)}, u32[]{:S(2)}) collective-permute-start(f32[256,128]{1,0:T(8,128)S(1)} %get-tuple-element.20), channel_id=1, source_target_pairs={{0,48},{16,0},{32,16},{48,32},{64,112},{80,64},{96,80},{112,96},{1... | collective-permute-start | bytes 393224 | tf_op jit(solution)/shard_map/ppermute | solution.py:192
  35.9 3.2 %near_products.1 = f32[3,2,256,128]{3,2,1,0:T(8,128)S(1)} custom-call(bf16[2,8,128,256]{3,2,1,0:T(8,128)(2,1)S(1)} %get-tuple-element.11.refs_0_, bf16[2,2,256,256]{3,2,1,0:T(8,128)(2,1)S(1)} %copy-done, bf16[2,2,256,256]{3,2,1,0:T(8,128)(2,1)S(1)} %collective-permute-done.8.refs_9_.refs_2_, ...), custom_call_target="tpu_custom_call" | custom-call | flops 1024 | bytes 1024 | tf_op jit(solution)/shard_map/near_products/pallas_call | solution.py:175
  39.2 3.2 %collective-permute-start.15 = (f32[256,128]{1,0:T(8,128)S(1)}, f32[256,128]{1,0:T(8,128)S(1)}, u32[]{:S(2)}, u32[]{:S(2)}) collective-permute-start(f32[256,128]{1,0:T(8,128)S(1)} %get-tuple-element.15), channel_id=1, source_target_pairs={{0,48},{16,0},{32,16},{48,32},{64,112},{80,64},{96,80},{112,96},{1... | collective-permute-start | bytes 393224 | tf_op jit(solution)/shard_map/ppermute | solution.py:192
  42.5 3.2 %collective-permute-start.17 = (f32[256,128]{1,0:T(8,128)S(1)}, f32[256,128]{1,0:T(8,128)S(1)}, u32[]{:S(2)}, u32[]{:S(2)}) collective-permute-start(f32[256,128]{1,0:T(8,128)S(1)} %get-tuple-element.13), channel_id=1, source_target_pairs={{0,48},{16,0},{32,16},{48,32},{64,112},{80,64},{96,80},{112,96},{1... | collective-permute-start | bytes 393224 | tf_op jit(solution)/shard_map/ppermute | solution.py:192
  45.7 2.9 %collective-permute-done.13 = f32[256,128]{1,0:T(8,128)S(1)} collective-permute-done((f32[256,128]{1,0:T(8,128)S(1)}, f32[256,128]{1,0:T(8,128)S(1)}, u32[]{:S(2)}, u32[]{:S(2)}) %collective-permute-start.13) | collective-permute-done | bytes 131104 | tf_op jit(solution)/shard_map/ppermute | solution.py:192
  48.7 2.8 %collective-permute-start.18 = (f32[256,128]{1,0:T(8,128)S(1)}, f32[256,128]{1,0:T(8,128)S(1)}, u32[]{:S(2)}, u32[]{:S(2)}) collective-permute-start(f32[256,128]{1,0:T(8,128)S(1)} %get-tuple-element.17), channel_id=1, source_target_pairs={{0,64},{16,80},{32,96},{48,112},{64,0},{80,16},{96,32},{112,48},{1... | collective-permute-start | bytes 393224 | tf_op jit(solution)/shard_map/ppermute | solution.py:196
  51.5 3.8 %collective-permute-done.18.across_ref = f32[256,128]{1,0:T(8,128)S(1)} collective-permute-done((f32[256,128]{1,0:T(8,128)S(1)}, f32[256,128]{1,0:T(8,128)S(1)}, u32[]{:S(2)}, u32[]{:S(2)}) %collective-permute-start.18) | collective-permute-done | bytes 131104 | tf_op jit(solution)/shard_map/ppermute | solution.py:196
  55.3 0.9 %finish.1 = bf16[128,1024]{1,0:T(8,128)(2,1)} custom-call(f32[2,256,128]{2,1,0:T(8,128)S(1)} %slice_bitcast_fusion.here, f32[256,128]{1,0:T(8,128)S(1)} %get-tuple-element.18.low, f32[256,128]{1,0:T(8,128)S(1)} %get-tuple-element.19.high, f32[256,128]{1,0:T(8,128)S(1)} %collective-permute-done.18.across_ref, s32[16,128]{1,0:T(8,128)S(1)} %copy-done.2), custom_call_target="tpu_custom_call" | custom-call | flops 1024 | bytes 1024 | tf_op jit(solution)/shard_map/finish/pallas_call | solution.py:175
  (41 shorter events, 1.4 us)
Async XLA Ops:
  0.0 6.9 %copy-start.1 = (bf16[1,128,4,1024]{3,2,1,0:T(4,128)(2,1)S(1)}, bf16[1,128,4,1024]{3,2,1,0:T(4,128)(2,1)}, u32[]{:S(2)}) copy-start(bf16[1,128,4,1024]{3,2,1,0:T(4,128)(2,1)} %param.8) | copy-start | bytes 3145732
  2.6 4.3 %copy-start.6 = (s32[16]{0:T(128)S(1)}, s32[16]{0:T(128)}, u32[]{:S(2)}) copy-start(s32[16]{0:T(128)} %refs_3_.1) | copy-start | bytes 196
  2.6 4.3 %copy-start.3 = (s32[8]{0:T(128)S(1)}, s32[8]{0:T(128)}, u32[]{:S(2)}) copy-start(s32[8]{0:T(128)} %refs_0_.1) | copy-start | bytes 100
  2.7 18.5 %collective-permute-start.8 = (bf16[2,2,256,256]{3,2,1,0:T(8,128)(2,1)}, bf16[2,2,256,256]{3,2,1,0:T(8,128)(2,1)S(1)}, u32[]{:S(2)}, u32[]{:S(2)}) collective-permute-start(bf16[2,2,256,256]{3,2,1,0:T(8,128)(2,1)} %get-tuple-element.9.refs_8_.refs_1_), channel_id=1, source_target_pairs={{0,4},{4,8},{8,12},{12,0},{1,5},{5,9},{9,13},{13,1},{2,6},{6,10},{... | collective-permute-start | bytes 1572872 | tf_op jit(solution)/shard_map/ppermute | solution.py:188
  4.7 16.5 %collective-permute-start.9 = (bf16[2,2,256,256]{3,2,1,0:T(8,128)(2,1)}, bf16[2,2,256,256]{3,2,1,0:T(8,128)(2,1)S(1)}, u32[]{:S(2)}, u32[]{:S(2)}) collective-permute-start(bf16[2,2,256,256]{3,2,1,0:T(8,128)(2,1)} %get-tuple-element.9.refs_8_.refs_1_), channel_id=1, source_target_pairs={{0,12},{4,0},{8,4},{12,8},{1,13},{5,1},{9,5},{13,9},{2,14},{6,2},{... | collective-permute-start | bytes 1572872 | tf_op jit(solution)/shard_map/ppermute | solution.py:188
  8.8 2.3 %collective-permute-start = (bf16[2,128,256]{2,1,0:T(8,128)(2,1)S(1)}, bf16[2,128,256]{2,1,0:T(8,128)(2,1)S(1)}, u32[]{:S(2)}, u32[]{:S(2)}) collective-permute-start(bf16[2,128,256]{2,1,0:T(8,128)(2,1)S(1)} %get-tuple-element.23), channel_id=1, source_target_pairs={{0,0},{1,32},{2,64},{3,96},{16,16},{17,48},{18,80},{19,112},{32,1}... | collective-permute-start | bytes 393224 | tf_op jit(solution)/shard_map/ppermute | solution.py:221
  9.4 21.7 %copy-start = (bf16[2,2,256,256]{3,2,1,0:T(8,128)(2,1)S(1)}, bf16[2,2,256,256]{3,2,1,0:T(8,128)(2,1)}, u32[]{:S(2)}) copy-start(bf16[2,2,256,256]{3,2,1,0:T(8,128)(2,1)} %get-tuple-element.9.refs_8_.refs_1_) | copy-start | bytes 1572868
  9.4 10.6 %collective-permute-start.1 = (bf16[2,128,256]{2,1,0:T(8,128)(2,1)S(1)}, bf16[2,128,256]{2,1,0:T(8,128)(2,1)S(1)}, u32[]{:S(2)}, u32[]{:S(2)}) collective-permute-start(bf16[2,128,256]{2,1,0:T(8,128)(2,1)S(1)} %get-tuple-element.22), channel_id=1, source_target_pairs={{0,16},{1,48},{2,80},{3,112},{16,0},{17,32},{18,64},{19,96},{32,17... | collective-permute-start | bytes 393224 | tf_op jit(solution)/shard_map/ppermute | solution.py:221
  11.1 13.5 %collective-permute-start.2 = (bf16[2,128,256]{2,1,0:T(8,128)(2,1)S(1)}, bf16[2,128,256]{2,1,0:T(8,128)(2,1)S(1)}, u32[]{:S(2)}, u32[]{:S(2)}) collective-permute-start(bf16[2,128,256]{2,1,0:T(8,128)(2,1)S(1)} %collective-permute-done.refs_0_), channel_id=1, source_target_pairs={{0,2},{1,3},{2,0},{3,1},{4,6},{5,7},{6,4},{7,5},{8,10},{9,11},{10,... | collective-permute-start | bytes 393224 | tf_op jit(solution)/shard_map/ppermute | solution.py:196
  17.1 9.4 %collective-permute-start.4 = (bf16[2,128,256]{2,1,0:T(8,128)(2,1)S(1)}, bf16[2,128,256]{2,1,0:T(8,128)(2,1)S(1)}, u32[]{:S(2)}, u32[]{:S(2)}) collective-permute-start(bf16[2,128,256]{2,1,0:T(8,128)(2,1)S(1)} %collective-permute-done.refs_0_), channel_id=1, source_target_pairs={{0,1},{1,0},{2,3},{3,2},{4,5},{5,4},{6,7},{7,6},{8,9},{9,8},{10,11... | collective-permute-start | bytes 393224 | tf_op jit(solution)/shard_map/ppermute | solution.py:196
  20.0 6.1 %collective-permute-start.3 = (bf16[2,128,256]{2,1,0:T(8,128)(2,1)S(1)}, bf16[2,128,256]{2,1,0:T(8,128)(2,1)S(1)}, u32[]{:S(2)}, u32[]{:S(2)}) collective-permute-start(bf16[2,128,256]{2,1,0:T(8,128)(2,1)S(1)} %collective-permute-done.1.refs_1_), channel_id=1, source_target_pairs={{0,2},{1,3},{2,0},{3,1},{4,6},{5,7},{6,4},{7,5},{8,10},{9,11},{10,... | collective-permute-start | bytes 393224 | tf_op jit(solution)/shard_map/ppermute | solution.py:196
  21.2 10.0 %copy-start.2 = (s32[16,128]{1,0:T(8,128)S(1)}, s32[16,128]{1,0:T(8,128)}, u32[]{:S(2)}) copy-start(s32[16,128]{1,0:T(8,128)} %get-tuple-element.10.refs_13_.refs_6_.table) | copy-start | bytes 24580
  21.2 9.9 %collective-permute-start.10 = (bf16[2,256,256]{2,1,0:T(8,128)(2,1)S(1)}, bf16[2,256,256]{2,1,0:T(8,128)(2,1)S(1)}, u32[]{:S(2)}, u32[]{:S(2)}) collective-permute-start(bf16[2,256,256]{2,1,0:T(8,128)(2,1)S(1)} %slice_bitcast_fusion.2), channel_id=1, source_target_pairs={{0,4},{4,8},{8,12},{12,0},{1,5},{5,9},{9,13},{13,1},{2,6},{6,10},{... | collective-permute-start | bytes 786440 | tf_op jit(solution)/shard_map/ppermute | solution.py:188
  21.3 9.8 %collective-permute-start.11 = (bf16[2,256,256]{2,1,0:T(8,128)(2,1)S(1)}, bf16[2,256,256]{2,1,0:T(8,128)(2,1)S(1)}, u32[]{:S(2)}, u32[]{:S(2)}) collective-permute-start(bf16[2,256,256]{2,1,0:T(8,128)(2,1)S(1)} %slice_bitcast_fusion.1), channel_id=1, source_target_pairs={{0,12},{4,0},{8,4},{12,8},{1,13},{5,1},{9,5},{13,9},{2,14},{6,2},{... | collective-permute-start | bytes 786440 | tf_op jit(solution)/shard_map/ppermute | solution.py:188
  24.6 2.0 %collective-permute-start.5 = (bf16[2,128,256]{2,1,0:T(8,128)(2,1)S(1)}, bf16[2,128,256]{2,1,0:T(8,128)(2,1)S(1)}, u32[]{:S(2)}, u32[]{:S(2)}) collective-permute-start(bf16[2,128,256]{2,1,0:T(8,128)(2,1)S(1)} %collective-permute-done.1.refs_1_), channel_id=1, source_target_pairs={{0,1},{1,0},{2,3},{3,2},{4,5},{5,4},{6,7},{7,6},{8,9},{9,8},{10,11... | collective-permute-start | bytes 393224 | tf_op jit(solution)/shard_map/ppermute | solution.py:196
  26.1 1.4 %collective-permute-start.6 = (bf16[2,128,256]{2,1,0:T(8,128)(2,1)S(1)}, bf16[2,128,256]{2,1,0:T(8,128)(2,1)S(1)}, u32[]{:S(2)}, u32[]{:S(2)}) collective-permute-start(bf16[2,128,256]{2,1,0:T(8,128)(2,1)S(1)} %collective-permute-done.2.refs_2_), channel_id=1, source_target_pairs={{0,1},{1,0},{2,3},{3,2},{4,5},{5,4},{6,7},{7,6},{8,9},{9,8},{10,11... | collective-permute-start | bytes 393224 | tf_op jit(solution)/shard_map/ppermute | solution.py:196
  26.5 1.3 %collective-permute-start.7 = (bf16[2,128,256]{2,1,0:T(8,128)(2,1)S(1)}, bf16[2,128,256]{2,1,0:T(8,128)(2,1)S(1)}, u32[]{:S(2)}, u32[]{:S(2)}) collective-permute-start(bf16[2,128,256]{2,1,0:T(8,128)(2,1)S(1)} %collective-permute-done.3.refs_3_), channel_id=1, source_target_pairs={{0,1},{1,0},{2,3},{3,2},{4,5},{5,4},{6,7},{7,6},{8,9},{9,8},{10,11... | collective-permute-start | bytes 393224 | tf_op jit(solution)/shard_map/ppermute | solution.py:196
  32.6 9.8 %collective-permute-start.12 = (f32[256,128]{1,0:T(8,128)S(1)}, f32[256,128]{1,0:T(8,128)S(1)}, u32[]{:S(2)}, u32[]{:S(2)}) collective-permute-start(f32[256,128]{1,0:T(8,128)S(1)} %get-tuple-element.21), channel_id=1, source_target_pairs={{0,16},{16,32},{32,48},{48,0},{64,80},{80,96},{96,112},{112,64},{1... | collective-permute-start | bytes 393224 | tf_op jit(solution)/shard_map/ppermute | solution.py:192
  33.4 9.0 %collective-permute-start.16 = (f32[256,128]{1,0:T(8,128)S(1)}, f32[256,128]{1,0:T(8,128)S(1)}, u32[]{:S(2)}, u32[]{:S(2)}) collective-permute-start(f32[256,128]{1,0:T(8,128)S(1)} %get-tuple-element.20), channel_id=1, source_target_pairs={{0,48},{16,0},{32,16},{48,32},{64,112},{80,64},{96,80},{112,96},{1... | collective-permute-start | bytes 393224 | tf_op jit(solution)/shard_map/ppermute | solution.py:192
  39.1 6.7 %collective-permute-start.14 = (f32[256,128]{1,0:T(8,128)S(1)}, f32[256,128]{1,0:T(8,128)S(1)}, u32[]{:S(2)}, u32[]{:S(2)}) collective-permute-start(f32[256,128]{1,0:T(8,128)S(1)} %get-tuple-element.16), channel_id=1, source_target_pairs={{0,16},{16,32},{32,48},{48,0},{64,80},{80,96},{96,112},{112,64},{1... | collective-permute-start | bytes 393224 | tf_op jit(solution)/shard_map/ppermute | solution.py:192
  39.2 6.6 %collective-permute-start.15 = (f32[256,128]{1,0:T(8,128)S(1)}, f32[256,128]{1,0:T(8,128)S(1)}, u32[]{:S(2)}, u32[]{:S(2)}) collective-permute-start(f32[256,128]{1,0:T(8,128)S(1)} %get-tuple-element.15), channel_id=1, source_target_pairs={{0,48},{16,0},{32,16},{48,32},{64,112},{80,64},{96,80},{112,96},{1... | collective-permute-start | bytes 393224 | tf_op jit(solution)/shard_map/ppermute | solution.py:192
  42.4 6.2 %collective-permute-start.13 = (f32[256,128]{1,0:T(8,128)S(1)}, f32[256,128]{1,0:T(8,128)S(1)}, u32[]{:S(2)}, u32[]{:S(2)}) collective-permute-start(f32[256,128]{1,0:T(8,128)S(1)} %get-tuple-element.14), channel_id=1, source_target_pairs={{0,16},{16,32},{32,48},{48,0},{64,80},{80,96},{96,112},{112,64},{1... | collective-permute-start | bytes 393224 | tf_op jit(solution)/shard_map/ppermute | solution.py:192
  42.5 6.2 %collective-permute-start.17 = (f32[256,128]{1,0:T(8,128)S(1)}, f32[256,128]{1,0:T(8,128)S(1)}, u32[]{:S(2)}, u32[]{:S(2)}) collective-permute-start(f32[256,128]{1,0:T(8,128)S(1)} %get-tuple-element.13), channel_id=1, source_target_pairs={{0,48},{16,0},{32,16},{48,32},{64,112},{80,64},{96,80},{112,96},{1... | collective-permute-start | bytes 393224 | tf_op jit(solution)/shard_map/ppermute | solution.py:192
  48.7 6.6 %collective-permute-start.18 = (f32[256,128]{1,0:T(8,128)S(1)}, f32[256,128]{1,0:T(8,128)S(1)}, u32[]{:S(2)}, u32[]{:S(2)}) collective-permute-start(f32[256,128]{1,0:T(8,128)S(1)} %get-tuple-element.17), channel_id=1, source_target_pairs={{0,64},{16,80},{32,96},{48,112},{64,0},{80,16},{96,32},{112,48},{1... | collective-permute-start | bytes 393224 | tf_op jit(solution)/shard_map/ppermute | solution.py:196
  (2 other events, 8.6 us)
